TPU v7x, 32 devices: a whole 2x2x4 slice. The times are simulated.
32 devices in a mesh: fc: 8 (over z, core), tok: 4 (over y, x).
Axes of the slice: x: 2, y: 2, z: 4, core: 2. Of those that a mesh axis runs over, the one named last changes fastest.
Arguments:
- tokens: bfloat16 [8, 32, 128, 1024], P('fc', 'tok'), may hold values from -6 to 6
- slot_keys: bfloat16 [1024, 256], replicated, may hold values from -2 to 2
- norm_gain: float32 [1024], replicated, may hold values from 0.25 to 1.75
- slot_gain: float32 [1024], replicated, may hold values from 0.25 to 1.75
- w_in: bfloat16 [64, 1024, 512], P(('fc', 'tok')), may hold values from -0.1875 to 0.1875
- w_out: bfloat16 [64, 512, 1024], P(('fc', 'tok')), may hold values from -0.25 to 0.25
- conv_weight: float32 [7, 7, 1024], replicated, may hold values from -0.875 to 0.875
- ln_gain: float32 [1024], replicated, may hold values from 0.25 to 1.75
- proj: bfloat16 [1024, 1024], replicated, may hold values from -0.1875 to 0.1875
- layer_scale: float32 [1024], replicated, may hold values from 0.25 to 1.75
Outputs:
- fields: bfloat16 [8, 32, 128, 1024], P('fc', 'tok')
All inputs are finite; a program needn't handle non-finite values.
Results may differ from a plain program's by a relative error of at most 0.008.
The roundings to bfloat16 on the way count: a program that leaves them out, or rounds other values in their place, can miss the bound.
Values may be sent and summed in bfloat16 or wider, within the bound.
No kernel may reach another device: no remote copies, remote signals or barrier semaphores. Data moves between devices by JAX's collectives and lax.ppermute only.
A program may use at most 64 MiB of HBM per device.

v0:
```python
import jax
import jax.numpy as jnp
from jax import lax
from jax.sharding import PartitionSpec as P


def with_halo(block, sides, width):
    for axis, dim in sides:
        count = lax.axis_size(axis)
        forward = [(i, i + 1) for i in range(count - 1)]
        backward = [(target, source) for source, target in forward]
        low = lax.ppermute(
            lax.slice_in_dim(block, block.shape[dim] - width, None, axis=dim), axis, forward
        )
        high = lax.ppermute(lax.slice_in_dim(block, 0, width, axis=dim), axis, backward)
        block = jnp.concatenate([low, block, high], axis=dim)
    return block


def rms_scale(value, gain):
    return value * lax.rsqrt(jnp.mean(value * value, axis=-1, keepdims=True) + 1e-06) * gain


def local(
    tokens, slot_keys, norm_gain, slot_gain, w_in, w_out, conv_weight, ln_gain, proj, layer_scale
):
    rows = tokens.shape[1]
    cols = tokens.shape[2]
    width = tokens.shape[3]
    count_fc = lax.axis_size("fc")
    count_tok = lax.axis_size("tok")
    slot_total = slot_keys.shape[1]
    slot_dev = slot_total // (count_fc * count_tok)
    cells = tokens.reshape(rows * cols, width)
    normed = rms_scale(cells.astype(jnp.float32), norm_gain).astype(jnp.bfloat16)
    logits = jnp.dot(normed, slot_keys, preferred_element_type=jnp.float32)
    peak = lax.pmax(jnp.max(logits, axis=0), "tok")
    shifted = jnp.exp(logits - peak)
    dispatch = shifted.astype(jnp.bfloat16)
    numer = lax.dot_general(
        dispatch, cells, (((0,), (0,)), ((), ())), preferred_element_type=jnp.float32
    )
    numer = numer.reshape(count_fc, count_tok * slot_dev, width)
    numer = lax.psum_scatter(
        numer.astype(jnp.bfloat16), "tok", scatter_dimension=1, tiled=True
    ).astype(jnp.float32)
    local_in = rms_scale(numer, slot_gain).astype(jnp.bfloat16)
    slot_in = lax.all_to_all(local_in, "fc", split_axis=0, concat_axis=0, tiled=True)
    grouped = slot_in.reshape(count_fc, w_in.shape[0], slot_dev // w_in.shape[0], width)
    hidden = jax.nn.gelu(
        jnp.einsum("mesd,edf->mesf", grouped, w_in, preferred_element_type=jnp.float32)
    ).astype(jnp.bfloat16)
    expert_out = jnp.einsum(
        "mesf,efd->mesd", hidden, w_out, preferred_element_type=jnp.float32
    ).astype(jnp.bfloat16)
    expert_out = expert_out.reshape(count_fc, slot_dev, width)
    returned = lax.all_to_all(expert_out, "fc", split_axis=0, concat_axis=0, tiled=True)
    every_slot = lax.all_gather(returned, "tok", axis=1, tiled=True).reshape(slot_total, width)
    combine = jax.nn.softmax(logits, axis=-1).astype(jnp.bfloat16)
    mixed = jnp.dot(combine, every_slot, preferred_element_type=jnp.float32)
    state = (cells.astype(jnp.float32) + mixed).astype(jnp.bfloat16).reshape(rows, cols, width)
    padded = with_halo(state, (("tok", 0),), 3)
    padded = jnp.concatenate([padded[:, cols - 3 :], padded, padded[:, :3]], axis=1)
    conv = jnp.zeros((rows, cols, width), jnp.float32)
    for row_tap in range(7):
        for col_tap in range(7):
            conv = (
                conv
                + padded[row_tap : row_tap + rows, col_tap : col_tap + cols].astype(jnp.float32)
                * conv_weight[row_tap, col_tap]
            )
    center = conv - jnp.mean(conv, axis=-1, keepdims=True)
    spread = jnp.mean(center * center, axis=-1, keepdims=True)
    normal = (center * lax.rsqrt(spread + 1e-06) * ln_gain).astype(jnp.bfloat16)
    branch = jnp.dot(normal.reshape(rows * cols, width), proj, preferred_element_type=jnp.float32)
    result = state.reshape(rows * cols, width).astype(jnp.float32) + layer_scale * jax.nn.gelu(
        branch
    )
    return result.astype(jnp.bfloat16).reshape(1, rows, cols, width)


def solution(mesh):
    return jax.shard_map(
        local,
        mesh=mesh,
        in_specs=(
            P("fc", "tok", None, None),
            P(),
            P(),
            P(),
            P(("fc", "tok"), None, None),
            P(("fc", "tok"), None, None),
            P(),
            P(),
            P(),
            P(),
        ),
        out_specs=P("fc", "tok", None, None),
        check_vma=False,
    )
```

profile of v0, /device:TPU:4, one launch (start us, length us, event | category | flops | bytes accessed | tf_op | source)
XLA Modules:
  0.0 195.9 jit_solution(10661281492974501635)
XLA Ops:
  6.5 2.2 %multiply_reduce_fusion.1 = f32[8,128]{1,0:T(8,128)S(1)} fusion(bf16[1,8,128,1024]{3,2,1,0:T(8,128)(2,1)} %param.10), kind=kLoop, calls=%fused_computation.19 | loop fusion | flops 3144704 | bytes 2101248 | tf_op jit(solution)/shard_map/reduce_sum | solution.py:21
  8.8 2.6 %fusion.66 = (f32[1024]{0:T(1024)S(1)}, f32[1024,256]{0,1:T(8,128)S(1)}) fusion(bf16[1024,256]{1,0:T(8,128)(2,1)} %param.11, bf16[1024,1024]{1,0:T(8,128)(2,1)} %bitcast.107, f32[1024]{0:T(1024)} %param.12, f32[1024]{0:T(1024)S(1)} %rsqrt_bitcast_fusion), kind=kOutput, calls=%fused_computation.87 | convolution fusion | flops 541326336 | bytes 3682304 | tf_op jit(solution)/shard_map/dot_general | solution.py:36
  11.4 0.3 fusion.33
  11.7 9.0 %pmax.7 = f32[256]{0:T(256)S(1)} all-reduce(f32[256]{0:T(256)S(1)} %get-tuple-element.6), channel_id=1, replica_groups=mesh['fc'=8,'tok'=4] {'tok'}, use_global_device_ids=true, to_apply=%region_4.0 | all-reduce | flops 256 | bytes 2048 | tf_op jit(solution)/shard_map/pmax | solution.py:37
  20.6 0.2 exponential_convert_fusion
  20.8 3.1 %convolution_convert_fusion = bf16[8,32,1024]{2,1,0:T(8,128)(2,1)} fusion(bf16[8,32,1024]{2,1,0:T(8,128)(2,1)S(1)} %bitcast.116, bf16[1024,1024,1]{1,0,2:T(8,128)(2,1)} %bitcast.108), kind=kOutput, calls=%fused_computation.47 | convolution fusion | flops 537133056 | bytes 3145728 | tf_op jit(solution)/shard_map/dot_general | solution.py:40
  24.0 0.7 dynamic-slice
  25.3 44.3 %all-reduce.3.cloned.1.call-done = bf16[8,32,1024]{2,1,0:T(8,128)(2,1)} async-done(((bf16[8,32,1024]{2,1,0:T(8,128)(2,1)}), bf16[8,32,1024]{2,1,0:T(8,128)(2,1)}) %all-reduce.3.cloned.1.call-update) | async-done | bytes 524304
  69.6 1.0 fusion.36
  70.6 1.0 fusion.38
  71.7 11.2 %all_to_all.10 = bf16[8,8,1024]{2,1,0:T(8,128)(2,1)S(1)} all-to-all(bf16[8,8,1024]{2,1,0:T(8,128)(2,1)S(1)} %fusion.38), channel_id=1, replica_groups=mesh['fc'=8,'tok'=4] {'fc'}, dimensions={0} | all-to-all | bytes 262144 | tf_op jit(solution)/shard_map/all_to_all | solution.py:48
  82.9 3.0 %fusion.27 = bf16[2,8,4,1024]{3,1,2,0:T(8,128)(2,1)S(1)} fusion(bf16[2,512,1024]{2,1,0:T(8,128)(2,1)} %param.15, bf16[8,2,4,1024]{3,0,2,1:T(8,128)(2,1)S(1)} %bitcast.114, bf16[2,1024,512]{2,1,0:T(8,128)(2,1)} %param.14), kind=kOutput, calls=%fused_computation.48 | convolution fusion | flops 134578176 | bytes 4456448 | tf_op jit(solution)/shard_map/mesf,efd->mesd/dot_general | solution.py:53
  86.0 9.3 %all_to_all.11 = bf16[8,8,1024]{2,1,0:T(8,128)(2,1)S(1)} all-to-all(bf16[8,8,1024]{2,1,0:T(8,128)(2,1)S(1)} %copy.15), channel_id=1, replica_groups=mesh['fc'=8,'tok'=4] {'fc'}, dimensions={0} | all-to-all | bytes 262144 | tf_op jit(solution)/shard_map/all_to_all | solution.py:57
  95.3 9.2 %all_gather.3 = bf16[8,32,1024]{2,1,0:T(8,128)(2,1)S(1)} all-gather(bf16[8,8,1024]{2,1,0:T(8,128)(2,1)S(1)} %all_to_all.11), channel_id=1, replica_groups=mesh['fc'=8,'tok'=4] {'tok'}, dimensions={1}, use_global_device_ids=true | all-gather | bytes 655360 | tf_op jit(solution)/shard_map/all_gather | solution.py:58
  104.5 2.4 %fusion.2 = bf16[1024,1024]{1,0:T(8,128)(2,1)S(1)} fusion(bf16[1024,1024]{1,0:T(8,128)(2,1)} %bitcast.109, bf16[256,1024]{1,0:T(8,128)(2,1)S(1)} %bitcast.113, f32[1024,256]{0,1:T(8,128)S(1)} %get-tuple-element.63, f32[1024]{0:T(1024)S(1)} %get-tuple-element.5, f32[1024]{0:T(1024)S(1)} %get-tuple-element.62), kind=kOutput, calls=%fused_computation.5 | convolution fusion | flops 540803072 | bytes 5775360 | tf_op jit(solution)/shard_map/dot_general | solution.py:60
  107.0 3.4 %collective-permute-start.1 = (bf16[3,128,1024]{2,1,0:T(8,128)(2,1)S(1)}, bf16[3,128,1024]{2,1,0:T(8,128)(2,1)S(1)}, u32[]{:S(2)}, u32[]{:S(2)}) collective-permute-start(bf16[3,128,1024]{2,1,0:T(8,128)(2,1)S(1)} %bitcast.112), channel_id=1, source_target_pairs={{1,0},{2,1},{3,2},{5,4},{6,5},{7,6},{9,8},{10,9},{11,10},{13,12},{... | collective-permute-start | bytes 2359304 | tf_op jit(solution)/shard_map/ppermute | solution.py:15
  110.4 2.7 %collective-permute-start = (bf16[3,128,1024]{2,1,0:T(8,128)(2,1)S(1)}, bf16[3,128,1024]{2,1,0:T(8,128)(2,1)S(1)}, u32[]{:S(2)}, u32[]{:S(2)}) collective-permute-start(bf16[3,128,1024]{2,1,0:T(8,128)(2,1)S(1)} %bitcast.111), channel_id=1, source_target_pairs={{0,1},{1,2},{2,3},{4,5},{5,6},{6,7},{8,9},{9,10},{10,11},{12,13},{... | collective-permute-start | bytes 2359304 | tf_op jit(solution)/shard_map/ppermute | solution.py:12
  113.3 15.1 %collective-permute-done.1 = bf16[3,128,1024]{2,1,0:T(8,128)(2,1)S(1)} collective-permute-done((bf16[3,128,1024]{2,1,0:T(8,128)(2,1)S(1)}, bf16[3,128,1024]{2,1,0:T(8,128)(2,1)S(1)}, u32[]{:S(2)}, u32[]{:S(2)}) %collective-permute-start.1) | collective-permute-done | bytes 786464 | tf_op jit(solution)/shard_map/ppermute | solution.py:15
  128.4 15.2 %collective-permute-done = bf16[3,128,1024]{2,1,0:T(8,128)(2,1)S(1)} collective-permute-done((bf16[3,128,1024]{2,1,0:T(8,128)(2,1)S(1)}, bf16[3,128,1024]{2,1,0:T(8,128)(2,1)S(1)}, u32[]{:S(2)}, u32[]{:S(2)}) %collective-permute-start) | collective-permute-done | bytes 786464 | tf_op jit(solution)/shard_map/ppermute | solution.py:12
  143.6 2.3 %fusion.14 = (bf16[14,131,1024]{2,1,0:T(8,128)(2,1)S(1)}, bf16[14,131,1024]{2,1,0:T(8,128)(2,1)S(1)}) fusion(bf16[3,128,1024]{2,1,0:T(8,128)(2,1)S(1)} %collective-permute-done.1, bf16[8,128,1024]{2,1,0:T(8,128)(2,1)S(1)} %bitcast.105, bf16[3,128,1024]{2,1,0:T(8,128)(2,1)S(1)} %collective-permute-done), kind=kLoop, calls=%fused_computation.24 | loop fusion | flops 45072384 | bytes 11182080 | tf_op jit(solution)/shard_map/concatenate | solution.py:63
  145.9 37.1 %fusion.61 = (f32[8,128]{1,0:T(8,128)S(1)}, f32[8,128,1024]{2,1,0:T(8,128)S(1)}) fusion(f32[1024]{0:T(1024)S(1)} %bitcast.126, bf16[14,131,1024]{2,1,0:T(8,128)(2,1)S(1)} %get-tuple-element.10, f32[1024]{0:T(1024)S(1)} %bitcast.127, f32[1024]{0:T(1024)S(1)} %bitcast.129, f32[1024]{0:T(1024)S(1)} %bitcast.130, ...), kind=kLoop, calls=%fused_computation.82 | loop fusion | flops 160431104 | bytes 96149504 | tf_op jit(solution)/shard_map/reduce_sum | solution.py:72
  183.0 0.5 multiply_reduce_fusion
  183.7 0.6 multiply_convert_fusion
  184.3 4.8 %fusion.12 = bf16[1024,1024]{1,0:T(8,128)(2,1)} fusion(bf16[1024,1024]{1,0:T(8,128)(2,1)S(1)} %fusion.2, f32[1024]{0:T(1024)S(1)} %copy-done.4, bf16[1024,1024]{1,0:T(8,128)(2,1)S(1)} %bitcast.110, bf16[1024,1024]{1,0:T(8,128)(2,1)S(1)} %copy-done), kind=kOutput, calls=%fused_computation.15 | convolution fusion | flops 2160066560 | bytes 8392704 | tf_op jit(solution)/shard_map/dot_general | solution.py:75
  (24 shorter events, 0.6 us)
Async XLA Ops:
  6.5 177.7 %copy-start = (bf16[1024,1024]{1,0:T(8,128)(2,1)S(1)}, bf16[1024,1024]{1,0:T(8,128)(2,1)}, u32[]{:S(2)}) copy-start(bf16[1024,1024]{1,0:T(8,128)(2,1)} %param.18) | copy-start | bytes 6291460
  6.5 63.1 %all-reduce.3.cloned.1.call-start = ((), (), s32[]{:S(2)}) async-start(), calls=%async_computation.2 | async-start | bytes 1048576
  11.4 12.6 %copy-start.5 = (u32[32]{0:T(128)S(1)}, u32[32]{0:T(128)}, u32[]{:S(2)}) copy-start(u32[32]{0:T(128)} %constant.34) | copy-start | bytes 388
  11.4 59.2 %copy-start.2 = (f32[1024]{0:T(1024)S(1)}, f32[1024]{0:T(1024)}, u32[]{:S(2)}) copy-start(f32[1024]{0:T(1024)} %param.13) | copy-start | bytes 12292
  104.5 8.6 %copy-start.1 = (f32[7,7,1024]{2,1,0:T(8,128)S(1)}, f32[7,7,1024]{2,1,0:T(8,128)}, u32[]{:S(2)}) copy-start(f32[7,7,1024]{2,1,0:T(8,128)} %param.16) | copy-start | bytes 602116
  107.0 21.4 %collective-permute-start.1 = (bf16[3,128,1024]{2,1,0:T(8,128)(2,1)S(1)}, bf16[3,128,1024]{2,1,0:T(8,128)(2,1)S(1)}, u32[]{:S(2)}, u32[]{:S(2)}) collective-permute-start(bf16[3,128,1024]{2,1,0:T(8,128)(2,1)S(1)} %bitcast.112), channel_id=1, source_target_pairs={{1,0},{2,1},{3,2},{5,4},{6,5},{7,6},{9,8},{10,9},{11,10},{13,12},{... | collective-permute-start | bytes 2359304 | tf_op jit(solution)/shard_map/ppermute | solution.py:15
  110.4 33.2 %collective-permute-start = (bf16[3,128,1024]{2,1,0:T(8,128)(2,1)S(1)}, bf16[3,128,1024]{2,1,0:T(8,128)(2,1)S(1)}, u32[]{:S(2)}, u32[]{:S(2)}) collective-permute-start(bf16[3,128,1024]{2,1,0:T(8,128)(2,1)S(1)} %bitcast.111), channel_id=1, source_target_pairs={{0,1},{1,2},{2,3},{4,5},{5,6},{6,7},{8,9},{9,10},{10,11},{12,13},{... | collective-permute-start | bytes 2359304 | tf_op jit(solution)/shard_map/ppermute | solution.py:12
  183.0 0.7 copy-start.3
  183.6 0.7 copy-start.4
Sparse Core Ops, SparseCore 0:
  24.1 45.4 all-reduce.2
where the time goes:
time: 196 us
  waiting for transfers between devices  74.6 us (38%)
  other arithmetic  45.2 us (23%)
  blocking collectives  38.6 us (20%)
  matrix products  15.9 us (8%)
  between operations  14.3 us (7%)
  starting transfers between devices  6.07 us (3%)
    unnamed x2, waiting for transfers between devices  44.3 us
    reduce_sum x1, other arithmetic, local(): center = conv - jnp.mean(conv, axis=-1, keepdims=True)  37.1 us
    ppermute x1, waiting for transfers between devices, with_halo(): lax.ppermute(lax.slice_in_dim(block, block.shape[dim] - width, None, axis...  15.2 us
    ppermute x1, waiting for transfers between devices, with_halo(): lax.ppermute(lax.slice_in_dim(block, 0, width, axis=dim), axis, backward)  15.1 us
    all_to_all x1, blocking collectives, local(): lax.all_to_all(local_in, 'fc', split_axis=0, concat_axis=0, tiled=True)  11.2 us
    all_to_all x1, blocking collectives, local(): lax.all_to_all(expert_out, 'fc', split_axis=0, concat_axis=0, tiled=True)  9.27 us
    all_gather x1, blocking collectives, local(): lax.all_gather(returned, 'tok', axis=1, tiled=True)  9.19 us
    pmax x1, blocking collectives, local(): peak = lax.pmax(jnp.max(logits, axis=0), 'tok')  8.95 us
  transfers between devices with their start and end apart: 3, of which 3 were waited for; matrix products, arithmetic and copies ran while one was open for 0% of the time, Pallas kernels for 0%

commit v1 on v0

v1 whole, which is shorter than its diff:
```python
import functools

import jax
import jax.numpy as jnp
from jax import lax
from jax.experimental import pallas as pl
from jax.experimental.pallas import tpu as pltpu
from jax.sharding import PartitionSpec as P

F32 = jnp.float32
BF16 = jnp.bfloat16
LANES = 128
EPS = 1e-06
MIB = 1024 * 1024
NT = (((1,), (1,)), ((), ()))
VMEM = pl.BlockSpec(memory_space=pltpu.VMEM)
SMEM = pl.BlockSpec(memory_space=pltpu.SMEM)


def dot_nt(left, right):
    return lax.dot_general(left, right, NT, preferred_element_type=F32)


def rms_scale(value, gain):
    return value * lax.rsqrt(jnp.mean(value * value, axis=-1, keepdims=True) + EPS) * gain


def cost(flops, moved, exps=0):
    return pl.CostEstimate(flops=flops, bytes_accessed=moved, transcendentals=exps)


def dispatch_kernel(layout, index_ref, cells_ref, keys_ref, gain_ref, keys_out, *rest):
    count_z, count_tok, slot_dev = layout
    outs, normed_ref = rest[:-1], rest[-1]
    total, width = cells_ref.shape
    slots = keys_ref.shape[1]
    my_z, my_tok = index_ref[0], index_ref[1]
    place = lax.broadcasted_iota(jnp.int32, (slots, slots), 0)
    source = lax.broadcasted_iota(jnp.int32, (slots, slots), 1)
    inner = lax.rem(place, slot_dev)
    core = lax.rem(place // slot_dev, 2)
    step_z = lax.rem(place // (2 * slot_dev), count_z)
    step_tok = place // (2 * slot_dev * count_z)
    at_z = lax.rem(step_z + my_z, count_z)
    at_tok = lax.rem(step_tok + my_tok, count_tok)
    wanted = ((at_z * 2 + core) * count_tok + at_tok) * slot_dev + inner
    pick = jnp.where(wanted == source, 1.0, 0.0).astype(BF16)
    keys_out[...] = dot_nt(pick, keys_ref[...]).astype(BF16)

    block = 128

    @pl.loop(0, total // block)
    def _(step):
        rows = pl.ds(pl.multiple_of(step * block, block), block)
        normed_ref[rows, :] = rms_scale(cells_ref[rows, :].astype(F32), gain_ref[...]).astype(BF16)

    part = slots // count_tok
    for at, out in enumerate(outs):
        logits = dot_nt(keys_out[at * part : (at + 1) * part, :], normed_ref[...])
        peak = jnp.max(logits, axis=1, keepdims=True)
        weight = jnp.exp(logits - peak).astype(BF16)
        out[:, :width] = jnp.dot(weight, cells_ref[...], preferred_element_type=F32).astype(BF16)
        first = peak.astype(BF16).astype(F32)
        second = (peak - first).astype(BF16).astype(F32)
        third = peak - first - second
        lane = lax.broadcasted_iota(jnp.int32, (part, LANES), 1)
        out[:, width:] = jnp.where(
            lane == 0, first, jnp.where(lane == 1, second, jnp.where(lane == 2, third, 0.0))
        ).astype(BF16)


def dispatch(index, cells, keys, gain, layout):
    count_z, count_tok, slot_dev = layout
    total, width = cells.shape
    slots = keys.shape[1]
    part = slots // count_tok
    return pl.pallas_call(
        functools.partial(dispatch_kernel, layout),
        out_shape=[jax.ShapeDtypeStruct((slots, width), BF16)]
        + [jax.ShapeDtypeStruct((part, width + LANES), BF16)] * count_tok,
        in_specs=[SMEM, VMEM, VMEM, VMEM],
        out_specs=[VMEM] * (1 + count_tok),
        scratch_shapes=[pltpu.VMEM((total, width), BF16)],
        compiler_params=pltpu.CompilerParams(vmem_limit_bytes=48 * MIB),
        cost_estimate=cost(4 * total * width * slots, 4 * total * width, total * slots),
        name="dispatch",
    )(index, cells, keys, gain)


def gather_kernel(count_z, gain_ref, *refs):
    count = len(refs) - count_z
    parts, outs = refs[:count], refs[count:]
    width = gain_ref.shape[1]
    peaks = []
    for ref in parts:
        piece = ref[:, width:].astype(F32)
        peaks.append(jnp.sum(piece, axis=1, keepdims=True))
    peak = functools.reduce(jnp.maximum, peaks)
    numer = None
    for ref, own in zip(parts, peaks):
        term = ref[:, :width].astype(F32) * jnp.exp(own - peak)
        numer = term if numer is None else numer + term
    value = rms_scale(numer, gain_ref[...]).astype(BF16)
    rows = value.shape[0] // count_z
    for at, out in enumerate(outs):
        out[...] = value[at * rows : (at + 1) * rows, :]


def gather_slots(parts, gain, count_z):
    rows, width = parts[0].shape[0] // count_z, gain.shape[1]
    return pl.pallas_call(
        functools.partial(gather_kernel, count_z),
        out_shape=[jax.ShapeDtypeStruct((rows, width), BF16)] * count_z,
        in_specs=[VMEM] * (1 + len(parts)),
        out_specs=[VMEM] * count_z,
        compiler_params=pltpu.CompilerParams(vmem_limit_bytes=32 * MIB),
        cost_estimate=cost(8 * len(parts) * rows * count_z * width, 4 * rows * count_z * width),
        name="gather_slots",
    )(gain, *parts)


def expert_kernel(count_z, slots_exp, core_ref, in_a, in_b, out_a, out_b, *refs):
    parts, outs, rows_ref, sum_ref = refs[:count_z], refs[count_z : 2 * count_z], refs[-2], refs[-1]
    each = parts[0].shape[0]
    step = pl.program_id(0)
    per_core = pl.num_programs(0)

    @pl.when(step == 0)
    def _():
        for at, ref in enumerate(parts):
            rows_ref[at * each : (at + 1) * each, :] = ref[...]
        sum_ref[...] = jnp.zeros_like(sum_ref)

    rows = rows_ref[...]
    place = lax.broadcasted_iota(jnp.int32, (rows.shape[0], 1), 0)
    expert = lax.rem(place, each) // slots_exp
    core = core_ref[0]
    for held, (w_in, w_out) in ((core, (in_a, out_a)), (1 - core, (in_b, out_b))):
        mine = expert == held * per_core + step
        hidden = jax.nn.gelu(jnp.dot(rows, w_in[0], preferred_element_type=F32))
        hidden = jnp.where(mine, hidden, 0.0).astype(BF16)
        sum_ref[...] += jnp.dot(hidden, w_out[0], preferred_element_type=F32)

    @pl.when(step == per_core - 1)
    def _():
        for at, out in enumerate(outs):
            out[...] = sum_ref[at * each : (at + 1) * each, :].astype(BF16)


def experts(core, parts, w_in, w_out, in_other, out_other, slots_exp):
    count_z = len(parts)
    each, width = parts[0].shape
    per_core, _, inner = w_in.shape
    whole = pl.BlockSpec((each, width), lambda i: (0, 0))
    spec_in = pl.BlockSpec((1, width, inner), lambda i: (i, 0, 0))
    spec_out = pl.BlockSpec((1, inner, width), lambda i: (i, 0, 0))
    rows = each * count_z
    return pl.pallas_call(
        functools.partial(expert_kernel, count_z, slots_exp),
        out_shape=[jax.ShapeDtypeStruct((each, width), BF16)] * count_z,
        grid=(per_core,),
        in_specs=[SMEM, spec_in, spec_in, spec_out, spec_out] + [whole] * count_z,
        out_specs=[whole] * count_z,
        scratch_shapes=[pltpu.VMEM((rows, width), BF16), pltpu.VMEM((rows, width), F32)],
        compiler_params=pltpu.CompilerParams(vmem_limit_bytes=40 * MIB),
        cost_estimate=cost(8 * rows * width * inner * per_core, 8 * width * inner * per_core),
        name="experts",
    )(core, w_in, in_other, w_out, out_other, *parts)


def combine_kernel(valid_ref, cells_ref, keys_ref, gain_ref, out_ref):
    normed = rms_scale(cells_ref[...].astype(F32), gain_ref[...]).astype(BF16)
    logits = dot_nt(normed, keys_ref[...])
    raised = jnp.exp(logits - jnp.max(logits, axis=-1, keepdims=True))
    share = raised * (1.0 / jnp.sum(raised, axis=-1, keepdims=True))
    out_ref[...] = jnp.where(valid_ref[0] > 0, share, 0.0).astype(BF16)


def combine_weights(valid, cells, keys, gain):
    total, width = cells.shape
    slots = keys.shape[0]
    block = 128
    return pl.pallas_call(
        combine_kernel,
        out_shape=jax.ShapeDtypeStruct((total, slots), BF16),
        grid=(total // block,),
        in_specs=[
            SMEM,
            pl.BlockSpec((block, width), lambda i: (i, 0)),
            pl.BlockSpec((slots, width), lambda i: (0, 0)),
            pl.BlockSpec((1, width), lambda i: (0, 0)),
        ],
        out_specs=pl.BlockSpec((block, slots), lambda i: (i, 0)),
        compiler_params=pltpu.CompilerParams(vmem_limit_bytes=40 * MIB),
        cost_estimate=cost(2 * total * width * slots, 2 * total * width, total * slots),
        name="combine_weights",
    )(valid, cells, keys, gain)


LEFT = 8


def block_kernel(
    dims, cells_ref, low_ref, high_ref, share_ref, share_low, share_high, weight_ref, ln_ref,
    proj_ref, scale_ref, *rest
):
    rows, cols, taps = dims
    slot_refs, out_ref = rest[:-5], rest[-5]
    slots_ref, state_ref, conv_ref, normal_ref = rest[-4:]
    reach = taps // 2
    width = cells_ref.shape[1]
    groups = width // LANES
    start = 0
    for ref in slot_refs:
        slots_ref[start : start + ref.shape[0], :] = ref[...]
        start += ref.shape[0]

    chunk = 2 * LANES

    def mix(cells, share, at, to):
        at = pl.multiple_of(at * cols, cols)
        picked = share[pl.ds(at, cols), :]
        for lane in range(0, width, chunk):
            mixed = jnp.dot(picked, slots_ref[:, lane : lane + chunk], preferred_element_type=F32)
            value = cells[pl.ds(at, cols), lane : lane + chunk].astype(F32) + mixed
            value = value.astype(BF16).astype(F32)
            for half in range(chunk // LANES):
                group = lane // LANES + half
                piece = value[:, half * LANES : (half + 1) * LANES]
                state_ref[group, to, LEFT : LEFT + cols, :] = piece
                state_ref[group, to, 0:LEFT, :] = piece[cols - LEFT :, :]
                state_ref[group, to, LEFT + cols : 2 * LEFT + cols, :] = piece[:LEFT, :]

    @pl.loop(0, reach)
    def _(row):
        mix(low_ref, share_low, row, row)

    @pl.loop(0, rows)
    def _(row):
        mix(cells_ref, share_ref, row, row + reach)

    @pl.loop(0, reach)
    def _(row):
        mix(high_ref, share_high, row, row + rows + reach)

    span = 16

    @pl.loop(0, groups)
    def _(group):
        lanes = pl.ds(pl.multiple_of(group * LANES, LANES), LANES)

        @pl.loop(0, cols // span)
        def _(piece):
            base = pl.multiple_of(piece * span, span)
            for first in range(0, rows, 8):
                sums = [[None] * (span // 8) for _ in range(8)]
                for col_tap in range(taps):
                    weights = [
                        jnp.broadcast_to(weight_ref[row_tap, col_tap : col_tap + 1, lanes], (8, LANES))
                        for row_tap in range(taps)
                    ]
                    for row in range(8 + taps - 1):
                        for part in range(span // 8):
                            value = state_ref[
                                group,
                                first + row,
                                pl.ds(base + (part * 8 + LEFT - reach + col_tap), 8),
                                :,
                            ]
                            for out_row in range(max(0, row - taps + 1), min(8, row + 1)):
                                term = value * weights[row - out_row]
                                have = sums[out_row][part]
                                sums[out_row][part] = term if have is None else have + term
                for out_row in range(8):
                    for part in range(span // 8):
                        conv_ref[
                            group, pl.ds((first + out_row) * cols + base + part * 8, 8), :
                        ] = sums[out_row][part]

    block = 64

    @pl.loop(0, rows * cols // block)
    def _(step):
        at = pl.ds(pl.multiple_of(step * block, block), block)
        values = [conv_ref[group, at, :] for group in range(groups)]
        mean = jnp.sum(sum(values), axis=-1, keepdims=True) * (1.0 / width)
        centers = [value - mean for value in values]
        spread = jnp.sum(sum(c * c for c in centers), axis=-1, keepdims=True) * (1.0 / width)
        factor = lax.rsqrt(spread + EPS)
        for group in range(groups):
            lanes = slice(group * LANES, (group + 1) * LANES)
            normal_ref[at, lanes] = (centers[group] * factor * ln_ref[:, lanes]).astype(BF16)

    @pl.loop(0, rows)
    def _(row):
        at = pl.ds(pl.multiple_of(row * cols, cols), cols)
        for lane in range(0, width, chunk):
            branch = jnp.dot(
                normal_ref[at, :], proj_ref[:, lane : lane + chunk], preferred_element_type=F32
            )
            branch = scale_ref[:, lane : lane + chunk] * jax.nn.gelu(branch)
            for half in range(chunk // LANES):
                group = lane // LANES + half
                state = state_ref[group, row + reach, LEFT : LEFT + cols, :]
                out_ref[at, group * LANES : (group + 1) * LANES] = (
                    state + branch[:, half * LANES : (half + 1) * LANES]
                ).astype(BF16)


def block_fields(dims, cells, halo, shares, weight, ln_gain, proj, scale, slot_parts):
    rows, cols, taps = dims
    total, width = cells.shape
    slots = sum(part.shape[0] for part in slot_parts)
    groups = width // LANES
    padded = rows + taps - 1
    return pl.pallas_call(
        functools.partial(block_kernel, dims),
        out_shape=jax.ShapeDtypeStruct((total, width), BF16),
        in_specs=[VMEM] * (10 + len(slot_parts)),
        out_specs=VMEM,
        scratch_shapes=[
            pltpu.VMEM((slots, width), BF16),
            pltpu.VMEM((groups, padded, cols + 2 * LEFT, LANES), F32),
            pltpu.VMEM((groups, total, LANES), F32),
            pltpu.VMEM((total, width), BF16),
        ],
        compiler_params=pltpu.CompilerParams(vmem_limit_bytes=48 * MIB),
        cost_estimate=cost(4 * total * width * width, 8 * total * width, total * width),
        name="block_fields",
    )(cells, *halo, *shares, weight, ln_gain, proj, scale, *slot_parts)


def local(
    tokens, slot_keys, norm_gain, slot_gain, w_in, w_out, conv_weight, ln_gain, proj, layer_scale
):
    rows, cols, width = tokens.shape[1:]
    count_fc = lax.axis_size("fc")
    count_tok = lax.axis_size("tok")
    count_z = count_fc // 2
    slots = slot_keys.shape[1]
    slot_dev = slots // (count_fc * count_tok)
    slots_exp = slot_dev // w_in.shape[0]
    taps = conv_weight.shape[0]
    reach = taps // 2
    at_fc, at_tok = lax.axis_index("fc"), lax.axis_index("tok")
    cells = tokens.reshape(rows * cols, width)
    norm_gain, slot_gain = norm_gain.reshape(1, width), slot_gain.reshape(1, width)
    ln_gain, layer_scale = ln_gain.reshape(1, width), layer_scale.reshape(1, width)

    def shift(value, axis, step):
        count = lax.axis_size(axis)
        return lax.ppermute(value, axis, [(i, (i + step) % count) for i in range(count)])

    other = [(i, i ^ 1) for i in range(count_fc)]
    in_other = lax.ppermute(w_in, "fc", other)
    out_other = lax.ppermute(w_out, "fc", other)

    index = jnp.stack([at_fc // 2, at_tok]).astype(jnp.int32)
    keys, *numer = dispatch(index, cells, slot_keys, norm_gain, (count_z, count_tok, slot_dev))
    parts = [numer[0]] + [shift(numer[k], "tok", k) for k in range(1, count_tok)]

    forward = [(i, i + 1) for i in range(count_tok - 1)]
    backward = [(i + 1, i) for i in range(count_tok - 1)]
    low = lax.ppermute(cells[(rows - reach) * cols :], "tok", forward)
    high = lax.ppermute(cells[: reach * cols], "tok", backward)
    always = jnp.ones((1,), jnp.int32)
    has_low = (at_tok > 0).astype(jnp.int32).reshape(1)
    has_high = (at_tok < count_tok - 1).astype(jnp.int32).reshape(1)
    share = combine_weights(always, cells, keys, norm_gain)
    share_low = combine_weights(has_low, low, keys, norm_gain)
    share_high = combine_weights(has_high, high, keys, norm_gain)

    slot_in = gather_slots(parts, slot_gain, count_z)
    arrived = [slot_in[0]] + [shift(slot_in[k], "fc", 2 * k) for k in range(1, count_z)]
    core = (at_fc % 2).astype(jnp.int32).reshape(1)
    made = experts(core, arrived, w_in, w_out, in_other, out_other, slots_exp)
    back = [made[0]] + [shift(made[k], "fc", -2 * k) for k in range(1, count_z)]
    mine = jnp.concatenate(back, axis=0)
    every = [mine] + [shift(mine, "tok", -k) for k in range(1, count_tok)]

    fields = block_fields(
        (rows, cols, taps), cells, (low, high), (share, share_low, share_high), conv_weight,
        ln_gain, proj, layer_scale, every,
    )
    return fields.reshape(1, rows, cols, width)


def solution(mesh):
    return jax.shard_map(
        local,
        mesh=mesh,
        in_specs=(
            P("fc", "tok", None, None),
            P(),
            P(),
            P(),
            P(("fc", "tok"), None, None),
            P(("fc", "tok"), None, None),
            P(),
            P(),
            P(),
            P(),
        ),
        out_specs=P("fc", "tok", None, None),
        check_vma=False,
    )
```

time: 196 us -> 110 us (0.56)
  the two profiles are of different devices: /device:TPU:4 before, /device:TPU:0 now
where the time goes in v1:
time: 110 us
  Pallas kernels  55.8 us (51%)
  starting transfers between devices  25.6 us (23%)
  waiting for transfers between devices  17.4 us (16%)
  local copies, waits for them, and re-layouts  10.7 us (10%)
    pallas_call x1, Pallas kernels, block_fields(): pl.pallas_call(functools.partial(block_kernel, dims), out_shape=jax.Shape...  35.7 us
    ppermute x12, starting transfers between devices, shift(): lax.ppermute(value, axis, [(i, (i + step) % count) for i in range(count)])  21 us
    ppermute x12, waiting for transfers between devices, shift(): lax.ppermute(value, axis, [(i, (i + step) % count) for i in range(count)])  17.3 us
    unnamed x29, local copies, waits for them, and re-layouts  9.45 us
    pallas_call x3, Pallas kernels, combine_weights(): pl.pallas_call(combine_kernel, out_shape=jax.ShapeDtypeStruct((total, slo...  8.74 us
    pallas_call x1, Pallas kernels, dispatch(): pl.pallas_call(functools.partial(dispatch_kernel, layout), out_shape=[jax...  6.93 us
    pallas_call x1, Pallas kernels, experts(): pl.pallas_call(functools.partial(expert_kernel, count_z, slots_exp), out_...  3.58 us
    ppermute x1, starting transfers between devices, local(): low = lax.ppermute(cells[(rows - reach) * cols:], 'tok', forward)  2.75 us
  transfers between devices with their start and end apart: 16, of which 7 were waited for; matrix products, arithmetic and copies ran while one was open for 1% of the time, Pallas kernels for 18%

profile of v1, /device:TPU:0, one launch (start us, length us, event | category | flops | bytes accessed | tf_op | source)
XLA Modules:
  0.0 109.7 jit_solution(12898479269609933938)
XLA Ops:
  0.6 1.6 %copy-done = bf16[1,8,128,1024]{3,2,1,0:T(8,128)(2,1)S(1)} copy-done((bf16[1,8,128,1024]{3,2,1,0:T(8,128)(2,1)S(1)}, bf16[1,8,128,1024]{3,2,1,0:T(8,128)(2,1)}, u32[]{:S(2)}) %copy-start) | copy-done | bytes 2097176
  3.9 6.9 %dispatch.1 = (bf16[256,1024]{1,0:T(8,128)(2,1)S(1)}, bf16[64,1152]{1,0:T(8,128)(2,1)S(1)}, bf16[64,1152]{1,0:T(8,128)(2,1)S(1)}, bf16[64,1152]{1,0:T(8,128)(2,1)S(1)}, bf16[64,1152]{1,0:T(8,128)(2,1)S(1)}) custom-call(s32[2]{0:T(128)S(1)} %pad_add_fusion.index_ref, bf16[1024,1024]{1,0:T(8,128)(2,1)S(1)} %bitcast.13, bf16[1024,256]{1,0:T(8,128)(2,1)S(1)} %copy-done.9, ...), custom_call_target="tpu_custom_call" | custom-call | flops 1073741824 | bytes 4194304 | tf_op jit(solution)/shard_map/dispatch/pallas_call | solution.py:77
  10.9 3.0 %collective-permute-start.4 = (bf16[64,1152]{1,0:T(8,128)(2,1)S(1)}, bf16[64,1152]{1,0:T(8,128)(2,1)S(1)}, u32[]{:S(2)}, u32[]{:S(2)}) collective-permute-start(bf16[64,1152]{1,0:T(8,128)(2,1)S(1)} %get-tuple-element.20), channel_id=1, source_target_pairs={{0,1},{1,2},{2,3},{3,0},{4,5},{5,6},{6,7},{7,4},{8,9},{9,10},{10,1... | collective-permute-start | bytes 442376 | tf_op jit(solution)/shard_map/ppermute | solution.py:352
  13.8 1.5 %collective-permute-start.5 = (bf16[64,1152]{1,0:T(8,128)(2,1)S(1)}, bf16[64,1152]{1,0:T(8,128)(2,1)S(1)}, u32[]{:S(2)}, u32[]{:S(2)}) collective-permute-start(bf16[64,1152]{1,0:T(8,128)(2,1)S(1)} %get-tuple-element.21), channel_id=1, source_target_pairs={{0,2},{1,3},{2,0},{3,1},{4,6},{5,7},{6,4},{7,5},{8,10},{9,11},{10,... | collective-permute-start | bytes 442376 | tf_op jit(solution)/shard_map/ppermute | solution.py:352
  15.4 1.4 %collective-permute-start.6 = (bf16[64,1152]{1,0:T(8,128)(2,1)S(1)}, bf16[64,1152]{1,0:T(8,128)(2,1)S(1)}, u32[]{:S(2)}, u32[]{:S(2)}) collective-permute-start(bf16[64,1152]{1,0:T(8,128)(2,1)S(1)} %get-tuple-element.22), channel_id=1, source_target_pairs={{0,3},{1,0},{2,1},{3,2},{4,7},{5,4},{6,5},{7,6},{8,11},{9,8},{10,9... | collective-permute-start | bytes 442376 | tf_op jit(solution)/shard_map/ppermute | solution.py:352
  18.1 1.4 %collective-permute-done.4.refs_1_ = bf16[64,1152]{1,0:T(8,128)(2,1)S(1)} collective-permute-done((bf16[64,1152]{1,0:T(8,128)(2,1)S(1)}, bf16[64,1152]{1,0:T(8,128)(2,1)S(1)}, u32[]{:S(2)}, u32[]{:S(2)}) %collective-permute-start.4) | collective-permute-done | bytes 147488 | tf_op jit(solution)/shard_map/ppermute | solution.py:352
  19.5 2.7 %collective-permute-start = (bf16[384,1024]{1,0:T(8,128)(2,1)}, bf16[384,1024]{1,0:T(8,128)(2,1)S(1)}, u32[]{:S(2)}, u32[]{:S(2)}) collective-permute-start(bf16[384,1024]{1,0:T(8,128)(2,1)} %bitcast.1), channel_id=1, source_target_pairs={{0,1},{1,2},{2,3},{4,5},{5,6},{6,7},{8,9},{9,10},{10,11},{12,13},{... | collective-permute-start | bytes 2359304 | tf_op jit(solution)/shard_map/ppermute | solution.py:364
  24.4 1.6 %collective-permute-start.7 = (bf16[16,1024]{1,0:T(8,128)(2,1)S(1)}, bf16[16,1024]{1,0:T(8,128)(2,1)S(1)}, u32[]{:S(2)}, u32[]{:S(2)}) collective-permute-start(bf16[16,1024]{1,0:T(8,128)(2,1)S(1)} %get-tuple-element.24), channel_id=1, source_target_pairs={{0,8},{4,12},{8,16},{12,20},{16,24},{20,28},{24,0},{28,4},{1,9},{5... | collective-permute-start | bytes 98312 | tf_op jit(solution)/shard_map/ppermute | solution.py:352
  26.0 4.1 %collective-permute-done.7.refs_1_ = bf16[16,1024]{1,0:T(8,128)(2,1)S(1)} collective-permute-done((bf16[16,1024]{1,0:T(8,128)(2,1)S(1)}, bf16[16,1024]{1,0:T(8,128)(2,1)S(1)}, u32[]{:S(2)}, u32[]{:S(2)}) %collective-permute-start.7) | collective-permute-done | bytes 32800 | tf_op jit(solution)/shard_map/ppermute | solution.py:352
  31.0 4.3 %collective-permute-done.8.refs_2_ = bf16[16,1024]{1,0:T(8,128)(2,1)S(1)} collective-permute-done((bf16[16,1024]{1,0:T(8,128)(2,1)S(1)}, bf16[16,1024]{1,0:T(8,128)(2,1)S(1)}, u32[]{:S(2)}, u32[]{:S(2)}) %collective-permute-start.8) | collective-permute-done | bytes 32800 | tf_op jit(solution)/shard_map/ppermute | solution.py:352
  35.3 1.7 %collective-permute-start.9 = (bf16[16,1024]{1,0:T(8,128)(2,1)}, bf16[16,1024]{1,0:T(8,128)(2,1)S(1)}, u32[]{:S(2)}, u32[]{:S(2)}) collective-permute-start(bf16[16,1024]{1,0:T(8,128)(2,1)} %get-tuple-element.26), channel_id=1, source_target_pairs={{0,24},{4,28},{8,0},{12,4},{16,8},{20,12},{24,16},{28,20},{1,25},{... | collective-permute-start | bytes 98312 | tf_op jit(solution)/shard_map/ppermute | solution.py:352
  37.0 2.4 %collective-permute-done.9.refs_3_ = bf16[16,1024]{1,0:T(8,128)(2,1)S(1)} collective-permute-done((bf16[16,1024]{1,0:T(8,128)(2,1)}, bf16[16,1024]{1,0:T(8,128)(2,1)S(1)}, u32[]{:S(2)}, u32[]{:S(2)}) %collective-permute-start.9) | collective-permute-done | bytes 32800 | tf_op jit(solution)/shard_map/ppermute | solution.py:352
  40.8 1.6 %copy-done.2 = bf16[2,1024,512]{2,1,0:T(8,128)(2,1)S(1)} copy-done((bf16[2,1024,512]{2,1,0:T(8,128)(2,1)S(1)}, bf16[2,1024,512]{2,1,0:T(8,128)(2,1)}, u32[]{:S(2)}) %copy-start.2) | copy-done | bytes 2097176
  42.4 1.6 %copy-done.3 = bf16[2,512,1024]{2,1,0:T(8,128)(2,1)S(1)} copy-done((bf16[2,512,1024]{2,1,0:T(8,128)(2,1)S(1)}, bf16[2,512,1024]{2,1,0:T(8,128)(2,1)}, u32[]{:S(2)}) %copy-start.3) | copy-done | bytes 2097176
  43.9 1.6 %copy-done.5 = bf16[2,1024,512]{2,1,0:T(8,128)(2,1)S(1)} copy-done((bf16[2,1024,512]{2,1,0:T(8,128)(2,1)S(1)}, bf16[2,1024,512]{2,1,0:T(8,128)(2,1)}, u32[]{:S(2)}) %copy-start.5) | copy-done | bytes 2097176
  45.5 3.6 %experts.1 = (bf16[16,1024]{1,0:T(8,128)(2,1)S(1)}, bf16[16,1024]{1,0:T(8,128)(2,1)S(1)}, bf16[16,1024]{1,0:T(8,128)(2,1)S(1)}, bf16[16,1024]{1,0:T(8,128)(2,1)S(1)}) custom-call(s32[1]{0:T(128)} %bitcast.10.core_ref, bf16[2,1024,512]{2,1,0:T(8,128)(2,1)S(1)} %copy-done.2, bf16[2,1024,512]{2,1,0:T(8,128)(2,1)S(1)} %copy-done.5, ...), custom_call_target="tpu_custom_call" | custom-call | flops 536870912 | bytes 8388608 | tf_op jit(solution)/shard_map/experts/pallas_call | solution.py:158
  49.1 3.6 %collective-permute-start.10 = (bf16[16,1024]{1,0:T(8,128)(2,1)S(1)}, bf16[16,1024]{1,0:T(8,128)(2,1)S(1)}, u32[]{:S(2)}, u32[]{:S(2)}) collective-permute-start(bf16[16,1024]{1,0:T(8,128)(2,1)S(1)} %get-tuple-element.28), channel_id=1, source_target_pairs={{0,24},{4,28},{8,0},{12,4},{16,8},{20,12},{24,16},{28,20},{1,25},{... | collective-permute-start | bytes 98312 | tf_op jit(solution)/shard_map/ppermute | solution.py:352
  54.3 3.2 %collective-permute-done.11 = bf16[16,1024]{1,0:T(8,128)(2,1)S(1)} collective-permute-done((bf16[16,1024]{1,0:T(8,128)(2,1)S(1)}, bf16[16,1024]{1,0:T(8,128)(2,1)S(1)}, u32[]{:S(2)}, u32[]{:S(2)}) %collective-permute-start.11) | collective-permute-done | bytes 32800 | tf_op jit(solution)/shard_map/ppermute | solution.py:352
  58.4 4.7 %collective-permute-start.13 = (bf16[64,1024]{1,0:T(8,128)(2,1)S(1)}, bf16[64,1024]{1,0:T(8,128)(2,1)}, u32[]{:S(2)}, u32[]{:S(2)}) collective-permute-start(bf16[64,1024]{1,0:T(8,128)(2,1)S(1)} %constant_dynamic-update-slice_fusion.rest_0_), channel_id=1, source_target_pairs={{0,3},{1,0},{2,1},{3,2},{4,7},{5,4},{6,5},{7,6},{8,11},{9,8},{10,9... | collective-permute-start | bytes 393224 | tf_op jit(solution)/shard_map/ppermute | solution.py:352
  63.1 2.0 %collective-permute-start.15 = (bf16[64,1024]{1,0:T(8,128)(2,1)S(1)}, bf16[64,1024]{1,0:T(8,128)(2,1)}, u32[]{:S(2)}, u32[]{:S(2)}) collective-permute-start(bf16[64,1024]{1,0:T(8,128)(2,1)S(1)} %constant_dynamic-update-slice_fusion.rest_0_), channel_id=1, source_target_pairs={{0,1},{1,2},{2,3},{3,0},{4,5},{5,6},{6,7},{7,4},{8,9},{9,10},{10,1... | collective-permute-start | bytes 393224 | tf_op jit(solution)/shard_map/ppermute | solution.py:352
  65.2 4.2 %combine_weights.3.share_ref = bf16[1024,256]{1,0:T(8,128)(2,1)S(1)} custom-call(s32[1]{0:T(128)} %constant.29.clone.1.valid_ref, bf16[1024,1024]{1,0:T(8,128)(2,1)S(1)} %bitcast.14, bf16[256,1024]{1,0:T(8,128)(2,1)S(1)} %get-tuple-element.18.keys_ref, f32[1,1024]{1,0:T(1,128)S(1)} %bitcast.17), custom_call_target="tpu_custom_call" | custom-call | flops 536870912 | bytes 2097152 | tf_op jit(solution)/shard_map/combine_weights/pallas_call | solution.py:183
  69.4 1.6 %combine_weights.4.share_low = bf16[384,256]{1,0:T(8,128)(2,1)S(1)} custom-call(s32[1]{0:T(128)} %bitcast.6.valid_ref, bf16[384,1024]{1,0:T(8,128)(2,1)S(1)} %collective-permute-done.cells_ref.low_ref, bf16[256,1024]{1,0:T(8,128)(2,1)S(1)} %get-tuple-element.18.keys_ref, f32[1,1024]{1,0:T(1,128)S(1)} %bitcast.18), custom_call_target="tpu_custom_call" | custom-call | flops 201326592 | bytes 786432 | tf_op jit(solution)/shard_map/combine_weights/pallas_call | solution.py:183
  71.0 3.0 %combine_weights.5.share_high = bf16[384,256]{1,0:T(8,128)(2,1)S(1)} custom-call(s32[1]{0:T(128)} %bitcast.7.valid_ref, bf16[384,1024]{1,0:T(8,128)(2,1)} %collective-permute-done.1.cells_ref.high_ref, bf16[256,1024]{1,0:T(8,128)(2,1)S(1)} %get-tuple-element.18.keys_ref, f32[1,1024]{1,0:T(1,128)S(1)} %bitcast.19), custom_call_target="tpu_custom_call" | custom-call | flops 201326592 | bytes 786432 | tf_op jit(solution)/shard_map/combine_weights/pallas_call | solution.py:183
  74.1 35.7 %block_fields.1 = bf16[1024,1024]{1,0:T(8,128)(2,1)} custom-call(bf16[1024,1024]{1,0:T(8,128)(2,1)S(1)} %bitcast.15, bf16[384,1024]{1,0:T(8,128)(2,1)S(1)} %collective-permute-done.cells_ref.low_ref, bf16[384,1024]{1,0:T(8,128)(2,1)} %collective-permute-done.1.cells_ref.high_ref, bf16[1024,256]{1,0:T(8,128)(2,1)S(1)} %combine_weights.3.share_ref, ...), custom_call_target="tpu_custom_call" | custom-call | flops 4294967296 | bytes 8388608 | tf_op jit(solution)/shard_map/block_fields/pallas_call | solution.py:316
  (47 shorter events, 10.5 us)
Async XLA Ops:
  0.0 39.4 %collective-permute-start.2 = (bf16[2,1024,512]{2,1,0:T(8,128)(2,1)}, bf16[2,1024,512]{2,1,0:T(8,128)(2,1)S(1)}, u32[]{:S(2)}, u32[]{:S(2)}) collective-permute-start(bf16[2,1024,512]{2,1,0:T(8,128)(2,1)} %in_a.1), channel_id=1, source_target_pairs={{0,4},{4,0},{8,12},{12,8},{16,20},{20,16},{24,28},{28,24},{1,5},{5... | collective-permute-start | bytes 6291464 | tf_op jit(solution)/shard_map/ppermute | solution.py:355
  0.5 40.3 %collective-permute-start.3 = (bf16[2,512,1024]{2,1,0:T(8,128)(2,1)}, bf16[2,512,1024]{2,1,0:T(8,128)(2,1)}, u32[]{:S(2)}, u32[]{:S(2)}) collective-permute-start(bf16[2,512,1024]{2,1,0:T(8,128)(2,1)} %out_a.1), channel_id=1, source_target_pairs={{0,4},{4,0},{8,12},{12,8},{16,20},{20,16},{24,28},{28,24},{1,5},{5... | collective-permute-start | bytes 6291464 | tf_op jit(solution)/shard_map/ppermute | solution.py:356
  0.6 1.6 %copy-start = (bf16[1,8,128,1024]{3,2,1,0:T(8,128)(2,1)S(1)}, bf16[1,8,128,1024]{3,2,1,0:T(8,128)(2,1)}, u32[]{:S(2)}) copy-start(bf16[1,8,128,1024]{3,2,1,0:T(8,128)(2,1)} %param.10) | copy-start | bytes 6291460
  10.8 12.7 %copy-start.8 = (f32[1024]{0:T(1024)S(1)}, f32[1024]{0:T(1024)}, u32[]{:S(2)}) copy-start(f32[1024]{0:T(1024)} %param.13) | copy-start | bytes 12292
  10.9 8.6 %collective-permute-start.4 = (bf16[64,1152]{1,0:T(8,128)(2,1)S(1)}, bf16[64,1152]{1,0:T(8,128)(2,1)S(1)}, u32[]{:S(2)}, u32[]{:S(2)}) collective-permute-start(bf16[64,1152]{1,0:T(8,128)(2,1)S(1)} %get-tuple-element.20), channel_id=1, source_target_pairs={{0,1},{1,2},{2,3},{3,0},{4,5},{5,6},{6,7},{7,4},{8,9},{9,10},{10,1... | collective-permute-start | bytes 442376 | tf_op jit(solution)/shard_map/ppermute | solution.py:352
  13.8 8.4 %collective-permute-start.5 = (bf16[64,1152]{1,0:T(8,128)(2,1)S(1)}, bf16[64,1152]{1,0:T(8,128)(2,1)S(1)}, u32[]{:S(2)}, u32[]{:S(2)}) collective-permute-start(bf16[64,1152]{1,0:T(8,128)(2,1)S(1)} %get-tuple-element.21), channel_id=1, source_target_pairs={{0,2},{1,3},{2,0},{3,1},{4,6},{5,7},{6,4},{7,5},{8,10},{9,11},{10,... | collective-permute-start | bytes 442376 | tf_op jit(solution)/shard_map/ppermute | solution.py:352
  15.4 8.2 %collective-permute-start.6 = (bf16[64,1152]{1,0:T(8,128)(2,1)S(1)}, bf16[64,1152]{1,0:T(8,128)(2,1)S(1)}, u32[]{:S(2)}, u32[]{:S(2)}) collective-permute-start(bf16[64,1152]{1,0:T(8,128)(2,1)S(1)} %get-tuple-element.22), channel_id=1, source_target_pairs={{0,3},{1,0},{2,1},{3,2},{4,7},{5,4},{6,5},{7,6},{8,11},{9,8},{10,9... | collective-permute-start | bytes 442376 | tf_op jit(solution)/shard_map/ppermute | solution.py:352
  19.5 49.9 %collective-permute-start = (bf16[384,1024]{1,0:T(8,128)(2,1)}, bf16[384,1024]{1,0:T(8,128)(2,1)S(1)}, u32[]{:S(2)}, u32[]{:S(2)}) collective-permute-start(bf16[384,1024]{1,0:T(8,128)(2,1)} %bitcast.1), channel_id=1, source_target_pairs={{0,1},{1,2},{2,3},{4,5},{5,6},{6,7},{8,9},{9,10},{10,11},{12,13},{... | collective-permute-start | bytes 2359304 | tf_op jit(solution)/shard_map/ppermute | solution.py:364
  22.3 48.7 %collective-permute-start.1 = (bf16[384,1024]{1,0:T(8,128)(2,1)}, bf16[384,1024]{1,0:T(8,128)(2,1)}, u32[]{:S(2)}, u32[]{:S(2)}) collective-permute-start(bf16[384,1024]{1,0:T(8,128)(2,1)} %bitcast.2), channel_id=1, source_target_pairs={{1,0},{2,1},{3,2},{5,4},{6,5},{7,6},{9,8},{10,9},{11,10},{13,12},{... | collective-permute-start | bytes 2359304 | tf_op jit(solution)/shard_map/ppermute | solution.py:365
  24.4 5.7 %collective-permute-start.7 = (bf16[16,1024]{1,0:T(8,128)(2,1)S(1)}, bf16[16,1024]{1,0:T(8,128)(2,1)S(1)}, u32[]{:S(2)}, u32[]{:S(2)}) collective-permute-start(bf16[16,1024]{1,0:T(8,128)(2,1)S(1)} %get-tuple-element.24), channel_id=1, source_target_pairs={{0,8},{4,12},{8,16},{12,20},{16,24},{20,28},{24,0},{28,4},{1,9},{5... | collective-permute-start | bytes 98312 | tf_op jit(solution)/shard_map/ppermute | solution.py:352
  30.2 5.1 %collective-permute-start.8 = (bf16[16,1024]{1,0:T(8,128)(2,1)S(1)}, bf16[16,1024]{1,0:T(8,128)(2,1)S(1)}, u32[]{:S(2)}, u32[]{:S(2)}) collective-permute-start(bf16[16,1024]{1,0:T(8,128)(2,1)S(1)} %get-tuple-element.25), channel_id=1, source_target_pairs={{0,16},{4,20},{8,24},{12,28},{16,0},{20,4},{24,8},{28,12},{1,17},{... | collective-permute-start | bytes 98312 | tf_op jit(solution)/shard_map/ppermute | solution.py:352
  35.3 4.1 %collective-permute-start.9 = (bf16[16,1024]{1,0:T(8,128)(2,1)}, bf16[16,1024]{1,0:T(8,128)(2,1)S(1)}, u32[]{:S(2)}, u32[]{:S(2)}) collective-permute-start(bf16[16,1024]{1,0:T(8,128)(2,1)} %get-tuple-element.26), channel_id=1, source_target_pairs={{0,24},{4,28},{8,0},{12,4},{16,8},{20,12},{24,16},{28,20},{1,25},{... | collective-permute-start | bytes 98312 | tf_op jit(solution)/shard_map/ppermute | solution.py:352
  40.8 1.6 %copy-start.2 = (bf16[2,1024,512]{2,1,0:T(8,128)(2,1)S(1)}, bf16[2,1024,512]{2,1,0:T(8,128)(2,1)}, u32[]{:S(2)}) copy-start(bf16[2,1024,512]{2,1,0:T(8,128)(2,1)} %in_a.1) | copy-start | bytes 6291460
  45.5 19.6 %copy-start.1 = (bf16[1,8,128,1024]{3,2,1,0:T(8,128)(2,1)S(1)}, bf16[1,8,128,1024]{3,2,1,0:T(8,128)(2,1)}, u32[]{:S(2)}) copy-start(bf16[1,8,128,1024]{3,2,1,0:T(8,128)(2,1)} %param.10) | copy-start | bytes 6291460
  45.5 19.6 %copy-start.7 = (f32[1024]{0:T(1024)S(1)}, f32[1024]{0:T(1024)}, u32[]{:S(2)}) copy-start(f32[1024]{0:T(1024)} %param.12) | copy-start | bytes 12292
  49.1 5.2 %collective-permute-start.10 = (bf16[16,1024]{1,0:T(8,128)(2,1)S(1)}, bf16[16,1024]{1,0:T(8,128)(2,1)S(1)}, u32[]{:S(2)}, u32[]{:S(2)}) collective-permute-start(bf16[16,1024]{1,0:T(8,128)(2,1)S(1)} %get-tuple-element.28), channel_id=1, source_target_pairs={{0,24},{4,28},{8,0},{12,4},{16,8},{20,12},{24,16},{28,20},{1,25},{... | collective-permute-start | bytes 98312 | tf_op jit(solution)/shard_map/ppermute | solution.py:352
  52.7 4.8 %collective-permute-start.11 = (bf16[16,1024]{1,0:T(8,128)(2,1)S(1)}, bf16[16,1024]{1,0:T(8,128)(2,1)S(1)}, u32[]{:S(2)}, u32[]{:S(2)}) collective-permute-start(bf16[16,1024]{1,0:T(8,128)(2,1)S(1)} %get-tuple-element.29), channel_id=1, source_target_pairs={{0,16},{4,20},{8,24},{12,28},{16,0},{20,4},{24,8},{28,12},{1,17},{... | collective-permute-start | bytes 98312 | tf_op jit(solution)/shard_map/ppermute | solution.py:352
  52.7 5.7 %collective-permute-start.12 = (bf16[16,1024]{1,0:T(8,128)(2,1)S(1)}, bf16[16,1024]{1,0:T(8,128)(2,1)S(1)}, u32[]{:S(2)}, u32[]{:S(2)}) collective-permute-start(bf16[16,1024]{1,0:T(8,128)(2,1)S(1)} %get-tuple-element.30), channel_id=1, source_target_pairs={{0,8},{4,12},{8,16},{12,20},{16,24},{20,28},{24,0},{28,4},{1,9},{5... | collective-permute-start | bytes 98312 | tf_op jit(solution)/shard_map/ppermute | solution.py:352
  58.4 15.6 %collective-permute-start.13 = (bf16[64,1024]{1,0:T(8,128)(2,1)S(1)}, bf16[64,1024]{1,0:T(8,128)(2,1)}, u32[]{:S(2)}, u32[]{:S(2)}) collective-permute-start(bf16[64,1024]{1,0:T(8,128)(2,1)S(1)} %constant_dynamic-update-slice_fusion.rest_0_), channel_id=1, source_target_pairs={{0,3},{1,0},{2,1},{3,2},{4,7},{5,4},{6,5},{7,6},{8,11},{9,8},{10,9... | collective-permute-start | bytes 393224 | tf_op jit(solution)/shard_map/ppermute | solution.py:352
  63.1 10.9 %collective-permute-start.14 = (bf16[64,1024]{1,0:T(8,128)(2,1)S(1)}, bf16[64,1024]{1,0:T(8,128)(2,1)}, u32[]{:S(2)}, u32[]{:S(2)}) collective-permute-start(bf16[64,1024]{1,0:T(8,128)(2,1)S(1)} %constant_dynamic-update-slice_fusion.rest_0_), channel_id=1, source_target_pairs={{0,2},{1,3},{2,0},{3,1},{4,6},{5,7},{6,4},{7,5},{8,10},{9,11},{10,... | collective-permute-start | bytes 393224 | tf_op jit(solution)/shard_map/ppermute | solution.py:352
  63.1 10.9 %collective-permute-start.15 = (bf16[64,1024]{1,0:T(8,128)(2,1)S(1)}, bf16[64,1024]{1,0:T(8,128)(2,1)}, u32[]{:S(2)}, u32[]{:S(2)}) collective-permute-start(bf16[64,1024]{1,0:T(8,128)(2,1)S(1)} %constant_dynamic-update-slice_fusion.rest_0_), channel_id=1, source_target_pairs={{0,1},{1,2},{2,3},{3,0},{4,5},{5,6},{6,7},{7,4},{8,9},{9,10},{10,1... | collective-permute-start | bytes 393224 | tf_op jit(solution)/shard_map/ppermute | solution.py:352
  69.4 4.7 %copy-start.10 = (f32[7,7,1024]{2,1,0:T(8,128)S(1)}, f32[7,7,1024]{2,1,0:T(8,128)}, u32[]{:S(2)}) copy-start(f32[7,7,1024]{2,1,0:T(8,128)} %weight_ref.1) | copy-start | bytes 602116
  69.4 4.7 %copy-start.11 = (f32[1024]{0:T(1024)S(1)}, f32[1024]{0:T(1024)}, u32[]{:S(2)}) copy-start(f32[1024]{0:T(1024)} %param.17) | copy-start | bytes 12292
  69.4 4.7 %copy-start.12 = (f32[1024]{0:T(1024)S(1)}, f32[1024]{0:T(1024)}, u32[]{:S(2)}) copy-start(f32[1024]{0:T(1024)} %param.19) | copy-start | bytes 12292
  (5 other events, 6.2 us)

commit v2 on v1

v2 whole, which is shorter than its diff:
```python
import functools

import jax
import jax.numpy as jnp
import ml_dtypes
import numpy as np
from jax import lax
from jax.experimental import pallas as pl
from jax.experimental.pallas import tpu as pltpu
from jax.sharding import PartitionSpec as P

F32 = jnp.float32
BF16 = jnp.bfloat16
LANES = 128
EPS = 1e-06
MIB = 1024 * 1024
LIMIT_D = 16
LIMIT_E = 16
NT = (((1,), (1,)), ((), ()))
VMEM = pl.BlockSpec(memory_space=pltpu.VMEM)
SMEM = pl.BlockSpec(memory_space=pltpu.SMEM)
HBM = pl.BlockSpec(memory_space=pltpu.HBM)
ANY = pl.BlockSpec(memory_space=pl.ANY)


def dot_nt(left, right):
    return lax.dot_general(left, right, NT, preferred_element_type=F32)


def rms_scale(value, gain):
    return value * lax.rsqrt(jnp.mean(value * value, axis=-1, keepdims=True) + EPS) * gain


def split_index(value, count):
    if count & (count - 1) == 0:
        return value >> (count.bit_length() - 1), value & (count - 1)
    return value // count, lax.rem(value, count)


def cost(flops, moved, exps=0):
    return pl.CostEstimate(flops=flops, bytes_accessed=moved, transcendentals=exps)


def dispatch_kernel(layout, index_ref, cells_hbm, keys_hbm, gain_ref, keys_out, *rest):
    count_z, count_tok, slot_dev = layout
    outs, (cells_ref, keys_ref, normed_ref, cell_sems, key_sem) = rest[:-5], rest[-5:]
    total, width = cells_ref.shape
    slots = keys_ref.shape[1]
    my_z, my_tok = index_ref[0], index_ref[1]
    count = cell_sems.shape[0]
    block = total // count
    key_copy = pltpu.make_async_copy(keys_hbm, keys_ref, key_sem)
    key_copy.start()
    copies = []
    for step in range(count):
        rows = slice(step * block, (step + 1) * block)
        copies.append(
            pltpu.make_async_copy(cells_hbm.at[rows], cells_ref.at[rows], cell_sems.at[step])
        )
        copies[-1].start()
    place = lax.broadcasted_iota(jnp.int32, (slots, 1), 0)
    source = lax.broadcasted_iota(jnp.int32, (slots, slots), 1)
    outer, inner = split_index(place, slot_dev)
    outer, core = split_index(outer, 2)
    step_tok, step_z = split_index(outer, count_z)
    at_z = split_index(step_z + my_z, count_z)[1]
    at_tok = split_index(step_tok + my_tok, count_tok)[1]
    wanted = ((at_z * 2 + core) * count_tok + at_tok) * slot_dev + inner
    pick = jnp.where(wanted == source, 1.0, 0.0).astype(BF16)
    key_copy.wait()
    keys = dot_nt(pick, keys_ref[...]).astype(BF16)
    keys_out[...] = keys

    for step in range(count):
        rows = slice(step * block, (step + 1) * block)
        copies[step].wait()
        normed_ref[rows, :] = rms_scale(cells_ref[rows, :].astype(F32), gain_ref[...]).astype(BF16)

    part = slots // count_tok
    logits = dot_nt(keys, normed_ref[...])
    peak = jnp.max(logits, axis=1, keepdims=True)
    weight = jnp.exp(logits - peak).astype(BF16)
    first = peak.astype(BF16).astype(F32)
    second = (peak - first).astype(BF16).astype(F32)
    third = peak - first - second
    lane = lax.broadcasted_iota(jnp.int32, (slots, LANES), 1)
    marks = jnp.where(
        lane == 0, first, jnp.where(lane == 1, second, jnp.where(lane == 2, third, 0.0))
    ).astype(BF16)
    for at, out in enumerate(outs):
        out[:, width:] = marks[at * part : (at + 1) * part, :]
    for lane in range(0, width, 2 * LANES):
        lanes = slice(lane, lane + 2 * LANES)
        numer = jnp.dot(weight, cells_ref[:, lanes], preferred_element_type=F32).astype(BF16)
        for at, out in enumerate(outs):
            out[:, lanes] = numer[at * part : (at + 1) * part, :]


def dispatch(index, cells, keys, gain, layout):
    count_z, count_tok, slot_dev = layout
    total, width = cells.shape
    slots = keys.shape[1]
    part = slots // count_tok
    count = 8
    return pl.pallas_call(
        functools.partial(dispatch_kernel, layout),
        out_shape=[jax.ShapeDtypeStruct((slots, width), BF16)]
        + [jax.ShapeDtypeStruct((part, width + LANES), BF16)] * count_tok,
        in_specs=[SMEM, HBM, HBM, VMEM],
        out_specs=[VMEM] * (1 + count_tok),
        scratch_shapes=[
            pltpu.VMEM((total, width), BF16),
            pltpu.VMEM((width, slots), BF16),
            pltpu.VMEM((total, width), BF16),
            pltpu.SemaphoreType.DMA((count,)),
            pltpu.SemaphoreType.DMA,
        ],
        compiler_params=pltpu.CompilerParams(vmem_limit_bytes=LIMIT_D * MIB),
        cost_estimate=cost(4 * total * width * slots, 4 * total * width, total * slots),
        name="dispatch",
    )(index, cells, keys, gain)


def gather_kernel(count_z, gain_ref, *refs):
    count = len(refs) - count_z
    parts, outs = refs[:count], refs[count:]
    width = gain_ref.shape[1]
    peaks = []
    for ref in parts:
        piece = ref[:, width:].astype(F32)
        peaks.append(jnp.sum(piece, axis=1, keepdims=True))
    peak = functools.reduce(jnp.maximum, peaks)
    numer = None
    for ref, own in zip(parts, peaks):
        term = ref[:, :width].astype(F32) * jnp.exp(own - peak)
        numer = term if numer is None else numer + term
    value = rms_scale(numer, gain_ref[...]).astype(BF16)
    rows = value.shape[0] // count_z
    for at, out in enumerate(outs):
        out[...] = value[at * rows : (at + 1) * rows, :]


def gather_slots(parts, gain, count_z):
    rows, width = parts[0].shape[0] // count_z, gain.shape[1]
    return pl.pallas_call(
        functools.partial(gather_kernel, count_z),
        out_shape=[jax.ShapeDtypeStruct((rows, width), BF16)] * count_z,
        in_specs=[VMEM] * (1 + len(parts)),
        out_specs=[VMEM] * count_z,
        compiler_params=pltpu.CompilerParams(vmem_limit_bytes=8 * MIB),
        cost_estimate=cost(8 * len(parts) * rows * count_z * width, 4 * rows * count_z * width),
        name="gather_slots",
    )(gain, *parts)


def expert_kernel(count_z, slots_exp, core_ref, _, in_own, out_own, in_other, out_other, *refs):
    parts, outs = refs[:count_z], refs[count_z : 2 * count_z]
    rows_ref, sum_ref, in_ref, out_ref, sems = refs[2 * count_z :]
    each = parts[0].shape[0]
    per_core = in_own.shape[0]
    copies = []
    for which, pair in enumerate(((in_own, out_own), (in_other, out_other))):
        for at in range(per_core):
            place = which * per_core + at
            for kind, (source, target) in enumerate(zip(pair, (in_ref, out_ref))):
                copies.append(
                    pltpu.make_async_copy(
                        source.at[at], target.at[place], sems.at[2 * place + kind]
                    )
                )
                copies[-1].start()
    for at, ref in enumerate(parts):
        rows_ref[at * each : (at + 1) * each, :] = ref[...]
    rows = rows_ref[...]
    place = lax.broadcasted_iota(jnp.int32, (rows.shape[0], 1), 0)
    expert = lax.rem(place, each) // slots_exp
    core = core_ref[0]

    for at in range(2 * per_core):
        held = core if at < per_core else 1 - core
        mine = expert == held * per_core + at % per_core
        copies[2 * at].wait()
        hidden = jax.nn.gelu(jnp.dot(rows, in_ref[at], preferred_element_type=F32))
        hidden = jnp.where(mine, hidden, 0.0).astype(BF16)
        copies[2 * at + 1].wait()
        made = jnp.dot(hidden, out_ref[at], preferred_element_type=F32)
        if at == 0:
            sum_ref[...] = made
        else:
            sum_ref[...] += made
    for at, out in enumerate(outs):
        out[...] = sum_ref[at * each : (at + 1) * each, :].astype(BF16)


def experts(core, after, parts, w_in, w_out, in_other, out_other, slots_exp):
    count_z = len(parts)
    each, width = parts[0].shape
    per_core, _, inner = w_in.shape
    rows = each * count_z
    return pl.pallas_call(
        functools.partial(expert_kernel, count_z, slots_exp),
        out_shape=[jax.ShapeDtypeStruct((each, width), BF16)] * count_z,
        in_specs=[SMEM, ANY, HBM, HBM, HBM, HBM] + [VMEM] * count_z,
        out_specs=[VMEM] * count_z,
        scratch_shapes=[
            pltpu.VMEM((rows, width), BF16),
            pltpu.VMEM((rows, width), F32),
            pltpu.VMEM((2 * per_core, width, inner), BF16),
            pltpu.VMEM((2 * per_core, inner, width), BF16),
            pltpu.SemaphoreType.DMA((4 * per_core,)),
        ],
        compiler_params=pltpu.CompilerParams(vmem_limit_bytes=LIMIT_E * MIB),
        cost_estimate=cost(8 * rows * width * inner * per_core, 8 * width * inner * per_core),
        name="experts",
    )(core, after, w_in, w_out, in_other, out_other, *parts)


def copy_kernel(start_ref, cells_ref, _, out_ref):
    rows = out_ref.shape[0]
    out_ref[...] = cells_ref[pl.ds(pl.multiple_of(start_ref[0], LANES), rows), :]


def edge_rows(start, cells, rows, after):
    return pl.pallas_call(
        copy_kernel,
        out_shape=jax.ShapeDtypeStruct((rows, cells.shape[1]), BF16),
        in_specs=[SMEM, VMEM, ANY],
        out_specs=VMEM,
        compiler_params=pltpu.CompilerParams(vmem_limit_bytes=8 * MIB),
        cost_estimate=cost(0, 4 * rows * cells.shape[1]),
        name="edge_rows",
    )(start, cells, after)


def combine_kernel(count, valid_ref, keys_ref, gain_ref, _, *refs):
    block = 128
    for at, (cells_ref, out_ref) in enumerate(zip(refs[:count], refs[count:])):
        for start in range(0, cells_ref.shape[0], block):
            rows = slice(start, start + block)
            normed = rms_scale(cells_ref[rows, :].astype(F32), gain_ref[...]).astype(BF16)
            logits = dot_nt(normed, keys_ref[...])
            raised = jnp.exp(logits - jnp.max(logits, axis=-1, keepdims=True))
            share = raised * (1.0 / jnp.sum(raised, axis=-1, keepdims=True))
            out_ref[rows, :] = jnp.where(valid_ref[at] > 0, share, 0.0).astype(BF16)


def combine_weights(valid, cells, keys, gain, after):
    width, slots = gain.shape[1], keys.shape[0]
    total = sum(part.shape[0] for part in cells)
    return pl.pallas_call(
        functools.partial(combine_kernel, len(cells)),
        out_shape=[jax.ShapeDtypeStruct((part.shape[0], slots), BF16) for part in cells],
        in_specs=[SMEM, VMEM, VMEM, ANY] + [VMEM] * len(cells),
        out_specs=[VMEM] * len(cells),
        compiler_params=pltpu.CompilerParams(vmem_limit_bytes=16 * MIB),
        cost_estimate=cost(2 * total * width * slots, 2 * total * width, total * slots),
        name="combine_weights",
    )(valid, keys, gain, after, *cells)


def pieces(value, count):
    out = []
    for _ in range(count):
        piece = value.astype(BF16)
        out.append(piece)
        value = value - piece.astype(value.dtype)
    return out


def wave(cols, taps):
    half = cols // 2
    freq = np.arange(half)[:, None]
    angle = 2 * np.pi * ((freq * np.arange(cols)[None, :]) % cols) / cols
    sign = np.where(np.arange(cols) % 2 == 0, 1.0, -1.0)
    real, imag = np.cos(angle), -np.sin(angle)
    imag[0] = sign
    to_freq = np.concatenate([real, imag], axis=0)
    back_real, back_imag = 2 * np.cos(angle).T / cols, -2 * np.sin(angle).T / cols
    back_real[:, 0] = sign / cols
    back_imag[:, 0] = 1 / cols
    to_cols = np.concatenate([back_real, back_imag], axis=1)
    offset = np.arange(taps) - taps // 2
    turn = 2 * np.pi * freq * offset[None, :] / cols
    first, second, third = np.cos(turn), np.sin(turn) - np.cos(turn), np.sin(turn) + np.cos(turn)
    first[0], second[0] = 0.0, 1.0
    third[0] = np.where(offset % 2 == 0, -1.0, 1.0)
    spectrum = np.zeros((3 * half, 8))
    spectrum[:, :taps] = np.concatenate([first, second, third], axis=0)

    def split(value):
        high = value.astype(np.float32).astype(ml_dtypes.bfloat16)
        return high, (value - high.astype(np.float64)).astype(np.float32).astype(ml_dtypes.bfloat16)

    f_high, f_low = split(to_freq)
    c_high, c_low = split(to_cols)
    s_high, s_low = split(spectrum)
    return (
        np.concatenate([f_high, f_low], axis=1),
        np.concatenate([c_high, c_high], axis=1),
        c_low,
        np.concatenate([s_high, s_high, s_high, s_low, s_low], axis=1),
    )


def fill_spectrum(coef_ref, weight_ref, out_ref):
    taps, _, width = weight_ref.shape
    fill = jnp.zeros((8 - taps, width), F32)
    for tap in range(taps):
        row = jnp.concatenate([weight_ref[tap], fill], axis=0)
        one, two, three = (p.astype(F32) for p in pieces(row, 3))
        stack = jnp.concatenate([one, two, three, one, two], axis=0).astype(BF16)
        out_ref[tap] = jnp.dot(coef_ref[...], stack, preferred_element_type=F32)


def block_kernel(
    dims, place_ref, cells_ref, low_ref, high_ref, share_ref, share_low, share_high, weight_ref, freq_ref,
    cols_ref, fine_ref, coef_ref, ln_ref, proj_ref, scale_ref, *rest
):
    rows, cols, taps = dims
    slot_refs, out_ref = rest[:-7], rest[-7]
    slots_ref, state_ref, freqs_ref, back_ref, conv_ref, spectrum_ref = rest[-6:]
    reach = taps // 2
    half = cols // 2
    width = cells_ref.shape[1]
    start = 0
    for ref in slot_refs:
        slots_ref[start : start + ref.shape[0], :] = ref[...]
        start += ref.shape[0]
    fill_spectrum(coef_ref, weight_ref, spectrum_ref)

    chunk = 2 * LANES

    def mix(cells, share, row, to, keep):
        at = pl.ds(pl.multiple_of(row * cols, cols), cols)
        picked = share[at, :]
        for lane in range(0, width, chunk):
            lanes = slice(lane, lane + chunk)
            mixed = jnp.dot(picked, slots_ref[:, lanes], preferred_element_type=F32)
            state = (cells[at, lanes].astype(F32) + mixed).astype(BF16)
            if keep:
                state_ref[at, lanes] = state
            twice = jnp.concatenate([state, state], axis=0)
            freqs_ref[to, :, lanes] = jnp.dot(freq_ref[...], twice, preferred_element_type=F32)

    @pl.loop(0, reach)
    def _(row):
        mix(low_ref, share_low, row, row + place_ref[0], False)
        mix(high_ref, share_high, row, row + place_ref[1], False)

    @pl.loop(0, rows)
    def _(row):
        mix(cells_ref, share_ref, row, row + reach, True)

    tile = 16

    @pl.loop(0, width // LANES)
    def _(group):
        lanes = pl.ds(pl.multiple_of(group * LANES, LANES), LANES)

        @pl.loop(0, half // tile)
        def _(step):
            base = pl.multiple_of(step * tile, tile)
            for first in range(0, rows, 8):
                parts = ([], [])
                for sub in range(0, tile, 8):
                    real_at, imag_at = pl.ds(base + sub, 8), pl.ds(base + half + sub, 8)
                    third_at = pl.ds(base + 2 * half + sub, 8)
                    weights = [
                        [spectrum_ref[tap, at, lanes] for tap in range(taps)]
                        for at in (real_at, imag_at, third_at)
                    ]
                    sums = [[None] * 8 for _ in range(3)]
                    for row in range(8 + taps - 1):
                        real = freqs_ref[first + row, real_at, lanes]
                        imag = freqs_ref[first + row, imag_at, lanes]
                        for kind, value in enumerate((real + imag, real, imag)):
                            for to in range(max(0, row - taps + 1), min(8, row + 1)):
                                term = value * weights[kind][row - to]
                                have = sums[kind][to]
                                sums[kind][to] = term if have is None else have + term
                    parts[0].append([sums[0][to] - sums[2][to] for to in range(8)])
                    parts[1].append([sums[0][to] + sums[1][to] for to in range(8)])
                for to in range(8):
                    for which in range(2):
                        value = jnp.concatenate([sub[to] for sub in parts[which]], axis=0)
                        high, low = pieces(value, 2)
                        back_ref[first + to, pl.ds(base + which * half, tile), lanes] = high
                        back_ref[first + to, pl.ds(base + cols + which * half, tile), lanes] = low

    pair = 2 if rows % 2 == 0 else 1

    @pl.loop(0, rows // pair)
    def _(step):
        for one in range(pair):
            total = None
            for lane in range(0, width, chunk):
                lanes = slice(lane, lane + chunk)
                row = step * pair + one
                conv = jnp.dot(cols_ref[...], back_ref[row, :, lanes], preferred_element_type=F32)
                conv += jnp.dot(fine_ref[...], back_ref[row, :cols, lanes], preferred_element_type=F32)
                conv_ref[one * cols : (one + 1) * cols, lanes] = conv
        at = pl.ds(pl.multiple_of(step * (pair * cols), pair * cols), pair * cols)
        conv = conv_ref[...]
        center = conv - jnp.mean(conv, axis=-1, keepdims=True)
        spread = jnp.mean(center * center, axis=-1, keepdims=True)
        normal = (center * lax.rsqrt(spread + EPS) * ln_ref[...]).astype(BF16)
        for lane in range(0, width, chunk):
            lanes = slice(lane, lane + chunk)
            branch = jnp.dot(normal, proj_ref[:, lanes], preferred_element_type=F32)
            branch = scale_ref[:, lanes] * jax.nn.gelu(branch)
            out_ref[at, lanes] = (state_ref[at, lanes].astype(F32) + branch).astype(BF16)


def block_fields(dims, places, cells, halo, shares, weight, ln_gain, proj, scale, slot_parts):
    rows, cols, taps = dims
    total, width = cells.shape
    slots = sum(part.shape[0] for part in slot_parts)
    padded = rows + taps - 1
    freq, to_cols, fine, coef = wave(cols, taps)
    return pl.pallas_call(
        functools.partial(block_kernel, dims),
        out_shape=jax.ShapeDtypeStruct((total, width), BF16),
        in_specs=[SMEM] + [VMEM] * (14 + len(slot_parts)),
        out_specs=VMEM,
        scratch_shapes=[
            pltpu.VMEM((slots, width), BF16),
            pltpu.VMEM((total, width), BF16),
            pltpu.VMEM((padded, cols, width), F32),
            pltpu.VMEM((rows, 2 * cols, width), BF16),
            pltpu.VMEM(((2 if rows % 2 == 0 else 1) * cols, width), F32),
            pltpu.VMEM((taps, coef.shape[0], width), F32),
        ],
        compiler_params=pltpu.CompilerParams(vmem_limit_bytes=32 * MIB),
        cost_estimate=cost(6 * total * width * width, 8 * total * width, total * width),
        name="block_fields",
    )(places, cells, *halo, *shares, weight, freq, to_cols, fine, coef, ln_gain, proj, scale, *slot_parts)


def local(
    tokens, slot_keys, norm_gain, slot_gain, w_in, w_out, conv_weight, ln_gain, proj, layer_scale
):
    rows, cols, width = tokens.shape[1:]
    count_fc = lax.axis_size("fc")
    count_tok = lax.axis_size("tok")
    count_z = count_fc // 2
    slots = slot_keys.shape[1]
    slot_dev = slots // (count_fc * count_tok)
    slots_exp = slot_dev // w_in.shape[0]
    taps = conv_weight.shape[0]
    reach = taps // 2
    at_fc, at_tok = lax.axis_index("fc"), lax.axis_index("tok")
    other = [(i, i ^ 1) for i in range(count_fc)]
    cells = tokens.reshape(rows * cols, width)
    norm_gain, slot_gain = norm_gain.reshape(1, width), slot_gain.reshape(1, width)
    ln_gain, layer_scale = ln_gain.reshape(1, width), layer_scale.reshape(1, width)

    def shift(value, axis, step):
        count = lax.axis_size(axis)
        return lax.ppermute(value, axis, [(i, (i + step) % count) for i in range(count)])

    other = [(i, i ^ 1) for i in range(count_fc)]
    tie = lax.optimization_barrier
    even = at_tok % 2 == 0
    last = (rows - reach) * cols

    def swap(start):
        pairs = [(i, i + 1) for i in range(start, count_tok - 1, 2)]
        return pairs + [(j, i) for i, j in pairs]

    edge = lax.dynamic_slice_in_dim(cells, jnp.where(even, last, 0), reach * cols, axis=0)
    first_halo = lax.ppermute(edge, "tok", swap(0))
    in_other = lax.ppermute(w_in, "fc", other)
    out_other = lax.ppermute(w_out, "fc", other)

    index = jnp.stack([at_fc // 2, at_tok]).astype(jnp.int32)
    keys, *numer = dispatch(index, cells, slot_keys, norm_gain, (count_z, count_tok, slot_dev))
    numer[1], in_other, out_other = tie((numer[1], in_other, out_other))
    parts = [numer[0]] + [shift(numer[k], "tok", k) for k in range(1, count_tok)]

    slot_in = gather_slots(parts, slot_gain, count_z)
    arrived = [slot_in[0]] + [shift(slot_in[k], "fc", 2 * k) for k in range(1, count_z)]
    first = edge_rows(jnp.where(even, 0, last).reshape(1), cells, reach * cols, slot_in[0])
    second_halo = lax.ppermute(first, "tok", swap(1))
    always = jnp.ones((1,), jnp.int32)
    (share,) = combine_weights(always, [cells], keys, norm_gain, first)
    core = (at_fc % 2).astype(jnp.int32).reshape(1)
    made = experts(core, share, arrived, w_in, w_out, in_other, out_other, slots_exp)
    back = [made[0]] + [shift(made[k], "fc", -2 * k) for k in range(1, count_z)]
    mine = jnp.concatenate(back, axis=0)
    above, below = at_tok > 0, at_tok < count_tok - 1
    inside = jnp.stack([jnp.where(even, below, above), jnp.where(even, above, below)])
    halo = (first_halo, second_halo)
    halo_shares = combine_weights(inside.astype(jnp.int32), halo, keys, norm_gain, made[0])
    places = jnp.where(even, jnp.array([rows + reach, 0]), jnp.array([0, rows + reach]))
    every = [mine] + [shift(mine, "tok", -k) for k in range(1, count_tok)]

    fields = block_fields(
        (rows, cols, taps), places.astype(jnp.int32), cells, halo, (share, *halo_shares), conv_weight,
        ln_gain, proj, layer_scale, every,
    )
    return fields.reshape(1, rows, cols, width)


def solution(mesh):
    return jax.shard_map(
        local,
        mesh=mesh,
        in_specs=(
            P("fc", "tok", None, None),
            P(),
            P(),
            P(),
            P(("fc", "tok"), None, None),
            P(("fc", "tok"), None, None),
            P(),
            P(),
            P(),
            P(),
        ),
        out_specs=P("fc", "tok", None, None),
        check_vma=False,
    )
```

time: 110 us -> 78.9 us (0.72)
  the two profiles are of different devices: /device:TPU:0 before, /device:TPU:27 now
where the time goes in v2:
time: 78.9 us; the launch traced here: 78.6 us
  Pallas kernels  32 us (41%)
  waiting for transfers between devices  26.1 us (33%)
  starting transfers between devices  15.1 us (19%)
  local copies, waits for them, and re-layouts  5.02 us (6%)
    pallas_call x1, Pallas kernels, block_fields(): pl.pallas_call(functools.partial(block_kernel, dims), out_shape=jax.Shape...  19.2 us
    ppermute x12, waiting for transfers between devices, shift(): lax.ppermute(value, axis, [(i, (i + step) % count) for i in range(count)])  14.2 us
    ppermute x1, waiting for transfers between devices, local(): second_halo = lax.ppermute(first, 'tok', swap(1))  11.9 us
    ppermute x12, starting transfers between devices, shift(): lax.ppermute(value, axis, [(i, (i + step) % count) for i in range(count)])  10.9 us
    pallas_call x1, Pallas kernels, dispatch(): pl.pallas_call(functools.partial(dispatch_kernel, layout), out_shape=[jax...  4.55 us
    unnamed x37, local copies, waits for them, and re-layouts  4.09 us
    pallas_call x2, Pallas kernels, combine_weights(): pl.pallas_call(functools.partial(combine_kernel, len(cells)), out_shape=[...  3.97 us
    ppermute x1, starting transfers between devices, local(): second_halo = lax.ppermute(first, 'tok', swap(1))  3.5 us
  transfers between devices with their start and end apart: 16, of which 10 were waited for; matrix products, arithmetic and copies ran while one was open for 1% of the time, Pallas kernels for 16%

profile of v2, /device:TPU:27, one launch (start us, length us, event | category | flops | bytes accessed | tf_op | source)
XLA Modules:
  0.0 78.6 jit_solution(8768017465827949485)
XLA Ops:
  0.8 1.6 %copy-done = bf16[1,8,128,1024]{3,2,1,0:T(8,128)(2,1)S(1)} copy-done((bf16[1,8,128,1024]{3,2,1,0:T(8,128)(2,1)S(1)}, bf16[1,8,128,1024]{3,2,1,0:T(8,128)(2,1)}, u32[]{:S(2)}) %copy-start) | copy-done | bytes 2097176
  3.0 1.0 %copy-done.8 = bf16[1024,256]{1,0:T(8,128)(2,1)S(1)} copy-done((bf16[1024,256]{1,0:T(8,128)(2,1)S(1)}, bf16[1024,256]{1,0:T(8,128)(2,1)}, u32[]{:S(2)}) %copy-start.8) | copy-done | bytes 524312
  4.1 4.5 %dispatch.1 = (bf16[256,1024]{1,0:T(8,128)(2,1)S(1)}, bf16[64,1152]{1,0:T(8,128)(2,1)S(1)}, bf16[64,1152]{1,0:T(8,128)(2,1)}, bf16[64,1152]{1,0:T(8,128)(2,1)}, bf16[64,1152]{1,0:T(8,128)(2,1)}) custom-call(s32[2]{0:T(128)S(1)} %pad_add_fusion.index_ref, bf16[1024,1024]{1,0:T(8,128)(2,1)S(1)} %bitcast.12, bf16[1024,256]{1,0:T(8,128)(2,1)S(1)} %copy-done.8, ...), custom_call_target="tpu_custom_call" | custom-call | flops 1073741824 | bytes 4194304 | tf_op jit(solution)/shard_map/dispatch/pallas_call | solution.py:105
  8.6 1.3 %collective-permute-start.4 = (bf16[64,1152]{1,0:T(8,128)(2,1)}, bf16[64,1152]{1,0:T(8,128)(2,1)}, u32[]{:S(2)}, u32[]{:S(2)}) collective-permute-start(bf16[64,1152]{1,0:T(8,128)(2,1)} %get-tuple-element.26), channel_id=1, source_target_pairs={{0,2},{1,3},{2,0},{3,1},{4,6},{5,7},{6,4},{7,5},{8,10},{9,11},{10,... | collective-permute-start | bytes 442376 | tf_op jit(solution)/shard_map/ppermute | solution.py:459
  10.2 2.1 %collective-permute-start.3 = (bf16[64,1152]{1,0:T(8,128)(2,1)}, bf16[64,1152]{1,0:T(8,128)(2,1)}, u32[]{:S(2)}, u32[]{:S(2)}) collective-permute-start(bf16[64,1152]{1,0:T(8,128)(2,1)} %get-tuple-element.25), channel_id=1, source_target_pairs={{0,1},{1,2},{2,3},{3,0},{4,5},{5,6},{6,7},{7,4},{8,9},{9,10},{10,1... | collective-permute-start | bytes 442376 | tf_op jit(solution)/shard_map/ppermute | solution.py:459
  12.3 0.9 %constant_dynamic-slice_fusion = bf16[384,1024]{1,0:T(8,128)(2,1)} fusion(bf16[1024,1024]{1,0:T(8,128)(2,1)S(1)} %bitcast.13, s32[]{:T(128)S(6)} %select_n.41), kind=kLoop, calls=%fused_computation.7 | loop fusion | bytes 1572868 | tf_op jit(solution)/shard_map/dynamic_slice | solution.py:470
  13.2 2.2 %collective-permute-done.4.refs_2_ = bf16[64,1152]{1,0:T(8,128)(2,1)} collective-permute-done((bf16[64,1152]{1,0:T(8,128)(2,1)}, bf16[64,1152]{1,0:T(8,128)(2,1)}, u32[]{:S(2)}, u32[]{:S(2)}) %collective-permute-start.4) | collective-permute-done | bytes 147488 | tf_op jit(solution)/shard_map/ppermute | solution.py:459
  15.8 2.2 %collective-permute-done.3.refs_1_ = bf16[64,1152]{1,0:T(8,128)(2,1)} collective-permute-done((bf16[64,1152]{1,0:T(8,128)(2,1)}, bf16[64,1152]{1,0:T(8,128)(2,1)}, u32[]{:S(2)}, u32[]{:S(2)}) %collective-permute-start.3) | collective-permute-done | bytes 147488 | tf_op jit(solution)/shard_map/ppermute | solution.py:459
  18.0 0.7 copy-done.6
  18.7 1.4 %gather_slots.1 = (bf16[16,1024]{1,0:T(8,128)(2,1)S(1)}, bf16[16,1024]{1,0:T(8,128)(2,1)S(1)}, bf16[16,1024]{1,0:T(8,128)(2,1)S(1)}, bf16[16,1024]{1,0:T(8,128)(2,1)S(1)}) custom-call(f32[1,1024]{1,0:T(1,128)S(1)} %bitcast.20, bf16[64,1152]{1,0:T(8,128)(2,1)S(1)} %get-tuple-element.23.refs_0_, bf16[64,1152]{1,0:T(8,128)(2,1)} %collective-permute-done.3.refs_1_, ...), custom_call_target="tpu_custom_call" | custom-call | flops 2097152 | bytes 262144 | tf_op jit(solution)/shard_map/gather_slots/pallas_call | solution.py:145
  20.2 3.5 %collective-permute-start.6 = (bf16[384,1024]{1,0:T(8,128)(2,1)S(1)}, bf16[384,1024]{1,0:T(8,128)(2,1)S(1)}, u32[]{:S(2)}, u32[]{:S(2)}) collective-permute-start(bf16[384,1024]{1,0:T(8,128)(2,1)S(1)} %edge_rows.1._), channel_id=1, source_target_pairs={{1,2},{2,1},{5,6},{6,5},{9,10},{10,9},{13,14},{14,13},{17,18},{18,... | collective-permute-start | bytes 2359304 | tf_op jit(solution)/shard_map/ppermute | solution.py:483
  23.8 1.3 %collective-permute-start.8 = (bf16[16,1024]{1,0:T(8,128)(2,1)S(1)}, bf16[16,1024]{1,0:T(8,128)(2,1)S(1)}, u32[]{:S(2)}, u32[]{:S(2)}) collective-permute-start(bf16[16,1024]{1,0:T(8,128)(2,1)S(1)} %get-tuple-element.33), channel_id=1, source_target_pairs={{0,16},{4,20},{8,24},{12,28},{16,0},{20,4},{24,8},{28,12},{1,17},{... | collective-permute-start | bytes 98312 | tf_op jit(solution)/shard_map/ppermute | solution.py:459
  25.3 1.9 %combine_weights.2._.share_ref = bf16[1024,256]{1,0:T(8,128)(2,1)S(1)} custom-call(s32[1]{0:T(128)} %constant.57.clone.1.valid_ref, bf16[256,1024]{1,0:T(8,128)(2,1)S(1)} %get-tuple-element.29.keys_ref, f32[1,1024]{1,0:T(1,128)S(1)} %bitcast.18, bf16[384,1024]{1,0:T(8,128)(2,1)S(1)} %edge_rows.1._, bf16[1024,1024]{1,0:T(8,128)(2,1)S(1)} %bitcast.15), custom_call_target="tpu_custom_call" | custom-call | flops 536870912 | bytes 2097152 | tf_op jit(solution)/shard_map/combine_weights/pallas_call | solution.py:250
  27.5 2.5 %collective-permute-done.9.refs_3_ = bf16[16,1024]{1,0:T(8,128)(2,1)S(1)} collective-permute-done((bf16[16,1024]{1,0:T(8,128)(2,1)S(1)}, bf16[16,1024]{1,0:T(8,128)(2,1)S(1)}, u32[]{:S(2)}, u32[]{:S(2)}) %collective-permute-start.9) | collective-permute-done | bytes 32800 | tf_op jit(solution)/shard_map/ppermute | solution.py:459
  30.1 2.8 %experts.1 = (bf16[16,1024]{1,0:T(8,128)(2,1)S(1)}, bf16[16,1024]{1,0:T(8,128)(2,1)S(1)}, bf16[16,1024]{1,0:T(8,128)(2,1)S(1)}, bf16[16,1024]{1,0:T(8,128)(2,1)S(1)}) custom-call(s32[1]{0:T(128)} %bitcast.8.core_ref, bf16[1024,256]{1,0:T(8,128)(2,1)S(1)} %combine_weights.2._.share_ref, bf16[2,1024,512]{2,1,0:T(8,128)(2,1)S(1)} %copy-done.2, ...), custom_call_target="tpu_custom_call" | custom-call | flops 536870912 | bytes 8388608 | tf_op jit(solution)/shard_map/experts/pallas_call | solution.py:200
  33.7 2.6 %collective-permute-start.12 = (bf16[16,1024]{1,0:T(8,128)(2,1)S(1)}, bf16[16,1024]{1,0:T(8,128)(2,1)S(1)}, u32[]{:S(2)}, u32[]{:S(2)}) collective-permute-start(bf16[16,1024]{1,0:T(8,128)(2,1)S(1)} %get-tuple-element.40), channel_id=1, source_target_pairs={{0,8},{4,12},{8,16},{12,20},{16,24},{20,28},{24,0},{28,4},{1,9},{5... | collective-permute-start | bytes 98312 | tf_op jit(solution)/shard_map/ppermute | solution.py:459
  36.3 1.3 %collective-permute-done.10 = bf16[16,1024]{1,0:T(8,128)(2,1)S(1)} collective-permute-done((bf16[16,1024]{1,0:T(8,128)(2,1)S(1)}, bf16[16,1024]{1,0:T(8,128)(2,1)S(1)}, u32[]{:S(2)}, u32[]{:S(2)}) %collective-permute-start.10) | collective-permute-done | bytes 32800 | tf_op jit(solution)/shard_map/ppermute | solution.py:459
  38.3 1.1 %collective-permute-start.14 = (bf16[64,1024]{1,0:T(8,128)(2,1)S(1)}, bf16[64,1024]{1,0:T(8,128)(2,1)S(1)}, u32[]{:S(2)}, u32[]{:S(2)}) collective-permute-start(bf16[64,1024]{1,0:T(8,128)(2,1)S(1)} %constant_dynamic-update-slice_fusion.rest_0_), channel_id=1, source_target_pairs={{0,2},{1,3},{2,0},{3,1},{4,6},{5,7},{6,4},{7,5},{8,10},{9,11},{10,... | collective-permute-start | bytes 393224 | tf_op jit(solution)/shard_map/ppermute | solution.py:459
  39.4 1.3 %collective-permute-start.15 = (bf16[64,1024]{1,0:T(8,128)(2,1)S(1)}, bf16[64,1024]{1,0:T(8,128)(2,1)S(1)}, u32[]{:S(2)}, u32[]{:S(2)}) collective-permute-start(bf16[64,1024]{1,0:T(8,128)(2,1)S(1)} %constant_dynamic-update-slice_fusion.rest_0_), channel_id=1, source_target_pairs={{0,1},{1,2},{2,3},{3,0},{4,5},{5,6},{6,7},{7,4},{8,9},{9,10},{10,1... | collective-permute-start | bytes 393224 | tf_op jit(solution)/shard_map/ppermute | solution.py:459
  40.7 11.9 %collective-permute-done.6.refs_1_.high_ref = bf16[384,1024]{1,0:T(8,128)(2,1)S(1)} collective-permute-done((bf16[384,1024]{1,0:T(8,128)(2,1)S(1)}, bf16[384,1024]{1,0:T(8,128)(2,1)S(1)}, u32[]{:S(2)}, u32[]{:S(2)}) %collective-permute-start.6) | collective-permute-done | bytes 786464 | tf_op jit(solution)/shard_map/ppermute | solution.py:483
  52.6 2.0 %combine_weights.3 = (bf16[384,256]{1,0:T(8,128)(2,1)S(1)}, bf16[384,256]{1,0:T(8,128)(2,1)S(1)}) custom-call(s32[2]{0:T(128)S(1)} %add_convert_fusion.valid_ref, bf16[256,1024]{1,0:T(8,128)(2,1)S(1)} %get-tuple-element.29.keys_ref, f32[1,1024]{1,0:T(1,128)S(1)} %bitcast.19, bf16[16,1024]{1,0:T(8,128)(2,1)S(1)} %get-tuple-element.35._, ...), custom_call_target="tpu_custom_call" | custom-call | flops 402653184 | bytes 1572864 | tf_op jit(solution)/shard_map/combine_weights/pallas_call | solution.py:250
  54.7 0.8 collective-permute-done.13.rest_1_
  55.4 3.9 %collective-permute-done.14.rest_2_ = bf16[64,1024]{1,0:T(8,128)(2,1)S(1)} collective-permute-done((bf16[64,1024]{1,0:T(8,128)(2,1)S(1)}, bf16[64,1024]{1,0:T(8,128)(2,1)S(1)}, u32[]{:S(2)}, u32[]{:S(2)}) %collective-permute-start.14) | collective-permute-done | bytes 131104 | tf_op jit(solution)/shard_map/ppermute | solution.py:459
  59.4 19.2 %block_fields.1 = bf16[1024,1024]{1,0:T(8,128)(2,1)} custom-call(s32[2]{0:T(128)S(1)} %broadcast_select_fusion.place_ref, bf16[1024,1024]{1,0:T(8,128)(2,1)S(1)} %bitcast.16, bf16[384,1024]{1,0:T(8,128)(2,1)S(1)} %collective-permute-done.refs_0_.low_ref, bf16[384,1024]{1,0:T(8,128)(2,1)S(1)} %collective-permute-done.6.refs_1_.high_ref, ...), custom_call_target="tpu_custom_call" | custom-call | flops 6442450944 | bytes 8388608 | tf_op jit(solution)/shard_map/block_fields/pallas_call | solution.py:420
  (57 shorter events, 4.1 us)
Async XLA Ops:
  0.0 10.2 %collective-permute-start.1 = (bf16[2,1024,512]{2,1,0:T(8,128)(2,1)}, bf16[2,1024,512]{2,1,0:T(8,128)(2,1)}, u32[]{:S(2)}, u32[]{:S(2)}) collective-permute-start(bf16[2,1024,512]{2,1,0:T(8,128)(2,1)} %in_own.1), channel_id=1, source_target_pairs={{0,4},{4,0},{8,12},{12,8},{16,20},{20,16},{24,28},{28,24},{1,5},{5... | collective-permute-start | bytes 6291464 | tf_op jit(solution)/shard_map/ppermute | solution.py:472
  0.7 9.5 %collective-permute-start.2 = (bf16[2,512,1024]{2,1,0:T(8,128)(2,1)}, bf16[2,512,1024]{2,1,0:T(8,128)(2,1)}, u32[]{:S(2)}, u32[]{:S(2)}) collective-permute-start(bf16[2,512,1024]{2,1,0:T(8,128)(2,1)} %out_own.1), channel_id=1, source_target_pairs={{0,4},{4,0},{8,12},{12,8},{16,20},{20,16},{24,28},{28,24},{1,5},{5... | collective-permute-start | bytes 6291464 | tf_op jit(solution)/shard_map/ppermute | solution.py:473
  8.6 6.8 %collective-permute-start.4 = (bf16[64,1152]{1,0:T(8,128)(2,1)}, bf16[64,1152]{1,0:T(8,128)(2,1)}, u32[]{:S(2)}, u32[]{:S(2)}) collective-permute-start(bf16[64,1152]{1,0:T(8,128)(2,1)} %get-tuple-element.26), channel_id=1, source_target_pairs={{0,2},{1,3},{2,0},{3,1},{4,6},{5,7},{6,4},{7,5},{8,10},{9,11},{10,... | collective-permute-start | bytes 442376 | tf_op jit(solution)/shard_map/ppermute | solution.py:459
  9.9 5.9 %collective-permute-start.5 = (bf16[64,1152]{1,0:T(8,128)(2,1)}, bf16[64,1152]{1,0:T(8,128)(2,1)}, u32[]{:S(2)}, u32[]{:S(2)}) collective-permute-start(bf16[64,1152]{1,0:T(8,128)(2,1)} %get-tuple-element.27), channel_id=1, source_target_pairs={{0,3},{1,0},{2,1},{3,2},{4,7},{5,4},{6,5},{7,6},{8,11},{9,8},{10,9... | collective-permute-start | bytes 442376 | tf_op jit(solution)/shard_map/ppermute | solution.py:459
  10.2 7.9 %collective-permute-start.3 = (bf16[64,1152]{1,0:T(8,128)(2,1)}, bf16[64,1152]{1,0:T(8,128)(2,1)}, u32[]{:S(2)}, u32[]{:S(2)}) collective-permute-start(bf16[64,1152]{1,0:T(8,128)(2,1)} %get-tuple-element.25), channel_id=1, source_target_pairs={{0,1},{1,2},{2,3},{3,0},{4,5},{5,6},{6,7},{7,4},{8,9},{9,10},{10,1... | collective-permute-start | bytes 442376 | tf_op jit(solution)/shard_map/ppermute | solution.py:459
  13.2 27.5 %collective-permute-start = (bf16[384,1024]{1,0:T(8,128)(2,1)}, bf16[384,1024]{1,0:T(8,128)(2,1)S(1)}, u32[]{:S(2)}, u32[]{:S(2)}) collective-permute-start(bf16[384,1024]{1,0:T(8,128)(2,1)} %constant_dynamic-slice_fusion), channel_id=1, source_target_pairs={{0,1},{2,3},{1,0},{3,2},{4,5},{6,7},{5,4},{7,6},{8,9},{10,11},{9,8... | collective-permute-start | bytes 2359304 | tf_op jit(solution)/shard_map/ppermute | solution.py:471
  20.2 32.4 %collective-permute-start.6 = (bf16[384,1024]{1,0:T(8,128)(2,1)S(1)}, bf16[384,1024]{1,0:T(8,128)(2,1)S(1)}, u32[]{:S(2)}, u32[]{:S(2)}) collective-permute-start(bf16[384,1024]{1,0:T(8,128)(2,1)S(1)} %edge_rows.1._), channel_id=1, source_target_pairs={{1,2},{2,1},{5,6},{6,5},{9,10},{10,9},{13,14},{14,13},{17,18},{18,... | collective-permute-start | bytes 2359304 | tf_op jit(solution)/shard_map/ppermute | solution.py:483
  23.7 3.5 %collective-permute-start.7 = (bf16[16,1024]{1,0:T(8,128)(2,1)S(1)}, bf16[16,1024]{1,0:T(8,128)(2,1)S(1)}, u32[]{:S(2)}, u32[]{:S(2)}) collective-permute-start(bf16[16,1024]{1,0:T(8,128)(2,1)S(1)} %get-tuple-element.32), channel_id=1, source_target_pairs={{0,8},{4,12},{8,16},{12,20},{16,24},{20,28},{24,0},{28,4},{1,9},{5... | collective-permute-start | bytes 98312 | tf_op jit(solution)/shard_map/ppermute | solution.py:459
  23.8 3.7 %collective-permute-start.8 = (bf16[16,1024]{1,0:T(8,128)(2,1)S(1)}, bf16[16,1024]{1,0:T(8,128)(2,1)S(1)}, u32[]{:S(2)}, u32[]{:S(2)}) collective-permute-start(bf16[16,1024]{1,0:T(8,128)(2,1)S(1)} %get-tuple-element.33), channel_id=1, source_target_pairs={{0,16},{4,20},{8,24},{12,28},{16,0},{20,4},{24,8},{28,12},{1,17},{... | collective-permute-start | bytes 98312 | tf_op jit(solution)/shard_map/ppermute | solution.py:459
  25.1 4.9 %collective-permute-start.9 = (bf16[16,1024]{1,0:T(8,128)(2,1)S(1)}, bf16[16,1024]{1,0:T(8,128)(2,1)S(1)}, u32[]{:S(2)}, u32[]{:S(2)}) collective-permute-start(bf16[16,1024]{1,0:T(8,128)(2,1)S(1)} %get-tuple-element.34), channel_id=1, source_target_pairs={{0,24},{4,28},{8,0},{12,4},{16,8},{20,12},{24,16},{28,20},{1,25},{... | collective-permute-start | bytes 98312 | tf_op jit(solution)/shard_map/ppermute | solution.py:459
  30.1 29.3 %copy-start.13 = (bf16[128,256]{1,0:T(8,128)(2,1)S(1)}, bf16[128,256]{1,0:T(8,128)(2,1)}, u32[]{:S(2)}) copy-start(bf16[128,256]{1,0:T(8,128)(2,1)} %constant.62.clone.cols_ref) | copy-start | bytes 196612
  30.1 29.3 %copy-start.14 = (bf16[192,40]{1,0:T(8,128)(2,1)S(1)}, bf16[192,40]{1,0:T(8,128)(2,1)}, u32[]{:S(2)}) copy-start(bf16[192,40]{1,0:T(8,128)(2,1)} %constant.64.clone.coef_ref) | copy-start | bytes 46084
  30.1 29.3 %copy-start.15 = (bf16[128,128]{1,0:T(8,128)(2,1)S(1)}, bf16[128,128]{1,0:T(8,128)(2,1)}, u32[]{:S(2)}) copy-start(bf16[128,128]{1,0:T(8,128)(2,1)} %constant.63.clone.fine_ref) | copy-start | bytes 98308
  32.9 26.4 %copy-start.7 = (bf16[1024,1024]{1,0:T(8,128)(2,1)S(1)}, bf16[1024,1024]{1,0:T(8,128)(2,1)}, u32[]{:S(2)}) copy-start(bf16[1024,1024]{1,0:T(8,128)(2,1)} %proj_ref.1) | copy-start | bytes 6291460
  33.0 26.4 %copy-start.9 = (f32[7,7,1024]{2,1,0:T(8,128)S(1)}, f32[7,7,1024]{2,1,0:T(8,128)}, u32[]{:S(2)}) copy-start(f32[7,7,1024]{2,1,0:T(8,128)} %weight_ref.1) | copy-start | bytes 602116
  33.0 26.4 %copy-start.10 = (f32[1024]{0:T(1024)S(1)}, f32[1024]{0:T(1024)}, u32[]{:S(2)}) copy-start(f32[1024]{0:T(1024)} %param.23) | copy-start | bytes 12292
  33.0 26.4 %copy-start.11 = (f32[1024]{0:T(1024)S(1)}, f32[1024]{0:T(1024)}, u32[]{:S(2)}) copy-start(f32[1024]{0:T(1024)} %param.25) | copy-start | bytes 12292
  33.0 26.4 %copy-start.12 = (bf16[128,256]{1,0:T(8,128)(2,1)S(1)}, bf16[128,256]{1,0:T(8,128)(2,1)}, u32[]{:S(2)}) copy-start(bf16[128,256]{1,0:T(8,128)(2,1)} %constant.61.clone.freq_ref) | copy-start | bytes 196612
  33.0 4.6 %collective-permute-start.10 = (bf16[16,1024]{1,0:T(8,128)(2,1)S(1)}, bf16[16,1024]{1,0:T(8,128)(2,1)S(1)}, u32[]{:S(2)}, u32[]{:S(2)}) collective-permute-start(bf16[16,1024]{1,0:T(8,128)(2,1)S(1)} %get-tuple-element.38), channel_id=1, source_target_pairs={{0,24},{4,28},{8,0},{12,4},{16,8},{20,12},{24,16},{28,20},{1,25},{... | collective-permute-start | bytes 98312 | tf_op jit(solution)/shard_map/ppermute | solution.py:459
  33.1 4.5 %collective-permute-start.11 = (bf16[16,1024]{1,0:T(8,128)(2,1)S(1)}, bf16[16,1024]{1,0:T(8,128)(2,1)S(1)}, u32[]{:S(2)}, u32[]{:S(2)}) collective-permute-start(bf16[16,1024]{1,0:T(8,128)(2,1)S(1)} %get-tuple-element.39), channel_id=1, source_target_pairs={{0,16},{4,20},{8,24},{12,28},{16,0},{20,4},{24,8},{28,12},{1,17},{... | collective-permute-start | bytes 98312 | tf_op jit(solution)/shard_map/ppermute | solution.py:459
  33.7 4.6 %collective-permute-start.12 = (bf16[16,1024]{1,0:T(8,128)(2,1)S(1)}, bf16[16,1024]{1,0:T(8,128)(2,1)S(1)}, u32[]{:S(2)}, u32[]{:S(2)}) collective-permute-start(bf16[16,1024]{1,0:T(8,128)(2,1)S(1)} %get-tuple-element.40), channel_id=1, source_target_pairs={{0,8},{4,12},{8,16},{12,20},{16,24},{20,28},{24,0},{28,4},{1,9},{5... | collective-permute-start | bytes 98312 | tf_op jit(solution)/shard_map/ppermute | solution.py:459
  38.3 17.2 %collective-permute-start.13 = (bf16[64,1024]{1,0:T(8,128)(2,1)S(1)}, bf16[64,1024]{1,0:T(8,128)(2,1)S(1)}, u32[]{:S(2)}, u32[]{:S(2)}) collective-permute-start(bf16[64,1024]{1,0:T(8,128)(2,1)S(1)} %constant_dynamic-update-slice_fusion.rest_0_), channel_id=1, source_target_pairs={{0,3},{1,0},{2,1},{3,2},{4,7},{5,4},{6,5},{7,6},{8,11},{9,8},{10,9... | collective-permute-start | bytes 393224 | tf_op jit(solution)/shard_map/ppermute | solution.py:459
  38.3 21.1 %collective-permute-start.14 = (bf16[64,1024]{1,0:T(8,128)(2,1)S(1)}, bf16[64,1024]{1,0:T(8,128)(2,1)S(1)}, u32[]{:S(2)}, u32[]{:S(2)}) collective-permute-start(bf16[64,1024]{1,0:T(8,128)(2,1)S(1)} %constant_dynamic-update-slice_fusion.rest_0_), channel_id=1, source_target_pairs={{0,2},{1,3},{2,0},{3,1},{4,6},{5,7},{6,4},{7,5},{8,10},{9,11},{10,... | collective-permute-start | bytes 393224 | tf_op jit(solution)/shard_map/ppermute | solution.py:459
  39.4 20.0 %collective-permute-start.15 = (bf16[64,1024]{1,0:T(8,128)(2,1)S(1)}, bf16[64,1024]{1,0:T(8,128)(2,1)S(1)}, u32[]{:S(2)}, u32[]{:S(2)}) collective-permute-start(bf16[64,1024]{1,0:T(8,128)(2,1)S(1)} %constant_dynamic-update-slice_fusion.rest_0_), channel_id=1, source_target_pairs={{0,1},{1,2},{2,3},{3,0},{4,5},{5,6},{6,7},{7,4},{8,9},{9,10},{10,1... | collective-permute-start | bytes 393224 | tf_op jit(solution)/shard_map/ppermute | solution.py:459
  (9 other events, 49.1 us)

commit v3 on v2

--- a/solution.py
+++ b/solution.py
@@ -14,7 +14,7 @@
 LANES = 128
 EPS = 1e-06
 MIB = 1024 * 1024
-LIMIT_D = 16
+LIMIT_D = 56
 LIMIT_E = 16
 NT = (((1,), (1,)), ((), ()))
 VMEM = pl.BlockSpec(memory_space=pltpu.VMEM)
@@ -234,6 +234,9 @@
 
 def combine_kernel(count, valid_ref, keys_ref, gain_ref, _, *refs):
     block = 128
+    if len(refs) > 2 * count:
+        fill_spectrum(refs[count], refs[count + 1], refs[-1])
+        refs = refs[:count] + refs[count + 2 : -1]
     for at, (cells_ref, out_ref) in enumerate(zip(refs[:count], refs[count:])):
         for start in range(0, cells_ref.shape[0], block):
             rows = slice(start, start + block)
@@ -244,18 +247,24 @@
             out_ref[rows, :] = jnp.where(valid_ref[at] > 0, share, 0.0).astype(BF16)
 
 
-def combine_weights(valid, cells, keys, gain, after):
+def combine_weights(valid, cells, keys, gain, after, filters=()):
+    made = [(filters[1].shape[0], filters[0].shape[0], filters[1].shape[2])] if filters else []
     width, slots = gain.shape[1], keys.shape[0]
     total = sum(part.shape[0] for part in cells)
     return pl.pallas_call(
         functools.partial(combine_kernel, len(cells)),
-        out_shape=[jax.ShapeDtypeStruct((part.shape[0], slots), BF16) for part in cells],
-        in_specs=[SMEM, VMEM, VMEM, ANY] + [VMEM] * len(cells),
-        out_specs=[VMEM] * len(cells),
+        out_shape=[jax.ShapeDtypeStruct((part.shape[0], slots), BF16) for part in cells]
+        + [jax.ShapeDtypeStruct(shape, F32) for shape in made],
+        in_specs=[SMEM, VMEM, VMEM, ANY] + [VMEM] * (len(cells) + len(filters)),
+        out_specs=[VMEM] * (len(cells) + len(made)),
         compiler_params=pltpu.CompilerParams(vmem_limit_bytes=16 * MIB),
         cost_estimate=cost(2 * total * width * slots, 2 * total * width, total * slots),
         name="combine_weights",
-    )(valid, keys, gain, after, *cells)
+    )(valid, keys, gain, after, *cells, *filters)
+
+
+def batch(rows):
+    return next(count for count in (8, 4, 2, 1) if rows % count == 0)
 
 
 def pieces(value, count):
@@ -313,12 +322,12 @@
 
 
 def block_kernel(
-    dims, place_ref, cells_ref, low_ref, high_ref, share_ref, share_low, share_high, weight_ref, freq_ref,
-    cols_ref, fine_ref, coef_ref, ln_ref, proj_ref, scale_ref, *rest
+    dims, place_ref, cells_ref, low_ref, high_ref, share_ref, share_low, share_high, spectrum_ref, freq_ref,
+    cols_ref, fine_ref, ln_ref, proj_ref, scale_ref, *rest
 ):
     rows, cols, taps = dims
-    slot_refs, out_ref = rest[:-7], rest[-7]
-    slots_ref, state_ref, freqs_ref, back_ref, conv_ref, spectrum_ref = rest[-6:]
+    slot_refs, out_ref = rest[:-6], rest[-6]
+    slots_ref, state_ref, freqs_ref, back_ref, conv_ref = rest[-5:]
     reach = taps // 2
     half = cols // 2
     width = cells_ref.shape[1]
@@ -326,8 +335,6 @@
     for ref in slot_refs:
         slots_ref[start : start + ref.shape[0], :] = ref[...]
         start += ref.shape[0]
-    fill_spectrum(coef_ref, weight_ref, spectrum_ref)
-
     chunk = 2 * LANES
 
     def mix(cells, share, row, to, keep):
@@ -342,14 +349,17 @@
             twice = jnp.concatenate([state, state], axis=0)
             freqs_ref[to, :, lanes] = jnp.dot(freq_ref[...], twice, preferred_element_type=F32)
 
-    @pl.loop(0, reach)
-    def _(row):
+    for row in range(reach):
         mix(low_ref, share_low, row, row + place_ref[0], False)
         mix(high_ref, share_high, row, row + place_ref[1], False)
 
-    @pl.loop(0, rows)
-    def _(row):
-        mix(cells_ref, share_ref, row, row + reach, True)
+    at_once = batch(rows)
+
+    @pl.loop(0, rows // at_once)
+    def _(step):
+        for extra in range(at_once):
+            row = step * at_once + extra
+            mix(cells_ref, share_ref, row, row + reach, True)
 
     tile = 16
 
@@ -387,7 +397,7 @@
                         back_ref[first + to, pl.ds(base + which * half, tile), lanes] = high
                         back_ref[first + to, pl.ds(base + cols + which * half, tile), lanes] = low
 
-    pair = 2 if rows % 2 == 0 else 1
+    pair = batch(rows)
 
     @pl.loop(0, rows // pair)
     def _(step):
@@ -411,29 +421,27 @@
             out_ref[at, lanes] = (state_ref[at, lanes].astype(F32) + branch).astype(BF16)
 
 
-def block_fields(dims, places, cells, halo, shares, weight, ln_gain, proj, scale, slot_parts):
+def block_fields(dims, places, cells, halo, shares, weight, ln_gain, proj, scale, slot_parts, waves):
     rows, cols, taps = dims
     total, width = cells.shape
     slots = sum(part.shape[0] for part in slot_parts)
     padded = rows + taps - 1
-    freq, to_cols, fine, coef = wave(cols, taps)
     return pl.pallas_call(
         functools.partial(block_kernel, dims),
         out_shape=jax.ShapeDtypeStruct((total, width), BF16),
-        in_specs=[SMEM] + [VMEM] * (14 + len(slot_parts)),
+        in_specs=[SMEM] + [VMEM] * (13 + len(slot_parts)),
         out_specs=VMEM,
         scratch_shapes=[
             pltpu.VMEM((slots, width), BF16),
             pltpu.VMEM((total, width), BF16),
             pltpu.VMEM((padded, cols, width), F32),
             pltpu.VMEM((rows, 2 * cols, width), BF16),
-            pltpu.VMEM(((2 if rows % 2 == 0 else 1) * cols, width), F32),
-            pltpu.VMEM((taps, coef.shape[0], width), F32),
+            pltpu.VMEM((batch(rows) * cols, width), F32),
         ],
         compiler_params=pltpu.CompilerParams(vmem_limit_bytes=32 * MIB),
         cost_estimate=cost(6 * total * width * width, 8 * total * width, total * width),
         name="block_fields",
-    )(places, cells, *halo, *shares, weight, freq, to_cols, fine, coef, ln_gain, proj, scale, *slot_parts)
+    )(places, cells, *halo, *shares, weight, *waves, ln_gain, proj, scale, *slot_parts)
 
 
 def local(
@@ -490,13 +498,16 @@
     above, below = at_tok > 0, at_tok < count_tok - 1
     inside = jnp.stack([jnp.where(even, below, above), jnp.where(even, above, below)])
     halo = (first_halo, second_halo)
-    halo_shares = combine_weights(inside.astype(jnp.int32), halo, keys, norm_gain, made[0])
+    freq, to_cols, fine, coef = wave(cols, taps)
+    *halo_shares, filters = combine_weights(
+        inside.astype(jnp.int32), halo, keys, norm_gain, made[0], (coef, conv_weight)
+    )
     places = jnp.where(even, jnp.array([rows + reach, 0]), jnp.array([0, rows + reach]))
     every = [mine] + [shift(mine, "tok", -k) for k in range(1, count_tok)]
 
     fields = block_fields(
-        (rows, cols, taps), places.astype(jnp.int32), cells, halo, (share, *halo_shares), conv_weight,
-        ln_gain, proj, layer_scale, every,
+        (rows, cols, taps), places.astype(jnp.int32), cells, halo, (share, *halo_shares), filters,
+        ln_gain, proj, layer_scale, every, (freq, to_cols, fine),
     )
     return fields.reshape(1, rows, cols, width)
 

time: 78.9 us -> 72.2 us (0.915)
  the two profiles are of different devices: /device:TPU:27 before, /device:TPU:0 now
where the time goes in v3:
time: 72.2 us; the launch traced here: 72 us
  Pallas kernels  28.2 us (39%)
  starting transfers between devices  26 us (36%)
  waiting for transfers between devices  14.2 us (20%)
  local copies, waits for them, and re-layouts  2.61 us (4%)
  other arithmetic  0.74 us (1%)
    ppermute x12, starting transfers between devices, shift(): lax.ppermute(value, axis, [(i, (i + step) % count) for i in range(count)])  22.2 us
    ppermute x12, waiting for transfers between devices, shift(): lax.ppermute(value, axis, [(i, (i + step) % count) for i in range(count)])  14.2 us
    pallas_call x1, Pallas kernels, block_fields(): pl.pallas_call(functools.partial(block_kernel, dims), out_shape=jax.Shape...  13.4 us
    pallas_call x1, Pallas kernels, dispatch(): pl.pallas_call(functools.partial(dispatch_kernel, layout), out_shape=[jax...  6.02 us
    pallas_call x2, Pallas kernels, combine_weights(): pl.pallas_call(functools.partial(combine_kernel, len(cells)), out_shape=[...  4.6 us
    pallas_call x1, Pallas kernels, experts(): pl.pallas_call(functools.partial(expert_kernel, count_z, slots_exp), out_...  2.84 us
    ppermute x1, starting transfers between devices, local(): first_halo = lax.ppermute(edge, 'tok', swap(0))  2.4 us
    unnamed x35, local copies, waits for them, and re-layouts  1.68 us
  transfers between devices with their start and end apart: 16, of which 8 were waited for; matrix products, arithmetic and copies ran while one was open for 2% of the time, Pallas kernels for 21%

profile of v3, /device:TPU:0, one launch (start us, length us, event | category | flops | bytes accessed | tf_op | source)
XLA Modules:
  0.0 72.0 jit_solution(18372830260872358449)
XLA Ops:
  1.2 6.0 %dispatch.1 = (bf16[256,1024]{1,0:T(8,128)(2,1)}, bf16[64,1152]{1,0:T(8,128)(2,1)}, bf16[64,1152]{1,0:T(8,128)(2,1)}, bf16[64,1152]{1,0:T(8,128)(2,1)}, bf16[64,1152]{1,0:T(8,128)(2,1)}) custom-call(s32[2]{0:T(128)} %pad_add_fusion.index_ref, bf16[1024,1024]{1,0:T(8,128)(2,1)} %bitcast.12, bf16[1024,256]{1,0:T(8,128)(2,1)} %keys_hbm.1, f32[1,1024]{1,0:T(1,128)} %bitcast.17), custom_call_target="tpu_custom_call" | custom-call | flops 1073741824 | bytes 4194304 | tf_op jit(solution)/shard_map/dispatch/pallas_call | solution.py:105
  7.2 3.0 %collective-permute-start.4 = (bf16[64,1152]{1,0:T(8,128)(2,1)}, bf16[64,1152]{1,0:T(8,128)(2,1)S(1)}, u32[]{:S(2)}, u32[]{:S(2)}) collective-permute-start(bf16[64,1152]{1,0:T(8,128)(2,1)} %get-tuple-element.27), channel_id=1, source_target_pairs={{0,2},{1,3},{2,0},{3,1},{4,6},{5,7},{6,4},{7,5},{8,10},{9,11},{10,... | collective-permute-start | bytes 442376 | tf_op jit(solution)/shard_map/ppermute | solution.py:467
  10.2 1.4 %collective-permute-start.5 = (bf16[64,1152]{1,0:T(8,128)(2,1)}, bf16[64,1152]{1,0:T(8,128)(2,1)}, u32[]{:S(2)}, u32[]{:S(2)}) collective-permute-start(bf16[64,1152]{1,0:T(8,128)(2,1)} %get-tuple-element.28), channel_id=1, source_target_pairs={{0,3},{1,0},{2,1},{3,2},{4,7},{5,4},{6,5},{7,6},{8,11},{9,8},{10,9... | collective-permute-start | bytes 442376 | tf_op jit(solution)/shard_map/ppermute | solution.py:467
  12.3 0.9 %constant_dynamic-slice_fusion = bf16[384,1024]{1,0:T(8,128)(2,1)} fusion(bf16[1024,1024]{1,0:T(8,128)(2,1)S(1)} %bitcast.13, s32[]{:T(128)S(6)} %select_n.41), kind=kLoop, calls=%fused_computation.7 | loop fusion | bytes 1572868 | tf_op jit(solution)/shard_map/dynamic_slice | solution.py:478
  13.2 2.4 %collective-permute-start = (bf16[384,1024]{1,0:T(8,128)(2,1)}, bf16[384,1024]{1,0:T(8,128)(2,1)S(1)}, u32[]{:S(2)}, u32[]{:S(2)}) collective-permute-start(bf16[384,1024]{1,0:T(8,128)(2,1)} %constant_dynamic-slice_fusion), channel_id=1, source_target_pairs={{0,1},{2,3},{1,0},{3,2},{4,5},{6,7},{5,4},{7,6},{8,9},{10,11},{9,8... | collective-permute-start | bytes 2359304 | tf_op jit(solution)/shard_map/ppermute | solution.py:479
  15.6 1.5 %collective-permute-done.5.refs_3_ = bf16[64,1152]{1,0:T(8,128)(2,1)} collective-permute-done((bf16[64,1152]{1,0:T(8,128)(2,1)}, bf16[64,1152]{1,0:T(8,128)(2,1)}, u32[]{:S(2)}, u32[]{:S(2)}) %collective-permute-start.5) | collective-permute-done | bytes 147488 | tf_op jit(solution)/shard_map/ppermute | solution.py:467
  17.1 2.7 %collective-permute-done.3.refs_1_ = bf16[64,1152]{1,0:T(8,128)(2,1)} collective-permute-done((bf16[64,1152]{1,0:T(8,128)(2,1)}, bf16[64,1152]{1,0:T(8,128)(2,1)}, u32[]{:S(2)}, u32[]{:S(2)}) %collective-permute-start.3) | collective-permute-done | bytes 147488 | tf_op jit(solution)/shard_map/ppermute | solution.py:467
  19.9 0.9 %copy-done.5 = bf16[64,1152]{1,0:T(8,128)(2,1)S(1)} copy-done((bf16[64,1152]{1,0:T(8,128)(2,1)S(1)}, bf16[64,1152]{1,0:T(8,128)(2,1)}, u32[]{:S(2)}) %copy-start.5) | copy-done | bytes 147480
  21.5 1.3 %gather_slots.1 = (bf16[16,1024]{1,0:T(8,128)(2,1)S(1)}, bf16[16,1024]{1,0:T(8,128)(2,1)S(1)}, bf16[16,1024]{1,0:T(8,128)(2,1)S(1)}, bf16[16,1024]{1,0:T(8,128)(2,1)S(1)}) custom-call(f32[1,1024]{1,0:T(1,128)S(1)} %bitcast.20, bf16[64,1152]{1,0:T(8,128)(2,1)S(1)} %copy-done.5, bf16[64,1152]{1,0:T(8,128)(2,1)} %collective-permute-done.3.refs_1_, ...), custom_call_target="tpu_custom_call" | custom-call | flops 2097152 | bytes 262144 | tf_op jit(solution)/shard_map/gather_slots/pallas_call | solution.py:145
  23.7 2.0 %collective-permute-start.7 = (bf16[16,1024]{1,0:T(8,128)(2,1)S(1)}, bf16[16,1024]{1,0:T(8,128)(2,1)S(1)}, u32[]{:S(2)}, u32[]{:S(2)}) collective-permute-start(bf16[16,1024]{1,0:T(8,128)(2,1)S(1)} %get-tuple-element.33), channel_id=1, source_target_pairs={{0,8},{4,12},{8,16},{12,20},{16,24},{20,28},{24,0},{28,4},{1,9},{5... | collective-permute-start | bytes 98312 | tf_op jit(solution)/shard_map/ppermute | solution.py:467
  25.8 2.6 %collective-permute-start.8 = (bf16[16,1024]{1,0:T(8,128)(2,1)S(1)}, bf16[16,1024]{1,0:T(8,128)(2,1)S(1)}, u32[]{:S(2)}, u32[]{:S(2)}) collective-permute-start(bf16[16,1024]{1,0:T(8,128)(2,1)S(1)} %get-tuple-element.34), channel_id=1, source_target_pairs={{0,16},{4,20},{8,24},{12,28},{16,0},{20,4},{24,8},{28,12},{1,17},{... | collective-permute-start | bytes 98312 | tf_op jit(solution)/shard_map/ppermute | solution.py:467
  28.4 1.3 %collective-permute-start.9 = (bf16[16,1024]{1,0:T(8,128)(2,1)S(1)}, bf16[16,1024]{1,0:T(8,128)(2,1)S(1)}, u32[]{:S(2)}, u32[]{:S(2)}) collective-permute-start(bf16[16,1024]{1,0:T(8,128)(2,1)S(1)} %get-tuple-element.35), channel_id=1, source_target_pairs={{0,24},{4,28},{8,0},{12,4},{16,8},{20,12},{24,16},{28,20},{1,25},{... | collective-permute-start | bytes 98312 | tf_op jit(solution)/shard_map/ppermute | solution.py:467
  29.7 1.9 %combine_weights.2._.share_ref = bf16[1024,256]{1,0:T(8,128)(2,1)S(1)} custom-call(s32[1]{0:T(128)} %constant.57.clone.1.valid_ref, bf16[256,1024]{1,0:T(8,128)(2,1)S(1)} %copy-done.3, f32[1,1024]{1,0:T(1,128)S(1)} %bitcast.18, bf16[384,1024]{1,0:T(8,128)(2,1)S(1)} %edge_rows.1._, bf16[1024,1024]{1,0:T(8,128)(2,1)S(1)} %bitcast.15), custom_call_target="tpu_custom_call" | custom-call | flops 536870912 | bytes 2097152 | tf_op jit(solution)/shard_map/combine_weights/pallas_call | solution.py:254
  32.3 2.8 %experts.1 = (bf16[16,1024]{1,0:T(8,128)(2,1)S(1)}, bf16[16,1024]{1,0:T(8,128)(2,1)S(1)}, bf16[16,1024]{1,0:T(8,128)(2,1)S(1)}, bf16[16,1024]{1,0:T(8,128)(2,1)S(1)}) custom-call(s32[1]{0:T(128)} %bitcast.8.core_ref, bf16[1024,256]{1,0:T(8,128)(2,1)S(1)} %combine_weights.2._.share_ref, bf16[2,1024,512]{2,1,0:T(8,128)(2,1)S(1)} %copy-done.1, ...), custom_call_target="tpu_custom_call" | custom-call | flops 536870912 | bytes 8388608 | tf_op jit(solution)/shard_map/experts/pallas_call | solution.py:200
  35.2 3.2 %collective-permute-start.10 = (bf16[16,1024]{1,0:T(8,128)(2,1)S(1)}, bf16[16,1024]{1,0:T(8,128)(2,1)S(1)}, u32[]{:S(2)}, u32[]{:S(2)}) collective-permute-start(bf16[16,1024]{1,0:T(8,128)(2,1)S(1)} %get-tuple-element.40), channel_id=1, source_target_pairs={{0,24},{4,28},{8,0},{12,4},{16,8},{20,12},{24,16},{28,20},{1,25},{... | collective-permute-start | bytes 98312 | tf_op jit(solution)/shard_map/ppermute | solution.py:467
  39.0 1.0 %collective-permute-done.10 = bf16[16,1024]{1,0:T(8,128)(2,1)S(1)} collective-permute-done((bf16[16,1024]{1,0:T(8,128)(2,1)S(1)}, bf16[16,1024]{1,0:T(8,128)(2,1)S(1)}, u32[]{:S(2)}, u32[]{:S(2)}) %collective-permute-start.10) | collective-permute-done | bytes 32800 | tf_op jit(solution)/shard_map/ppermute | solution.py:467
  40.0 3.2 %collective-permute-done.11 = bf16[16,1024]{1,0:T(8,128)(2,1)S(1)} collective-permute-done((bf16[16,1024]{1,0:T(8,128)(2,1)S(1)}, bf16[16,1024]{1,0:T(8,128)(2,1)S(1)}, u32[]{:S(2)}, u32[]{:S(2)}) %collective-permute-start.11) | collective-permute-done | bytes 32800 | tf_op jit(solution)/shard_map/ppermute | solution.py:467
  43.2 0.9 %collective-permute-done.12 = bf16[16,1024]{1,0:T(8,128)(2,1)S(1)} collective-permute-done((bf16[16,1024]{1,0:T(8,128)(2,1)S(1)}, bf16[16,1024]{1,0:T(8,128)(2,1)S(1)}, u32[]{:S(2)}, u32[]{:S(2)}) %collective-permute-start.12) | collective-permute-done | bytes 32800 | tf_op jit(solution)/shard_map/ppermute | solution.py:467
  44.1 4.3 %collective-permute-start.15 = (bf16[64,1024]{1,0:T(8,128)(2,1)S(1)}, bf16[64,1024]{1,0:T(8,128)(2,1)S(1)}, u32[]{:S(2)}, u32[]{:S(2)}) collective-permute-start(bf16[64,1024]{1,0:T(8,128)(2,1)S(1)} %constant_dynamic-update-slice_fusion.rest_0_), channel_id=1, source_target_pairs={{0,1},{1,2},{2,3},{3,0},{4,5},{5,6},{6,7},{7,4},{8,9},{9,10},{10,1... | collective-permute-start | bytes 393224 | tf_op jit(solution)/shard_map/ppermute | solution.py:467
  48.6 2.9 %collective-permute-start.13 = (bf16[64,1024]{1,0:T(8,128)(2,1)S(1)}, bf16[64,1024]{1,0:T(8,128)(2,1)S(1)}, u32[]{:S(2)}, u32[]{:S(2)}) collective-permute-start(bf16[64,1024]{1,0:T(8,128)(2,1)S(1)} %constant_dynamic-update-slice_fusion.rest_0_), channel_id=1, source_target_pairs={{0,3},{1,0},{2,1},{3,2},{4,7},{5,4},{6,5},{7,6},{8,11},{9,8},{10,9... | collective-permute-start | bytes 393224 | tf_op jit(solution)/shard_map/ppermute | solution.py:467
  51.6 2.7 %combine_weights.3 = (bf16[384,256]{1,0:T(8,128)(2,1)S(1)}, bf16[384,256]{1,0:T(8,128)(2,1)S(1)}, f32[7,192,1024]{2,1,0:T(8,128)S(1)}) custom-call(s32[2]{0:T(128)S(1)} %add_convert_fusion.valid_ref, bf16[256,1024]{1,0:T(8,128)(2,1)S(1)} %copy-done.3, f32[1,1024]{1,0:T(1,128)S(1)} %bitcast.19, bf16[16,1024]{1,0:T(8,128)(2,1)S(1)} %get-tuple-element.36._, ...), custom_call_target="tpu_custom_call" | custom-call | flops 402653184 | bytes 1572864 | tf_op jit(solution)/shard_map/combine_weights/pallas_call | solution.py:254
  54.3 3.2 %collective-permute-done.14.rest_2_ = bf16[64,1024]{1,0:T(8,128)(2,1)S(1)} collective-permute-done((bf16[64,1024]{1,0:T(8,128)(2,1)S(1)}, bf16[64,1024]{1,0:T(8,128)(2,1)S(1)}, u32[]{:S(2)}, u32[]{:S(2)}) %collective-permute-start.14) | collective-permute-done | bytes 131104 | tf_op jit(solution)/shard_map/ppermute | solution.py:467
  57.5 1.1 %collective-permute-done.13.rest_1_ = bf16[64,1024]{1,0:T(8,128)(2,1)S(1)} collective-permute-done((bf16[64,1024]{1,0:T(8,128)(2,1)S(1)}, bf16[64,1024]{1,0:T(8,128)(2,1)S(1)}, u32[]{:S(2)}, u32[]{:S(2)}) %collective-permute-start.13) | collective-permute-done | bytes 131104 | tf_op jit(solution)/shard_map/ppermute | solution.py:467
  58.6 13.4 %block_fields.1 = bf16[1024,1024]{1,0:T(8,128)(2,1)} custom-call(s32[2]{0:T(128)S(1)} %broadcast_select_fusion.place_ref, bf16[1024,1024]{1,0:T(8,128)(2,1)S(1)} %bitcast.16, bf16[384,1024]{1,0:T(8,128)(2,1)S(1)} %collective-permute-done.refs_0_.low_ref, bf16[384,1024]{1,0:T(8,128)(2,1)S(1)} %collective-permute-done.6.refs_1_.high_ref, ...), custom_call_target="tpu_custom_call" | custom-call | flops 6442450944 | bytes 8388608 | tf_op jit(solution)/shard_map/block_fields/pallas_call | solution.py:429
  (55 shorter events, 4.9 us)
Async XLA Ops:
  0.0 11.7 %collective-permute-start.1 = (bf16[2,1024,512]{2,1,0:T(8,128)(2,1)}, bf16[2,1024,512]{2,1,0:T(8,128)(2,1)}, u32[]{:S(2)}, u32[]{:S(2)}) collective-permute-start(bf16[2,1024,512]{2,1,0:T(8,128)(2,1)} %in_own.1), channel_id=1, source_target_pairs={{0,4},{4,0},{8,12},{12,8},{16,20},{20,16},{24,28},{28,24},{1,5},{5... | collective-permute-start | bytes 6291464 | tf_op jit(solution)/shard_map/ppermute | solution.py:480
  0.5 11.2 %collective-permute-start.2 = (bf16[2,512,1024]{2,1,0:T(8,128)(2,1)}, bf16[2,512,1024]{2,1,0:T(8,128)(2,1)}, u32[]{:S(2)}, u32[]{:S(2)}) collective-permute-start(bf16[2,512,1024]{2,1,0:T(8,128)(2,1)} %out_own.1), channel_id=1, source_target_pairs={{0,4},{4,0},{8,12},{12,8},{16,20},{20,16},{24,28},{28,24},{1,5},{5... | collective-permute-start | bytes 6291464 | tf_op jit(solution)/shard_map/ppermute | solution.py:481
  7.2 8.4 %collective-permute-start.4 = (bf16[64,1152]{1,0:T(8,128)(2,1)}, bf16[64,1152]{1,0:T(8,128)(2,1)S(1)}, u32[]{:S(2)}, u32[]{:S(2)}) collective-permute-start(bf16[64,1152]{1,0:T(8,128)(2,1)} %get-tuple-element.27), channel_id=1, source_target_pairs={{0,2},{1,3},{2,0},{3,1},{4,6},{5,7},{6,4},{7,5},{8,10},{9,11},{10,... | collective-permute-start | bytes 442376 | tf_op jit(solution)/shard_map/ppermute | solution.py:467
  10.2 6.9 %collective-permute-start.5 = (bf16[64,1152]{1,0:T(8,128)(2,1)}, bf16[64,1152]{1,0:T(8,128)(2,1)}, u32[]{:S(2)}, u32[]{:S(2)}) collective-permute-start(bf16[64,1152]{1,0:T(8,128)(2,1)} %get-tuple-element.28), channel_id=1, source_target_pairs={{0,3},{1,0},{2,1},{3,2},{4,7},{5,4},{6,5},{7,6},{8,11},{9,8},{10,9... | collective-permute-start | bytes 442376 | tf_op jit(solution)/shard_map/ppermute | solution.py:467
  11.7 8.2 %collective-permute-start.3 = (bf16[64,1152]{1,0:T(8,128)(2,1)}, bf16[64,1152]{1,0:T(8,128)(2,1)}, u32[]{:S(2)}, u32[]{:S(2)}) collective-permute-start(bf16[64,1152]{1,0:T(8,128)(2,1)} %get-tuple-element.26), channel_id=1, source_target_pairs={{0,1},{1,2},{2,3},{3,0},{4,5},{5,6},{6,7},{7,4},{8,9},{9,10},{10,1... | collective-permute-start | bytes 442376 | tf_op jit(solution)/shard_map/ppermute | solution.py:467
  13.2 38.3 %collective-permute-start = (bf16[384,1024]{1,0:T(8,128)(2,1)}, bf16[384,1024]{1,0:T(8,128)(2,1)S(1)}, u32[]{:S(2)}, u32[]{:S(2)}) collective-permute-start(bf16[384,1024]{1,0:T(8,128)(2,1)} %constant_dynamic-slice_fusion), channel_id=1, source_target_pairs={{0,1},{2,3},{1,0},{3,2},{4,5},{6,7},{5,4},{7,6},{8,9},{10,11},{9,8... | collective-permute-start | bytes 2359304 | tf_op jit(solution)/shard_map/ppermute | solution.py:479
  22.9 28.7 %collective-permute-start.6 = (bf16[384,1024]{1,0:T(8,128)(2,1)S(1)}, bf16[384,1024]{1,0:T(8,128)(2,1)S(1)}, u32[]{:S(2)}, u32[]{:S(2)}) collective-permute-start(bf16[384,1024]{1,0:T(8,128)(2,1)S(1)} %edge_rows.1._), channel_id=1, source_target_pairs={{1,2},{2,1},{5,6},{6,5},{9,10},{10,9},{13,14},{14,13},{17,18},{18,... | collective-permute-start | bytes 2359304 | tf_op jit(solution)/shard_map/ppermute | solution.py:491
  23.7 7.9 %collective-permute-start.7 = (bf16[16,1024]{1,0:T(8,128)(2,1)S(1)}, bf16[16,1024]{1,0:T(8,128)(2,1)S(1)}, u32[]{:S(2)}, u32[]{:S(2)}) collective-permute-start(bf16[16,1024]{1,0:T(8,128)(2,1)S(1)} %get-tuple-element.33), channel_id=1, source_target_pairs={{0,8},{4,12},{8,16},{12,20},{16,24},{20,28},{24,0},{28,4},{1,9},{5... | collective-permute-start | bytes 98312 | tf_op jit(solution)/shard_map/ppermute | solution.py:467
  25.8 5.9 %collective-permute-start.8 = (bf16[16,1024]{1,0:T(8,128)(2,1)S(1)}, bf16[16,1024]{1,0:T(8,128)(2,1)S(1)}, u32[]{:S(2)}, u32[]{:S(2)}) collective-permute-start(bf16[16,1024]{1,0:T(8,128)(2,1)S(1)} %get-tuple-element.34), channel_id=1, source_target_pairs={{0,16},{4,20},{8,24},{12,28},{16,0},{20,4},{24,8},{28,12},{1,17},{... | collective-permute-start | bytes 98312 | tf_op jit(solution)/shard_map/ppermute | solution.py:467
  28.4 3.9 %collective-permute-start.9 = (bf16[16,1024]{1,0:T(8,128)(2,1)S(1)}, bf16[16,1024]{1,0:T(8,128)(2,1)S(1)}, u32[]{:S(2)}, u32[]{:S(2)}) collective-permute-start(bf16[16,1024]{1,0:T(8,128)(2,1)S(1)} %get-tuple-element.35), channel_id=1, source_target_pairs={{0,24},{4,28},{8,0},{12,4},{16,8},{20,12},{24,16},{28,20},{1,25},{... | collective-permute-start | bytes 98312 | tf_op jit(solution)/shard_map/ppermute | solution.py:467
  32.3 19.3 %copy-start.4 = (f32[7,7,1024]{2,1,0:T(8,128)S(1)}, f32[7,7,1024]{2,1,0:T(8,128)}, u32[]{:S(2)}) copy-start(f32[7,7,1024]{2,1,0:T(8,128)} %refs_3_.1) | copy-start | bytes 602116
  32.3 19.3 %copy-start.6 = (bf16[192,40]{1,0:T(8,128)(2,1)S(1)}, bf16[192,40]{1,0:T(8,128)(2,1)}, u32[]{:S(2)}) copy-start(bf16[192,40]{1,0:T(8,128)(2,1)} %constant.59.clone.refs_2_) | copy-start | bytes 46084
  35.1 23.4 %copy-start.9 = (bf16[1024,1024]{1,0:T(8,128)(2,1)S(1)}, bf16[1024,1024]{1,0:T(8,128)(2,1)}, u32[]{:S(2)}) copy-start(bf16[1024,1024]{1,0:T(8,128)(2,1)} %proj_ref.1) | copy-start | bytes 6291460
  35.1 23.4 %copy-start.10 = (f32[1024]{0:T(1024)S(1)}, f32[1024]{0:T(1024)}, u32[]{:S(2)}) copy-start(f32[1024]{0:T(1024)} %param.23) | copy-start | bytes 12292
  35.2 23.4 %copy-start.11 = (f32[1024]{0:T(1024)S(1)}, f32[1024]{0:T(1024)}, u32[]{:S(2)}) copy-start(f32[1024]{0:T(1024)} %param.25) | copy-start | bytes 12292
  35.2 23.4 %copy-start.12 = (bf16[128,256]{1,0:T(8,128)(2,1)S(1)}, bf16[128,256]{1,0:T(8,128)(2,1)}, u32[]{:S(2)}) copy-start(bf16[128,256]{1,0:T(8,128)(2,1)} %constant.63.clone.cols_ref) | copy-start | bytes 196612
  35.2 23.3 %copy-start.13 = (bf16[128,256]{1,0:T(8,128)(2,1)S(1)}, bf16[128,256]{1,0:T(8,128)(2,1)}, u32[]{:S(2)}) copy-start(bf16[128,256]{1,0:T(8,128)(2,1)} %constant.62.clone.freq_ref) | copy-start | bytes 196612
  35.2 23.3 %copy-start.14 = (bf16[128,128]{1,0:T(8,128)(2,1)S(1)}, bf16[128,128]{1,0:T(8,128)(2,1)}, u32[]{:S(2)}) copy-start(bf16[128,128]{1,0:T(8,128)(2,1)} %constant.64.clone.fine_ref) | copy-start | bytes 98308
  35.2 4.8 %collective-permute-start.10 = (bf16[16,1024]{1,0:T(8,128)(2,1)S(1)}, bf16[16,1024]{1,0:T(8,128)(2,1)S(1)}, u32[]{:S(2)}, u32[]{:S(2)}) collective-permute-start(bf16[16,1024]{1,0:T(8,128)(2,1)S(1)} %get-tuple-element.40), channel_id=1, source_target_pairs={{0,24},{4,28},{8,0},{12,4},{16,8},{20,12},{24,16},{28,20},{1,25},{... | collective-permute-start | bytes 98312 | tf_op jit(solution)/shard_map/ppermute | solution.py:467
  38.4 4.8 %collective-permute-start.11 = (bf16[16,1024]{1,0:T(8,128)(2,1)S(1)}, bf16[16,1024]{1,0:T(8,128)(2,1)S(1)}, u32[]{:S(2)}, u32[]{:S(2)}) collective-permute-start(bf16[16,1024]{1,0:T(8,128)(2,1)S(1)} %get-tuple-element.41), channel_id=1, source_target_pairs={{0,16},{4,20},{8,24},{12,28},{16,0},{20,4},{24,8},{28,12},{1,17},{... | collective-permute-start | bytes 98312 | tf_op jit(solution)/shard_map/ppermute | solution.py:467
  38.4 5.7 %collective-permute-start.12 = (bf16[16,1024]{1,0:T(8,128)(2,1)S(1)}, bf16[16,1024]{1,0:T(8,128)(2,1)S(1)}, u32[]{:S(2)}, u32[]{:S(2)}) collective-permute-start(bf16[16,1024]{1,0:T(8,128)(2,1)S(1)} %get-tuple-element.42), channel_id=1, source_target_pairs={{0,8},{4,12},{8,16},{12,20},{16,24},{20,28},{24,0},{28,4},{1,9},{5... | collective-permute-start | bytes 98312 | tf_op jit(solution)/shard_map/ppermute | solution.py:467
  44.1 10.1 %collective-permute-start.15 = (bf16[64,1024]{1,0:T(8,128)(2,1)S(1)}, bf16[64,1024]{1,0:T(8,128)(2,1)S(1)}, u32[]{:S(2)}, u32[]{:S(2)}) collective-permute-start(bf16[64,1024]{1,0:T(8,128)(2,1)S(1)} %constant_dynamic-update-slice_fusion.rest_0_), channel_id=1, source_target_pairs={{0,1},{1,2},{2,3},{3,0},{4,5},{5,6},{6,7},{7,4},{8,9},{9,10},{10,1... | collective-permute-start | bytes 393224 | tf_op jit(solution)/shard_map/ppermute | solution.py:467
  48.4 9.0 %collective-permute-start.14 = (bf16[64,1024]{1,0:T(8,128)(2,1)S(1)}, bf16[64,1024]{1,0:T(8,128)(2,1)S(1)}, u32[]{:S(2)}, u32[]{:S(2)}) collective-permute-start(bf16[64,1024]{1,0:T(8,128)(2,1)S(1)} %constant_dynamic-update-slice_fusion.rest_0_), channel_id=1, source_target_pairs={{0,2},{1,3},{2,0},{3,1},{4,6},{5,7},{6,4},{7,5},{8,10},{9,11},{10,... | collective-permute-start | bytes 393224 | tf_op jit(solution)/shard_map/ppermute | solution.py:467
  48.6 10.0 %collective-permute-start.13 = (bf16[64,1024]{1,0:T(8,128)(2,1)S(1)}, bf16[64,1024]{1,0:T(8,128)(2,1)S(1)}, u32[]{:S(2)}, u32[]{:S(2)}) collective-permute-start(bf16[64,1024]{1,0:T(8,128)(2,1)S(1)} %constant_dynamic-update-slice_fusion.rest_0_), channel_id=1, source_target_pairs={{0,3},{1,0},{2,1},{3,2},{4,7},{5,4},{6,5},{7,6},{8,11},{9,8},{10,9... | collective-permute-start | bytes 393224 | tf_op jit(solution)/shard_map/ppermute | solution.py:467
  (8 other events, 59.8 us)

commit v4 on v3

--- a/solution.py
+++ b/solution.py
@@ -215,15 +215,32 @@
     )(core, after, w_in, w_out, in_other, out_other, *parts)
 
 
-def copy_kernel(start_ref, cells_ref, _, out_ref):
-    rows = out_ref.shape[0]
-    out_ref[...] = cells_ref[pl.ds(pl.multiple_of(start_ref[0], LANES), rows), :]
-
-
-def edge_rows(start, cells, rows, after):
-    return pl.pallas_call(
-        copy_kernel,
-        out_shape=jax.ShapeDtypeStruct((rows, cells.shape[1]), BF16),
+def pass_kernel(value_ref, _, out_ref):
+    out_ref[...] = value_ref[...]
+
+
+def after(value, other):
+    return pl.pallas_call(
+        pass_kernel,
+        out_shape=jax.ShapeDtypeStruct(value.shape, value.dtype),
+        in_specs=[VMEM, ANY],
+        out_specs=VMEM,
+        compiler_params=pltpu.CompilerParams(vmem_limit_bytes=8 * MIB),
+        cost_estimate=cost(0, 4 * value.size),
+        name="after",
+    )(value, other)
+
+
+def copy_kernel(lane, start_ref, cells_ref, _, out_ref):
+    rows, wide = out_ref.shape
+    at = pl.ds(pl.multiple_of(start_ref[0], LANES), rows)
+    out_ref[...] = cells_ref[at, lane : lane + wide]
+
+
+def edge_rows(start, cells, rows, lane, wide, after):
+    return pl.pallas_call(
+        functools.partial(copy_kernel, lane),
+        out_shape=jax.ShapeDtypeStruct((rows, wide), BF16),
         in_specs=[SMEM, VMEM, ANY],
         out_specs=VMEM,
         compiler_params=pltpu.CompilerParams(vmem_limit_bytes=8 * MIB),
@@ -232,15 +249,19 @@
     )(start, cells, after)
 
 
-def combine_kernel(count, valid_ref, keys_ref, gain_ref, _, *refs):
+def combine_kernel(counts, valid_ref, keys_ref, gain_ref, _, *refs):
     block = 128
-    if len(refs) > 2 * count:
-        fill_spectrum(refs[count], refs[count + 1], refs[-1])
-        refs = refs[:count] + refs[count + 2 : -1]
-    for at, (cells_ref, out_ref) in enumerate(zip(refs[:count], refs[count:])):
-        for start in range(0, cells_ref.shape[0], block):
+    total = sum(counts)
+    sources, refs = refs[:total], refs[total:]
+    if len(refs) > len(counts):
+        fill_spectrum(refs[0], refs[1], refs[-1])
+        refs = refs[2:-1]
+    for at, (count, out_ref) in enumerate(zip(counts, refs)):
+        held, sources = sources[:count], sources[count:]
+        for start in range(0, out_ref.shape[0], block):
             rows = slice(start, start + block)
-            normed = rms_scale(cells_ref[rows, :].astype(F32), gain_ref[...]).astype(BF16)
+            cells = jnp.concatenate([ref[rows, :] for ref in held], axis=1).astype(F32)
+            normed = rms_scale(cells, gain_ref[...]).astype(BF16)
             logits = dot_nt(normed, keys_ref[...])
             raised = jnp.exp(logits - jnp.max(logits, axis=-1, keepdims=True))
             share = raised * (1.0 / jnp.sum(raised, axis=-1, keepdims=True))
@@ -250,17 +271,18 @@
 def combine_weights(valid, cells, keys, gain, after, filters=()):
     made = [(filters[1].shape[0], filters[0].shape[0], filters[1].shape[2])] if filters else []
     width, slots = gain.shape[1], keys.shape[0]
-    total = sum(part.shape[0] for part in cells)
-    return pl.pallas_call(
-        functools.partial(combine_kernel, len(cells)),
-        out_shape=[jax.ShapeDtypeStruct((part.shape[0], slots), BF16) for part in cells]
+    total = sum(parts[0].shape[0] for parts in cells)
+    flat = [part for parts in cells for part in parts]
+    return pl.pallas_call(
+        functools.partial(combine_kernel, [len(parts) for parts in cells]),
+        out_shape=[jax.ShapeDtypeStruct((parts[0].shape[0], slots), BF16) for parts in cells]
         + [jax.ShapeDtypeStruct(shape, F32) for shape in made],
-        in_specs=[SMEM, VMEM, VMEM, ANY] + [VMEM] * (len(cells) + len(filters)),
+        in_specs=[SMEM, VMEM, VMEM, ANY] + [VMEM] * (len(flat) + len(filters)),
         out_specs=[VMEM] * (len(cells) + len(made)),
         compiler_params=pltpu.CompilerParams(vmem_limit_bytes=16 * MIB),
         cost_estimate=cost(2 * total * width * slots, 2 * total * width, total * slots),
         name="combine_weights",
-    )(valid, keys, gain, after, *cells, *filters)
+    )(valid, keys, gain, after, *flat, *filters)
 
 
 def batch(rows):
@@ -322,7 +344,7 @@
 
 
 def block_kernel(
-    dims, place_ref, cells_ref, low_ref, high_ref, share_ref, share_low, share_high, spectrum_ref, freq_ref,
+    dims, place_ref, cells_ref, first_ref, second_a, second_b, share_ref, share_low, share_high, spectrum_ref, freq_ref,
     cols_ref, fine_ref, ln_ref, proj_ref, scale_ref, *rest
 ):
     rows, cols, taps = dims
@@ -343,15 +365,17 @@
         for lane in range(0, width, chunk):
             lanes = slice(lane, lane + chunk)
             mixed = jnp.dot(picked, slots_ref[:, lanes], preferred_element_type=F32)
-            state = (cells[at, lanes].astype(F32) + mixed).astype(BF16)
+            wide = cells[0].shape[1]
+            held = cells[lane // wide][at, lane % wide : lane % wide + chunk]
+            state = (held.astype(F32) + mixed).astype(BF16)
             if keep:
                 state_ref[at, lanes] = state
             twice = jnp.concatenate([state, state], axis=0)
             freqs_ref[to, :, lanes] = jnp.dot(freq_ref[...], twice, preferred_element_type=F32)
 
     for row in range(reach):
-        mix(low_ref, share_low, row, row + place_ref[0], False)
-        mix(high_ref, share_high, row, row + place_ref[1], False)
+        mix((first_ref,), share_low, row, row + place_ref[0], False)
+        mix((second_a, second_b), share_high, row, row + place_ref[1], False)
 
     at_once = batch(rows)
 
@@ -359,7 +383,7 @@
     def _(step):
         for extra in range(at_once):
             row = step * at_once + extra
-            mix(cells_ref, share_ref, row, row + reach, True)
+            mix((cells_ref,), share_ref, row, row + reach, True)
 
     tile = 16
 
@@ -429,7 +453,7 @@
     return pl.pallas_call(
         functools.partial(block_kernel, dims),
         out_shape=jax.ShapeDtypeStruct((total, width), BF16),
-        in_specs=[SMEM] + [VMEM] * (13 + len(slot_parts)),
+        in_specs=[SMEM] + [VMEM] * (14 + len(slot_parts)),
         out_specs=VMEM,
         scratch_shapes=[
             pltpu.VMEM((slots, width), BF16),
@@ -475,8 +499,8 @@
         pairs = [(i, i + 1) for i in range(start, count_tok - 1, 2)]
         return pairs + [(j, i) for i, j in pairs]
 
-    edge = lax.dynamic_slice_in_dim(cells, jnp.where(even, last, 0), reach * cols, axis=0)
-    first_halo = lax.ppermute(edge, "tok", swap(0))
+    half = width // 2
+    place = jnp.where(even, 0, last).reshape(1)
     in_other = lax.ppermute(w_in, "fc", other)
     out_other = lax.ppermute(w_out, "fc", other)
 
@@ -485,19 +509,27 @@
     numer[1], in_other, out_other = tie((numer[1], in_other, out_other))
     parts = [numer[0]] + [shift(numer[k], "tok", k) for k in range(1, count_tok)]
 
+    first_halo = edge_rows(last - place, cells, reach * cols, 0, width, parts[1])
+    first_halo = lax.ppermute(first_halo, "tok", swap(0))
+    around = edge_rows(place, cells, reach * cols, half, half, parts[1])
+    around = lax.ppermute(around, "tok", [(1, 3), (2, 0)] if count_tok == 4 else swap(1))
+
     slot_in = gather_slots(parts, slot_gain, count_z)
     arrived = [slot_in[0]] + [shift(slot_in[k], "fc", 2 * k) for k in range(1, count_z)]
-    first = edge_rows(jnp.where(even, 0, last).reshape(1), cells, reach * cols, slot_in[0])
-    second_halo = lax.ppermute(first, "tok", swap(1))
+    around, seen = after(around, slot_in[0]), slot_in[0]
+    if count_tok == 4:
+        around = lax.ppermute(around, "tok", [(3, 2), (0, 1)])
     always = jnp.ones((1,), jnp.int32)
-    (share,) = combine_weights(always, [cells], keys, norm_gain, first)
+    (share,) = combine_weights(always, [[cells]], keys, norm_gain, seen)
     core = (at_fc % 2).astype(jnp.int32).reshape(1)
     made = experts(core, share, arrived, w_in, w_out, in_other, out_other, slots_exp)
+    direct = edge_rows(place, cells, reach * cols, 0, half, made[0])
+    direct = lax.ppermute(direct, "tok", swap(1))
     back = [made[0]] + [shift(made[k], "fc", -2 * k) for k in range(1, count_z)]
     mine = jnp.concatenate(back, axis=0)
     above, below = at_tok > 0, at_tok < count_tok - 1
     inside = jnp.stack([jnp.where(even, below, above), jnp.where(even, above, below)])
-    halo = (first_halo, second_halo)
+    halo = ((first_halo,), (direct, around))
     freq, to_cols, fine, coef = wave(cols, taps)
     *halo_shares, filters = combine_weights(
         inside.astype(jnp.int32), halo, keys, norm_gain, made[0], (coef, conv_weight)
@@ -506,7 +538,7 @@
     every = [mine] + [shift(mine, "tok", -k) for k in range(1, count_tok)]
 
     fields = block_fields(
-        (rows, cols, taps), places.astype(jnp.int32), cells, halo, (share, *halo_shares), filters,
+        (rows, cols, taps), places.astype(jnp.int32), cells, (first_halo, direct, around), (share, *halo_shares), filters,
         ln_gain, proj, layer_scale, every, (freq, to_cols, fine),
     )
     return fields.reshape(1, rows, cols, width)

time: 72.2 us -> 67.2 us (0.931)
  waiting for transfers between devices: 14.2 us -> 6.43 us
  starting transfers between devices: 26 us -> 31.5 us
  local copies, waits for them, and re-layouts: 2.61 us -> 0.12 us
  Pallas kernels: 28.2 us -> 27.3 us
    ppermute x12, waiting for transfers between devices: 14.2 us -> 4.11 us  [shift(): lax.ppermute(value, axis, [(i, (i + step) % count) for i in range(count)])]
    ppermute x2 -> x4, starting transfers between devices: 3.24 us -> 10.1 us  [the longest x1 4.61 us: local(): around = lax.ppermute(around, 'tok', [(3, 2), (0, 1)])]
    ppermute x2 -> x4, waiting for transfers between devices: 0.01 us -> 1.94 us  [the longest x1 1.93 us: local(): around = lax.ppermute(around, 'tok', [(3, 2), (0, 1)])]
    unnamed x35, local copies, waits for them, and re-layouts: 1.68 us -> 0.11 us
    ppermute x12, starting transfers between devices: 22.2 us -> 20.9 us  [shift(): lax.ppermute(value, axis, [(i, (i + step) % count) for i in range(count)])]
    pallas_call x1, Pallas kernels: 1.3 us -> 0.31 us  [gather_slots(): pl.pallas_call(functools.partial(gather_kernel, count_z), out_shape=[jax....]
    dynamic_slice x1 -> x0, local copies, waits for them, and re-layouts: 0.93 us -> none  [local(): lax.dynamic_slice_in_dim(cells, jnp.where(even, last, 0), reach * cols, a...]
    pallas_call x3 -> x6, Pallas kernels: 4.66 us -> 4.75 us  [the longest x2 4.62 us: combine_weights(): pl.pallas_call(functools.partial(combine_kernel, [len(parts) for parts in...]
  transfers between devices with their start and end apart: 16 -> 18, of which waited for: 8 -> 6; matrix products, arithmetic and copies ran while one was open for 2% -> 1% of each run, Pallas kernels for 21% -> 21%
where the time goes in v4:
time: 67.2 us; the launch traced here: 66.5 us
  starting transfers between devices  31.5 us (47%)
  Pallas kernels  27.3 us (41%)
  waiting for transfers between devices  6.43 us (10%)
  other arithmetic  0.73 us (1%)
    ppermute x12, starting transfers between devices, shift(): lax.ppermute(value, axis, [(i, (i + step) % count) for i in range(count)])  20.9 us
    pallas_call x1, Pallas kernels, block_fields(): pl.pallas_call(functools.partial(block_kernel, dims), out_shape=jax.Shape...  13.4 us
    pallas_call x1, Pallas kernels, dispatch(): pl.pallas_call(functools.partial(dispatch_kernel, layout), out_shape=[jax...  6.02 us
    pallas_call x2, Pallas kernels, combine_weights(): pl.pallas_call(functools.partial(combine_kernel, [len(parts) for parts in...  4.62 us
    ppermute x1, starting transfers between devices, local(): around = lax.ppermute(around, 'tok', [(3, 2), (0, 1)])  4.61 us
    ppermute x12, waiting for transfers between devices, shift(): lax.ppermute(value, axis, [(i, (i + step) % count) for i in range(count)])  4.11 us
    ppermute x1, starting transfers between devices, local(): first_halo = lax.ppermute(first_halo, 'tok', swap(0))  3.28 us
    pallas_call x1, Pallas kernels, experts(): pl.pallas_call(functools.partial(expert_kernel, count_z, slots_exp), out_...  2.84 us
  transfers between devices with their start and end apart: 18, of which 6 were waited for; matrix products, arithmetic and copies ran while one was open for 1% of the time, Pallas kernels for 21%

profile of v4, /device:TPU:0, one launch (start us, length us, event | category | flops | bytes accessed | tf_op | source)
XLA Modules:
  0.0 66.5 jit_solution(4715443661919618702)
XLA Ops:
  0.5 0.6 pad_add_fusion.index_ref
  1.2 6.0 %dispatch.1 = (bf16[256,1024]{1,0:T(8,128)(2,1)}, bf16[64,1152]{1,0:T(8,128)(2,1)}, bf16[64,1152]{1,0:T(8,128)(2,1)}, bf16[64,1152]{1,0:T(8,128)(2,1)}, bf16[64,1152]{1,0:T(8,128)(2,1)}) custom-call(s32[2]{0:T(128)} %pad_add_fusion.index_ref, bf16[1024,1024]{1,0:T(8,128)(2,1)} %bitcast.12, bf16[1024,256]{1,0:T(8,128)(2,1)} %keys_hbm.1, f32[1,1024]{1,0:T(1,128)} %bitcast.18), custom_call_target="tpu_custom_call" | custom-call | flops 1073741824 | bytes 4194304 | tf_op jit(solution)/shard_map/dispatch/pallas_call | solution.py:105
  7.6 2.9 %collective-permute-start.2 = (bf16[64,1152]{1,0:T(8,128)(2,1)}, bf16[64,1152]{1,0:T(8,128)(2,1)S(1)}, u32[]{:S(2)}, u32[]{:S(2)}) collective-permute-start(bf16[64,1152]{1,0:T(8,128)(2,1)} %get-tuple-element.25), channel_id=1, source_target_pairs={{0,1},{1,2},{2,3},{3,0},{4,5},{5,6},{6,7},{7,4},{8,9},{9,10},{10,1... | collective-permute-start | bytes 442376 | tf_op jit(solution)/shard_map/ppermute | solution.py:491
  10.4 1.5 %collective-permute-start.4 = (bf16[64,1152]{1,0:T(8,128)(2,1)}, bf16[64,1152]{1,0:T(8,128)(2,1)S(1)}, u32[]{:S(2)}, u32[]{:S(2)}) collective-permute-start(bf16[64,1152]{1,0:T(8,128)(2,1)} %get-tuple-element.28), channel_id=1, source_target_pairs={{0,2},{1,3},{2,0},{3,1},{4,6},{5,7},{6,4},{7,5},{8,10},{9,11},{10,... | collective-permute-start | bytes 442376 | tf_op jit(solution)/shard_map/ppermute | solution.py:491
  12.0 1.4 %collective-permute-start.5 = (bf16[64,1152]{1,0:T(8,128)(2,1)}, bf16[64,1152]{1,0:T(8,128)(2,1)S(1)}, u32[]{:S(2)}, u32[]{:S(2)}) collective-permute-start(bf16[64,1152]{1,0:T(8,128)(2,1)} %get-tuple-element.29), channel_id=1, source_target_pairs={{0,3},{1,0},{2,1},{3,2},{4,7},{5,4},{6,5},{7,6},{8,11},{9,8},{10,9... | collective-permute-start | bytes 442376 | tf_op jit(solution)/shard_map/ppermute | solution.py:491
  13.4 2.9 %collective-permute-done.2._.refs_1_ = bf16[64,1152]{1,0:T(8,128)(2,1)S(1)} collective-permute-done((bf16[64,1152]{1,0:T(8,128)(2,1)}, bf16[64,1152]{1,0:T(8,128)(2,1)S(1)}, u32[]{:S(2)}, u32[]{:S(2)}) %collective-permute-start.2) | collective-permute-done | bytes 147488 | tf_op jit(solution)/shard_map/ppermute | solution.py:491
  16.4 1.4 %collective-permute-start.10 = (bf16[384,512]{1,0:T(8,128)(2,1)S(1)}, bf16[384,512]{1,0:T(8,128)(2,1)S(1)}, u32[]{:S(2)}, u32[]{:S(2)}) collective-permute-start(bf16[384,512]{1,0:T(8,128)(2,1)S(1)} %edge_rows.5), channel_id=1, source_target_pairs={{1,3},{2,0},{5,7},{6,4},{9,11},{10,8},{13,15},{14,12},{17,19},{18,... | collective-permute-start | bytes 1179656 | tf_op jit(solution)/shard_map/ppermute | solution.py:515
  17.9 3.3 %collective-permute-start.3 = (bf16[384,1024]{1,0:T(8,128)(2,1)S(1)}, bf16[384,1024]{1,0:T(8,128)(2,1)S(1)}, u32[]{:S(2)}, u32[]{:S(2)}) collective-permute-start(bf16[384,1024]{1,0:T(8,128)(2,1)S(1)} %edge_rows.3), channel_id=1, source_target_pairs={{0,1},{2,3},{1,0},{3,2},{4,5},{6,7},{5,4},{7,6},{8,9},{10,11},{9,8... | collective-permute-start | bytes 2359304 | tf_op jit(solution)/shard_map/ppermute | solution.py:513
  21.5 1.6 %collective-permute-start.6 = (bf16[16,1024]{1,0:T(8,128)(2,1)S(1)}, bf16[16,1024]{1,0:T(8,128)(2,1)S(1)}, u32[]{:S(2)}, u32[]{:S(2)}) collective-permute-start(bf16[16,1024]{1,0:T(8,128)(2,1)S(1)} %get-tuple-element.33), channel_id=1, source_target_pairs={{0,8},{4,12},{8,16},{12,20},{16,24},{20,28},{24,0},{28,4},{1,9},{5... | collective-permute-start | bytes 98312 | tf_op jit(solution)/shard_map/ppermute | solution.py:491
  23.2 2.6 %collective-permute-start.7 = (bf16[16,1024]{1,0:T(8,128)(2,1)S(1)}, bf16[16,1024]{1,0:T(8,128)(2,1)S(1)}, u32[]{:S(2)}, u32[]{:S(2)}) collective-permute-start(bf16[16,1024]{1,0:T(8,128)(2,1)S(1)} %get-tuple-element.34), channel_id=1, source_target_pairs={{0,16},{4,20},{8,24},{12,28},{16,0},{20,4},{24,8},{28,12},{1,17},{... | collective-permute-start | bytes 98312 | tf_op jit(solution)/shard_map/ppermute | solution.py:491
  25.8 1.3 %collective-permute-start.8 = (bf16[16,1024]{1,0:T(8,128)(2,1)S(1)}, bf16[16,1024]{1,0:T(8,128)(2,1)S(1)}, u32[]{:S(2)}, u32[]{:S(2)}) collective-permute-start(bf16[16,1024]{1,0:T(8,128)(2,1)S(1)} %get-tuple-element.35), channel_id=1, source_target_pairs={{0,24},{4,28},{8,0},{12,4},{16,8},{20,12},{24,16},{28,20},{1,25},{... | collective-permute-start | bytes 98312 | tf_op jit(solution)/shard_map/ppermute | solution.py:491
  27.1 2.0 %combine_weights.2._.share_ref = bf16[1024,256]{1,0:T(8,128)(2,1)S(1)} custom-call(s32[1]{0:T(128)} %constant.57.clone.1.valid_ref, bf16[256,1024]{1,0:T(8,128)(2,1)S(1)} %copy-done.3, f32[1,1024]{1,0:T(1,128)S(1)} %bitcast.19, bf16[16,1024]{1,0:T(8,128)(2,1)S(1)} %get-tuple-element.30._.refs_0_, bf16[1024,1024]{1,0:T(8,128)(2,1)S(1)} %bitcast.15), custom_call_target="tpu_custom_call" | custom-call | flops 536870912 | bytes 2097152 | tf_op jit(solution)/shard_map/combine_weights/pallas_call | solution.py:276
  29.1 0.6 collective-permute-done.8.refs_3_
  29.7 2.8 %experts.1 = (bf16[16,1024]{1,0:T(8,128)(2,1)S(1)}, bf16[16,1024]{1,0:T(8,128)(2,1)S(1)}, bf16[16,1024]{1,0:T(8,128)(2,1)S(1)}, bf16[16,1024]{1,0:T(8,128)(2,1)S(1)}) custom-call(s32[1]{0:T(128)} %bitcast.5.core_ref, bf16[1024,256]{1,0:T(8,128)(2,1)S(1)} %combine_weights.2._.share_ref, bf16[2,1024,512]{2,1,0:T(8,128)(2,1)S(1)} %copy-done.1, ...), custom_call_target="tpu_custom_call" | custom-call | flops 536870912 | bytes 8388608 | tf_op jit(solution)/shard_map/experts/pallas_call | solution.py:200
  32.6 3.2 %collective-permute-start.12 = (bf16[16,1024]{1,0:T(8,128)(2,1)S(1)}, bf16[16,1024]{1,0:T(8,128)(2,1)S(1)}, u32[]{:S(2)}, u32[]{:S(2)}) collective-permute-start(bf16[16,1024]{1,0:T(8,128)(2,1)S(1)} %get-tuple-element.40), channel_id=1, source_target_pairs={{0,24},{4,28},{8,0},{12,4},{16,8},{20,12},{24,16},{28,20},{1,25},{... | collective-permute-start | bytes 98312 | tf_op jit(solution)/shard_map/ppermute | solution.py:491
  35.9 0.8 %collective-permute-start.9 = (bf16[384,512]{1,0:T(8,128)(2,1)S(1)}, bf16[384,512]{1,0:T(8,128)(2,1)S(1)}, u32[]{:S(2)}, u32[]{:S(2)}) collective-permute-start(bf16[384,512]{1,0:T(8,128)(2,1)S(1)} %edge_rows.4), channel_id=1, source_target_pairs={{1,2},{2,1},{5,6},{6,5},{9,10},{10,9},{13,14},{14,13},{17,18},{18,... | collective-permute-start | bytes 1179656 | tf_op jit(solution)/shard_map/ppermute | solution.py:527
  36.8 0.6 collective-permute-start.14
  37.4 4.6 %collective-permute-start.11 = (bf16[384,512]{1,0:T(8,128)(2,1)S(1)}, bf16[384,512]{1,0:T(8,128)(2,1)S(1)}, u32[]{:S(2)}, u32[]{:S(2)}) collective-permute-start(bf16[384,512]{1,0:T(8,128)(2,1)S(1)} %after.1), channel_id=1, source_target_pairs={{3,2},{0,1},{7,6},{4,5},{11,10},{8,9},{15,14},{12,13},{19,18},{16,... | collective-permute-start | bytes 1179656 | tf_op jit(solution)/shard_map/ppermute | solution.py:521
  42.0 0.5 collective-permute-done.14
  42.6 2.7 %collective-permute-start.17 = (bf16[64,1024]{1,0:T(8,128)(2,1)S(1)}, bf16[64,1024]{1,0:T(8,128)(2,1)S(1)}, u32[]{:S(2)}, u32[]{:S(2)}) collective-permute-start(bf16[64,1024]{1,0:T(8,128)(2,1)S(1)} %constant_dynamic-update-slice_fusion.rest_0_), channel_id=1, source_target_pairs={{0,1},{1,2},{2,3},{3,0},{4,5},{5,6},{6,7},{7,4},{8,9},{9,10},{10,1... | collective-permute-start | bytes 393224 | tf_op jit(solution)/shard_map/ppermute | solution.py:491
  45.3 2.9 %collective-permute-start.15 = (bf16[64,1024]{1,0:T(8,128)(2,1)S(1)}, bf16[64,1024]{1,0:T(8,128)(2,1)S(1)}, u32[]{:S(2)}, u32[]{:S(2)}) collective-permute-start(bf16[64,1024]{1,0:T(8,128)(2,1)S(1)} %constant_dynamic-update-slice_fusion.rest_0_), channel_id=1, source_target_pairs={{0,3},{1,0},{2,1},{3,2},{4,7},{5,4},{6,5},{7,6},{8,11},{9,8},{10,9... | collective-permute-start | bytes 393224 | tf_op jit(solution)/shard_map/ppermute | solution.py:491
  48.3 1.9 %collective-permute-done.11.refs_2_.second_b = bf16[384,512]{1,0:T(8,128)(2,1)S(1)} collective-permute-done((bf16[384,512]{1,0:T(8,128)(2,1)S(1)}, bf16[384,512]{1,0:T(8,128)(2,1)S(1)}, u32[]{:S(2)}, u32[]{:S(2)}) %collective-permute-start.11) | collective-permute-done | bytes 393248 | tf_op jit(solution)/shard_map/ppermute | solution.py:521
  50.2 2.6 %combine_weights.3 = (bf16[384,256]{1,0:T(8,128)(2,1)S(1)}, bf16[384,256]{1,0:T(8,128)(2,1)S(1)}, f32[7,192,1024]{2,1,0:T(8,128)S(1)}) custom-call(s32[2]{0:T(128)S(1)} %add_convert_fusion.valid_ref, bf16[256,1024]{1,0:T(8,128)(2,1)S(1)} %copy-done.3, f32[1,1024]{1,0:T(1,128)S(1)} %bitcast.20, bf16[16,1024]{1,0:T(8,128)(2,1)S(1)} %get-tuple-element.36._, ...), custom_call_target="tpu_custom_call" | custom-call | flops 402653184 | bytes 1572864 | tf_op jit(solution)/shard_map/combine_weights/pallas_call | solution.py:276
  53.0 13.4 %block_fields.1 = bf16[1024,1024]{1,0:T(8,128)(2,1)} custom-call(s32[2]{0:T(128)S(1)} %broadcast_select_fusion.place_ref, bf16[1024,1024]{1,0:T(8,128)(2,1)S(1)} %bitcast.17, bf16[384,1024]{1,0:T(8,128)(2,1)S(1)} %collective-permute-done.3.refs_0_.first_ref, bf16[384,512]{1,0:T(8,128)(2,1)S(1)} %collective-permute-done.9.refs_1_.second_a, ...), custom_call_target="tpu_custom_call" | custom-call | flops 6442450944 | bytes 8388608 | tf_op jit(solution)/shard_map/block_fields/pallas_call | solution.py:453
  (61 shorter events, 1.8 us)
Async XLA Ops:
  0.0 7.2 %collective-permute-start = (bf16[2,1024,512]{2,1,0:T(8,128)(2,1)}, bf16[2,1024,512]{2,1,0:T(8,128)(2,1)}, u32[]{:S(2)}, u32[]{:S(2)}) collective-permute-start(bf16[2,1024,512]{2,1,0:T(8,128)(2,1)} %in_own.1), channel_id=1, source_target_pairs={{0,4},{4,0},{8,12},{12,8},{16,20},{20,16},{24,28},{28,24},{1,5},{5... | collective-permute-start | bytes 6291464 | tf_op jit(solution)/shard_map/ppermute | solution.py:504
  0.5 7.1 %collective-permute-start.1 = (bf16[2,512,1024]{2,1,0:T(8,128)(2,1)}, bf16[2,512,1024]{2,1,0:T(8,128)(2,1)}, u32[]{:S(2)}, u32[]{:S(2)}) collective-permute-start(bf16[2,512,1024]{2,1,0:T(8,128)(2,1)} %out_own.1), channel_id=1, source_target_pairs={{0,4},{4,0},{8,12},{12,8},{16,20},{20,16},{24,28},{28,24},{1,5},{5... | collective-permute-start | bytes 6291464 | tf_op jit(solution)/shard_map/ppermute | solution.py:505
  7.6 8.7 %collective-permute-start.2 = (bf16[64,1152]{1,0:T(8,128)(2,1)}, bf16[64,1152]{1,0:T(8,128)(2,1)S(1)}, u32[]{:S(2)}, u32[]{:S(2)}) collective-permute-start(bf16[64,1152]{1,0:T(8,128)(2,1)} %get-tuple-element.25), channel_id=1, source_target_pairs={{0,1},{1,2},{2,3},{3,0},{4,5},{5,6},{6,7},{7,4},{8,9},{9,10},{10,1... | collective-permute-start | bytes 442376 | tf_op jit(solution)/shard_map/ppermute | solution.py:491
  10.4 10.7 %collective-permute-start.4 = (bf16[64,1152]{1,0:T(8,128)(2,1)}, bf16[64,1152]{1,0:T(8,128)(2,1)S(1)}, u32[]{:S(2)}, u32[]{:S(2)}) collective-permute-start(bf16[64,1152]{1,0:T(8,128)(2,1)} %get-tuple-element.28), channel_id=1, source_target_pairs={{0,2},{1,3},{2,0},{3,1},{4,6},{5,7},{6,4},{7,5},{8,10},{9,11},{10,... | collective-permute-start | bytes 442376 | tf_op jit(solution)/shard_map/ppermute | solution.py:491
  12.0 9.2 %collective-permute-start.5 = (bf16[64,1152]{1,0:T(8,128)(2,1)}, bf16[64,1152]{1,0:T(8,128)(2,1)S(1)}, u32[]{:S(2)}, u32[]{:S(2)}) collective-permute-start(bf16[64,1152]{1,0:T(8,128)(2,1)} %get-tuple-element.29), channel_id=1, source_target_pairs={{0,3},{1,0},{2,1},{3,2},{4,7},{5,4},{6,5},{7,6},{8,11},{9,8},{10,9... | collective-permute-start | bytes 442376 | tf_op jit(solution)/shard_map/ppermute | solution.py:491
  16.4 20.4 %collective-permute-start.10 = (bf16[384,512]{1,0:T(8,128)(2,1)S(1)}, bf16[384,512]{1,0:T(8,128)(2,1)S(1)}, u32[]{:S(2)}, u32[]{:S(2)}) collective-permute-start(bf16[384,512]{1,0:T(8,128)(2,1)S(1)} %edge_rows.5), channel_id=1, source_target_pairs={{1,3},{2,0},{5,7},{6,4},{9,11},{10,8},{13,15},{14,12},{17,19},{18,... | collective-permute-start | bytes 1179656 | tf_op jit(solution)/shard_map/ppermute | solution.py:515
  17.9 32.3 %collective-permute-start.3 = (bf16[384,1024]{1,0:T(8,128)(2,1)S(1)}, bf16[384,1024]{1,0:T(8,128)(2,1)S(1)}, u32[]{:S(2)}, u32[]{:S(2)}) collective-permute-start(bf16[384,1024]{1,0:T(8,128)(2,1)S(1)} %edge_rows.3), channel_id=1, source_target_pairs={{0,1},{2,3},{1,0},{3,2},{4,5},{6,7},{5,4},{7,6},{8,9},{10,11},{9,8... | collective-permute-start | bytes 2359304 | tf_op jit(solution)/shard_map/ppermute | solution.py:513
  21.5 7.6 %collective-permute-start.6 = (bf16[16,1024]{1,0:T(8,128)(2,1)S(1)}, bf16[16,1024]{1,0:T(8,128)(2,1)S(1)}, u32[]{:S(2)}, u32[]{:S(2)}) collective-permute-start(bf16[16,1024]{1,0:T(8,128)(2,1)S(1)} %get-tuple-element.33), channel_id=1, source_target_pairs={{0,8},{4,12},{8,16},{12,20},{16,24},{20,28},{24,0},{28,4},{1,9},{5... | collective-permute-start | bytes 98312 | tf_op jit(solution)/shard_map/ppermute | solution.py:491
  23.2 5.9 %collective-permute-start.7 = (bf16[16,1024]{1,0:T(8,128)(2,1)S(1)}, bf16[16,1024]{1,0:T(8,128)(2,1)S(1)}, u32[]{:S(2)}, u32[]{:S(2)}) collective-permute-start(bf16[16,1024]{1,0:T(8,128)(2,1)S(1)} %get-tuple-element.34), channel_id=1, source_target_pairs={{0,16},{4,20},{8,24},{12,28},{16,0},{20,4},{24,8},{28,12},{1,17},{... | collective-permute-start | bytes 98312 | tf_op jit(solution)/shard_map/ppermute | solution.py:491
  25.8 3.9 %collective-permute-start.8 = (bf16[16,1024]{1,0:T(8,128)(2,1)S(1)}, bf16[16,1024]{1,0:T(8,128)(2,1)S(1)}, u32[]{:S(2)}, u32[]{:S(2)}) collective-permute-start(bf16[16,1024]{1,0:T(8,128)(2,1)S(1)} %get-tuple-element.35), channel_id=1, source_target_pairs={{0,24},{4,28},{8,0},{12,4},{16,8},{20,12},{24,16},{28,20},{1,25},{... | collective-permute-start | bytes 98312 | tf_op jit(solution)/shard_map/ppermute | solution.py:491
  32.5 17.7 %copy-start.4 = (f32[7,7,1024]{2,1,0:T(8,128)S(1)}, f32[7,7,1024]{2,1,0:T(8,128)}, u32[]{:S(2)}) copy-start(f32[7,7,1024]{2,1,0:T(8,128)} %refs_4_.1) | copy-start | bytes 602116
  32.5 17.7 %copy-start.6 = (bf16[192,40]{1,0:T(8,128)(2,1)S(1)}, bf16[192,40]{1,0:T(8,128)(2,1)}, u32[]{:S(2)}) copy-start(bf16[192,40]{1,0:T(8,128)(2,1)} %constant.59.clone.refs_3_) | copy-start | bytes 46084
  32.6 4.8 %collective-permute-start.12 = (bf16[16,1024]{1,0:T(8,128)(2,1)S(1)}, bf16[16,1024]{1,0:T(8,128)(2,1)S(1)}, u32[]{:S(2)}, u32[]{:S(2)}) collective-permute-start(bf16[16,1024]{1,0:T(8,128)(2,1)S(1)} %get-tuple-element.40), channel_id=1, source_target_pairs={{0,24},{4,28},{8,0},{12,4},{16,8},{20,12},{24,16},{28,20},{1,25},{... | collective-permute-start | bytes 98312 | tf_op jit(solution)/shard_map/ppermute | solution.py:491
  35.8 17.2 %copy-start.9 = (bf16[1024,1024]{1,0:T(8,128)(2,1)S(1)}, bf16[1024,1024]{1,0:T(8,128)(2,1)}, u32[]{:S(2)}) copy-start(bf16[1024,1024]{1,0:T(8,128)(2,1)} %proj_ref.1) | copy-start | bytes 6291460
  35.8 17.2 %copy-start.10 = (f32[1024]{0:T(1024)S(1)}, f32[1024]{0:T(1024)}, u32[]{:S(2)}) copy-start(f32[1024]{0:T(1024)} %param.23) | copy-start | bytes 12292
  35.8 17.2 %copy-start.11 = (f32[1024]{0:T(1024)S(1)}, f32[1024]{0:T(1024)}, u32[]{:S(2)}) copy-start(f32[1024]{0:T(1024)} %param.25) | copy-start | bytes 12292
  35.8 17.2 %copy-start.12 = (bf16[128,256]{1,0:T(8,128)(2,1)S(1)}, bf16[128,256]{1,0:T(8,128)(2,1)}, u32[]{:S(2)}) copy-start(bf16[128,256]{1,0:T(8,128)(2,1)} %constant.63.clone.cols_ref) | copy-start | bytes 196612
  35.9 9.4 %collective-permute-start.9 = (bf16[384,512]{1,0:T(8,128)(2,1)S(1)}, bf16[384,512]{1,0:T(8,128)(2,1)S(1)}, u32[]{:S(2)}, u32[]{:S(2)}) collective-permute-start(bf16[384,512]{1,0:T(8,128)(2,1)S(1)} %edge_rows.4), channel_id=1, source_target_pairs={{1,2},{2,1},{5,6},{6,5},{9,10},{10,9},{13,14},{14,13},{17,18},{18,... | collective-permute-start | bytes 1179656 | tf_op jit(solution)/shard_map/ppermute | solution.py:527
  36.7 5.3 %collective-permute-start.13 = (bf16[16,1024]{1,0:T(8,128)(2,1)S(1)}, bf16[16,1024]{1,0:T(8,128)(2,1)S(1)}, u32[]{:S(2)}, u32[]{:S(2)}) collective-permute-start(bf16[16,1024]{1,0:T(8,128)(2,1)S(1)} %get-tuple-element.41), channel_id=1, source_target_pairs={{0,16},{4,20},{8,24},{12,28},{16,0},{20,4},{24,8},{28,12},{1,17},{... | collective-permute-start | bytes 98312 | tf_op jit(solution)/shard_map/ppermute | solution.py:491
  36.8 5.8 %collective-permute-start.14 = (bf16[16,1024]{1,0:T(8,128)(2,1)S(1)}, bf16[16,1024]{1,0:T(8,128)(2,1)S(1)}, u32[]{:S(2)}, u32[]{:S(2)}) collective-permute-start(bf16[16,1024]{1,0:T(8,128)(2,1)S(1)} %get-tuple-element.42), channel_id=1, source_target_pairs={{0,8},{4,12},{8,16},{12,20},{16,24},{20,28},{24,0},{28,4},{1,9},{5... | collective-permute-start | bytes 98312 | tf_op jit(solution)/shard_map/ppermute | solution.py:491
  37.4 12.8 %collective-permute-start.11 = (bf16[384,512]{1,0:T(8,128)(2,1)S(1)}, bf16[384,512]{1,0:T(8,128)(2,1)S(1)}, u32[]{:S(2)}, u32[]{:S(2)}) collective-permute-start(bf16[384,512]{1,0:T(8,128)(2,1)S(1)} %after.1), channel_id=1, source_target_pairs={{3,2},{0,1},{7,6},{4,5},{11,10},{8,9},{15,14},{12,13},{19,18},{16,... | collective-permute-start | bytes 1179656 | tf_op jit(solution)/shard_map/ppermute | solution.py:521
  42.6 10.3 %collective-permute-start.17 = (bf16[64,1024]{1,0:T(8,128)(2,1)S(1)}, bf16[64,1024]{1,0:T(8,128)(2,1)S(1)}, u32[]{:S(2)}, u32[]{:S(2)}) collective-permute-start(bf16[64,1024]{1,0:T(8,128)(2,1)S(1)} %constant_dynamic-update-slice_fusion.rest_0_), channel_id=1, source_target_pairs={{0,1},{1,2},{2,3},{3,0},{4,5},{5,6},{6,7},{7,4},{8,9},{9,10},{10,1... | collective-permute-start | bytes 393224 | tf_op jit(solution)/shard_map/ppermute | solution.py:491
  45.2 7.7 %collective-permute-start.16 = (bf16[64,1024]{1,0:T(8,128)(2,1)S(1)}, bf16[64,1024]{1,0:T(8,128)(2,1)S(1)}, u32[]{:S(2)}, u32[]{:S(2)}) collective-permute-start(bf16[64,1024]{1,0:T(8,128)(2,1)S(1)} %constant_dynamic-update-slice_fusion.rest_0_), channel_id=1, source_target_pairs={{0,2},{1,3},{2,0},{3,1},{4,6},{5,7},{6,4},{7,5},{8,10},{9,11},{10,... | collective-permute-start | bytes 393224 | tf_op jit(solution)/shard_map/ppermute | solution.py:491
  45.3 7.7 %collective-permute-start.15 = (bf16[64,1024]{1,0:T(8,128)(2,1)S(1)}, bf16[64,1024]{1,0:T(8,128)(2,1)S(1)}, u32[]{:S(2)}, u32[]{:S(2)}) collective-permute-start(bf16[64,1024]{1,0:T(8,128)(2,1)S(1)} %constant_dynamic-update-slice_fusion.rest_0_), channel_id=1, source_target_pairs={{0,3},{1,0},{2,1},{3,2},{4,7},{5,4},{6,5},{7,6},{8,11},{9,8},{10,9... | collective-permute-start | bytes 393224 | tf_op jit(solution)/shard_map/ppermute | solution.py:491
  (10 other events, 110.5 us)

commit v5 on v4

--- a/solution.py
+++ b/solution.py
@@ -521,10 +521,10 @@
         around = lax.ppermute(around, "tok", [(3, 2), (0, 1)])
     always = jnp.ones((1,), jnp.int32)
     (share,) = combine_weights(always, [[cells]], keys, norm_gain, seen)
+    direct = edge_rows(place, cells, reach * cols, 0, half, share)
+    direct = lax.ppermute(direct, "tok", swap(1))
     core = (at_fc % 2).astype(jnp.int32).reshape(1)
     made = experts(core, share, arrived, w_in, w_out, in_other, out_other, slots_exp)
-    direct = edge_rows(place, cells, reach * cols, 0, half, made[0])
-    direct = lax.ppermute(direct, "tok", swap(1))
     back = [made[0]] + [shift(made[k], "fc", -2 * k) for k in range(1, count_z)]
     mine = jnp.concatenate(back, axis=0)
     above, below = at_tok > 0, at_tok < count_tok - 1

time: 67.2 us -> 66.8 us (level)
  starting transfers between devices: 31.5 us -> 29.2 us
  waiting for transfers between devices: 6.43 us -> 8.26 us
    ppermute x1, waiting for transfers between devices: 1.93 us -> 3.73 us  [local(): around = lax.ppermute(around, 'tok', [(3, 2), (0, 1)])]
    ppermute x12, starting transfers between devices: 20.9 us -> 19.2 us  [shift(): lax.ppermute(value, axis, [(i, (i + step) % count) for i in range(count)])]
  transfers between devices with their start and end apart: 18 -> 18, of which waited for: 6 -> 5; matrix products, arithmetic and copies ran while one was open for 1% -> 1% of each run, Pallas kernels for 21% -> 21%
where the time goes in v5:
time: 66.8 us; the launch traced here: 66.6 us
  starting transfers between devices  29.2 us (44%)
  Pallas kernels  27.3 us (41%)
  waiting for transfers between devices  8.26 us (12%)
  local copies, waits for them, and re-layouts  0.78 us (1%)
  other arithmetic  0.73 us (1%)
    ppermute x12, starting transfers between devices, shift(): lax.ppermute(value, axis, [(i, (i + step) % count) for i in range(count)])  19.2 us
    pallas_call x1, Pallas kernels, block_fields(): pl.pallas_call(functools.partial(block_kernel, dims), out_shape=jax.Shape...  13.4 us
    pallas_call x1, Pallas kernels, dispatch(): pl.pallas_call(functools.partial(dispatch_kernel, layout), out_shape=[jax...  6.02 us
    pallas_call x2, Pallas kernels, combine_weights(): pl.pallas_call(functools.partial(combine_kernel, [len(parts) for parts in...  4.61 us
    ppermute x12, waiting for transfers between devices, shift(): lax.ppermute(value, axis, [(i, (i + step) % count) for i in range(count)])  4.14 us
    ppermute x1, starting transfers between devices, local(): around = lax.ppermute(around, 'tok', [(3, 2), (0, 1)])  3.96 us
    ppermute x1, waiting for transfers between devices, local(): around = lax.ppermute(around, 'tok', [(3, 2), (0, 1)])  3.73 us
    ppermute x1, starting transfers between devices, local(): first_halo = lax.ppermute(first_halo, 'tok', swap(0))  3.28 us
  transfers between devices with their start and end apart: 18, of which 5 were waited for; matrix products, arithmetic and copies ran while one was open for 1% of the time, Pallas kernels for 21%

profile of v5, /device:TPU:0, one launch (start us, length us, event | category | flops | bytes accessed | tf_op | source)
XLA Modules:
  0.0 66.6 jit_solution(15793487541885431069)
XLA Ops:
  0.5 0.6 pad_add_fusion.index_ref
  1.2 6.0 %dispatch.1 = (bf16[256,1024]{1,0:T(8,128)(2,1)}, bf16[64,1152]{1,0:T(8,128)(2,1)}, bf16[64,1152]{1,0:T(8,128)(2,1)}, bf16[64,1152]{1,0:T(8,128)(2,1)}, bf16[64,1152]{1,0:T(8,128)(2,1)}) custom-call(s32[2]{0:T(128)} %pad_add_fusion.index_ref, bf16[1024,1024]{1,0:T(8,128)(2,1)} %bitcast.12, bf16[1024,256]{1,0:T(8,128)(2,1)} %keys_hbm.1, f32[1,1024]{1,0:T(1,128)} %bitcast.18), custom_call_target="tpu_custom_call" | custom-call | flops 1073741824 | bytes 4194304 | tf_op jit(solution)/shard_map/dispatch/pallas_call | solution.py:105
  7.6 2.9 %collective-permute-start.2 = (bf16[64,1152]{1,0:T(8,128)(2,1)}, bf16[64,1152]{1,0:T(8,128)(2,1)S(1)}, u32[]{:S(2)}, u32[]{:S(2)}) collective-permute-start(bf16[64,1152]{1,0:T(8,128)(2,1)} %get-tuple-element.25), channel_id=1, source_target_pairs={{0,1},{1,2},{2,3},{3,0},{4,5},{5,6},{6,7},{7,4},{8,9},{9,10},{10,1... | collective-permute-start | bytes 442376 | tf_op jit(solution)/shard_map/ppermute | solution.py:491
  10.4 1.5 %collective-permute-start.4 = (bf16[64,1152]{1,0:T(8,128)(2,1)}, bf16[64,1152]{1,0:T(8,128)(2,1)S(1)}, u32[]{:S(2)}, u32[]{:S(2)}) collective-permute-start(bf16[64,1152]{1,0:T(8,128)(2,1)} %get-tuple-element.28), channel_id=1, source_target_pairs={{0,2},{1,3},{2,0},{3,1},{4,6},{5,7},{6,4},{7,5},{8,10},{9,11},{10,... | collective-permute-start | bytes 442376 | tf_op jit(solution)/shard_map/ppermute | solution.py:491
  12.0 1.4 %collective-permute-start.5 = (bf16[64,1152]{1,0:T(8,128)(2,1)}, bf16[64,1152]{1,0:T(8,128)(2,1)S(1)}, u32[]{:S(2)}, u32[]{:S(2)}) collective-permute-start(bf16[64,1152]{1,0:T(8,128)(2,1)} %get-tuple-element.29), channel_id=1, source_target_pairs={{0,3},{1,0},{2,1},{3,2},{4,7},{5,4},{6,5},{7,6},{8,11},{9,8},{10,9... | collective-permute-start | bytes 442376 | tf_op jit(solution)/shard_map/ppermute | solution.py:491
  13.4 2.9 %collective-permute-done.2._.refs_1_ = bf16[64,1152]{1,0:T(8,128)(2,1)S(1)} collective-permute-done((bf16[64,1152]{1,0:T(8,128)(2,1)}, bf16[64,1152]{1,0:T(8,128)(2,1)S(1)}, u32[]{:S(2)}, u32[]{:S(2)}) %collective-permute-start.2) | collective-permute-done | bytes 147488 | tf_op jit(solution)/shard_map/ppermute | solution.py:491
  16.4 1.4 %collective-permute-start.7 = (bf16[384,512]{1,0:T(8,128)(2,1)S(1)}, bf16[384,512]{1,0:T(8,128)(2,1)S(1)}, u32[]{:S(2)}, u32[]{:S(2)}) collective-permute-start(bf16[384,512]{1,0:T(8,128)(2,1)S(1)} %edge_rows.5), channel_id=1, source_target_pairs={{1,3},{2,0},{5,7},{6,4},{9,11},{10,8},{13,15},{14,12},{17,19},{18,... | collective-permute-start | bytes 1179656 | tf_op jit(solution)/shard_map/ppermute | solution.py:515
  17.9 3.3 %collective-permute-start.3 = (bf16[384,1024]{1,0:T(8,128)(2,1)S(1)}, bf16[384,1024]{1,0:T(8,128)(2,1)S(1)}, u32[]{:S(2)}, u32[]{:S(2)}) collective-permute-start(bf16[384,1024]{1,0:T(8,128)(2,1)S(1)} %edge_rows.3), channel_id=1, source_target_pairs={{0,1},{2,3},{1,0},{3,2},{4,5},{6,7},{5,4},{7,6},{8,9},{10,11},{9,8... | collective-permute-start | bytes 2359304 | tf_op jit(solution)/shard_map/ppermute | solution.py:513
  21.5 1.6 %collective-permute-start.9 = (bf16[16,1024]{1,0:T(8,128)(2,1)S(1)}, bf16[16,1024]{1,0:T(8,128)(2,1)S(1)}, u32[]{:S(2)}, u32[]{:S(2)}) collective-permute-start(bf16[16,1024]{1,0:T(8,128)(2,1)S(1)} %get-tuple-element.33), channel_id=1, source_target_pairs={{0,8},{4,12},{8,16},{12,20},{16,24},{20,28},{24,0},{28,4},{1,9},{5... | collective-permute-start | bytes 98312 | tf_op jit(solution)/shard_map/ppermute | solution.py:491
  23.2 2.6 %collective-permute-start.10 = (bf16[16,1024]{1,0:T(8,128)(2,1)S(1)}, bf16[16,1024]{1,0:T(8,128)(2,1)S(1)}, u32[]{:S(2)}, u32[]{:S(2)}) collective-permute-start(bf16[16,1024]{1,0:T(8,128)(2,1)S(1)} %get-tuple-element.34), channel_id=1, source_target_pairs={{0,16},{4,20},{8,24},{12,28},{16,0},{20,4},{24,8},{28,12},{1,17},{... | collective-permute-start | bytes 98312 | tf_op jit(solution)/shard_map/ppermute | solution.py:491
  25.7 1.3 %collective-permute-start.11 = (bf16[16,1024]{1,0:T(8,128)(2,1)S(1)}, bf16[16,1024]{1,0:T(8,128)(2,1)S(1)}, u32[]{:S(2)}, u32[]{:S(2)}) collective-permute-start(bf16[16,1024]{1,0:T(8,128)(2,1)S(1)} %get-tuple-element.35), channel_id=1, source_target_pairs={{0,24},{4,28},{8,0},{12,4},{16,8},{20,12},{24,16},{28,20},{1,25},{... | collective-permute-start | bytes 98312 | tf_op jit(solution)/shard_map/ppermute | solution.py:491
  27.1 2.0 %combine_weights.2._.share_ref = bf16[1024,256]{1,0:T(8,128)(2,1)S(1)} custom-call(s32[1]{0:T(128)} %constant.57.clone.1.valid_ref, bf16[256,1024]{1,0:T(8,128)(2,1)S(1)} %copy-done.3, f32[1,1024]{1,0:T(1,128)S(1)} %bitcast.19, bf16[16,1024]{1,0:T(8,128)(2,1)S(1)} %get-tuple-element.30._.refs_0_, bf16[1024,1024]{1,0:T(8,128)(2,1)S(1)} %bitcast.15), custom_call_target="tpu_custom_call" | custom-call | flops 536870912 | bytes 2097152 | tf_op jit(solution)/shard_map/combine_weights/pallas_call | solution.py:276
  29.1 0.8 %collective-permute-start.6 = (bf16[384,512]{1,0:T(8,128)(2,1)S(1)}, bf16[384,512]{1,0:T(8,128)(2,1)S(1)}, u32[]{:S(2)}, u32[]{:S(2)}) collective-permute-start(bf16[384,512]{1,0:T(8,128)(2,1)S(1)} %edge_rows.4), channel_id=1, source_target_pairs={{1,2},{2,1},{5,6},{6,5},{9,10},{10,9},{13,14},{14,13},{17,18},{18,... | collective-permute-start | bytes 1179656 | tf_op jit(solution)/shard_map/ppermute | solution.py:525
  30.0 0.7 %copy-done.1 = bf16[2,1024,512]{2,1,0:T(8,128)(2,1)S(1)} copy-done((bf16[2,1024,512]{2,1,0:T(8,128)(2,1)S(1)}, bf16[2,1024,512]{2,1,0:T(8,128)(2,1)}, u32[]{:S(2)}) %copy-start.1) | copy-done | bytes 2097176
  30.7 2.8 %experts.1 = (bf16[16,1024]{1,0:T(8,128)(2,1)S(1)}, bf16[16,1024]{1,0:T(8,128)(2,1)S(1)}, bf16[16,1024]{1,0:T(8,128)(2,1)S(1)}, bf16[16,1024]{1,0:T(8,128)(2,1)S(1)}) custom-call(s32[1]{0:T(128)} %bitcast.8.core_ref, bf16[1024,256]{1,0:T(8,128)(2,1)S(1)} %combine_weights.2._.share_ref, bf16[2,1024,512]{2,1,0:T(8,128)(2,1)S(1)} %copy-done.1, ...), custom_call_target="tpu_custom_call" | custom-call | flops 536870912 | bytes 8388608 | tf_op jit(solution)/shard_map/experts/pallas_call | solution.py:200
  33.6 2.2 %collective-permute-start.12 = (bf16[16,1024]{1,0:T(8,128)(2,1)S(1)}, bf16[16,1024]{1,0:T(8,128)(2,1)S(1)}, u32[]{:S(2)}, u32[]{:S(2)}) collective-permute-start(bf16[16,1024]{1,0:T(8,128)(2,1)S(1)} %get-tuple-element.40), channel_id=1, source_target_pairs={{0,24},{4,28},{8,0},{12,4},{16,8},{20,12},{24,16},{28,20},{1,25},{... | collective-permute-start | bytes 98312 | tf_op jit(solution)/shard_map/ppermute | solution.py:491
  35.8 0.6 collective-permute-start.14
  36.5 1.1 %collective-permute-done.12 = bf16[16,1024]{1,0:T(8,128)(2,1)S(1)} collective-permute-done((bf16[16,1024]{1,0:T(8,128)(2,1)S(1)}, bf16[16,1024]{1,0:T(8,128)(2,1)S(1)}, u32[]{:S(2)}, u32[]{:S(2)}) %collective-permute-start.12) | collective-permute-done | bytes 32800 | tf_op jit(solution)/shard_map/ppermute | solution.py:491
  37.6 4.0 %collective-permute-start.8 = (bf16[384,512]{1,0:T(8,128)(2,1)S(1)}, bf16[384,512]{1,0:T(8,128)(2,1)S(1)}, u32[]{:S(2)}, u32[]{:S(2)}) collective-permute-start(bf16[384,512]{1,0:T(8,128)(2,1)S(1)} %after.1), channel_id=1, source_target_pairs={{3,2},{0,1},{7,6},{4,5},{11,10},{8,9},{15,14},{12,13},{19,18},{16,... | collective-permute-start | bytes 1179656 | tf_op jit(solution)/shard_map/ppermute | solution.py:521
  41.6 2.0 %collective-permute-start.17 = (bf16[64,1024]{1,0:T(8,128)(2,1)S(1)}, bf16[64,1024]{1,0:T(8,128)(2,1)S(1)}, u32[]{:S(2)}, u32[]{:S(2)}) collective-permute-start(bf16[64,1024]{1,0:T(8,128)(2,1)S(1)} %constant_dynamic-update-slice_fusion.rest_0_), channel_id=1, source_target_pairs={{0,1},{1,2},{2,3},{3,0},{4,5},{5,6},{6,7},{7,4},{8,9},{9,10},{10,1... | collective-permute-start | bytes 393224 | tf_op jit(solution)/shard_map/ppermute | solution.py:491
  44.1 2.5 %collective-permute-start.15 = (bf16[64,1024]{1,0:T(8,128)(2,1)S(1)}, bf16[64,1024]{1,0:T(8,128)(2,1)S(1)}, u32[]{:S(2)}, u32[]{:S(2)}) collective-permute-start(bf16[64,1024]{1,0:T(8,128)(2,1)S(1)} %constant_dynamic-update-slice_fusion.rest_0_), channel_id=1, source_target_pairs={{0,3},{1,0},{2,1},{3,2},{4,7},{5,4},{6,5},{7,6},{8,11},{9,8},{10,9... | collective-permute-start | bytes 393224 | tf_op jit(solution)/shard_map/ppermute | solution.py:491
  46.6 3.7 %collective-permute-done.8.refs_2_.second_b = bf16[384,512]{1,0:T(8,128)(2,1)S(1)} collective-permute-done((bf16[384,512]{1,0:T(8,128)(2,1)S(1)}, bf16[384,512]{1,0:T(8,128)(2,1)S(1)}, u32[]{:S(2)}, u32[]{:S(2)}) %collective-permute-start.8) | collective-permute-done | bytes 393248 | tf_op jit(solution)/shard_map/ppermute | solution.py:521
  50.3 2.6 %combine_weights.3 = (bf16[384,256]{1,0:T(8,128)(2,1)S(1)}, bf16[384,256]{1,0:T(8,128)(2,1)S(1)}, f32[7,192,1024]{2,1,0:T(8,128)S(1)}) custom-call(s32[2]{0:T(128)S(1)} %add_convert_fusion.valid_ref, bf16[256,1024]{1,0:T(8,128)(2,1)S(1)} %copy-done.3, f32[1,1024]{1,0:T(1,128)S(1)} %bitcast.20, bf16[16,1024]{1,0:T(8,128)(2,1)S(1)} %get-tuple-element.36._, ...), custom_call_target="tpu_custom_call" | custom-call | flops 402653184 | bytes 1572864 | tf_op jit(solution)/shard_map/combine_weights/pallas_call | solution.py:276
  53.2 13.4 %block_fields.1 = bf16[1024,1024]{1,0:T(8,128)(2,1)} custom-call(s32[2]{0:T(128)S(1)} %broadcast_select_fusion.place_ref, bf16[1024,1024]{1,0:T(8,128)(2,1)S(1)} %bitcast.17, bf16[384,1024]{1,0:T(8,128)(2,1)S(1)} %collective-permute-done.3.refs_0_.first_ref, bf16[384,512]{1,0:T(8,128)(2,1)S(1)} %collective-permute-done.6.refs_1_.second_a, ...), custom_call_target="tpu_custom_call" | custom-call | flops 6442450944 | bytes 8388608 | tf_op jit(solution)/shard_map/block_fields/pallas_call | solution.py:453
  (61 shorter events, 2.2 us)
Async XLA Ops:
  0.0 7.2 %collective-permute-start = (bf16[2,1024,512]{2,1,0:T(8,128)(2,1)}, bf16[2,1024,512]{2,1,0:T(8,128)(2,1)}, u32[]{:S(2)}, u32[]{:S(2)}) collective-permute-start(bf16[2,1024,512]{2,1,0:T(8,128)(2,1)} %in_own.1), channel_id=1, source_target_pairs={{0,4},{4,0},{8,12},{12,8},{16,20},{20,16},{24,28},{28,24},{1,5},{5... | collective-permute-start | bytes 6291464 | tf_op jit(solution)/shard_map/ppermute | solution.py:504
  0.5 7.1 %collective-permute-start.1 = (bf16[2,512,1024]{2,1,0:T(8,128)(2,1)}, bf16[2,512,1024]{2,1,0:T(8,128)(2,1)}, u32[]{:S(2)}, u32[]{:S(2)}) collective-permute-start(bf16[2,512,1024]{2,1,0:T(8,128)(2,1)} %out_own.1), channel_id=1, source_target_pairs={{0,4},{4,0},{8,12},{12,8},{16,20},{20,16},{24,28},{28,24},{1,5},{5... | collective-permute-start | bytes 6291464 | tf_op jit(solution)/shard_map/ppermute | solution.py:505
  7.6 8.7 %collective-permute-start.2 = (bf16[64,1152]{1,0:T(8,128)(2,1)}, bf16[64,1152]{1,0:T(8,128)(2,1)S(1)}, u32[]{:S(2)}, u32[]{:S(2)}) collective-permute-start(bf16[64,1152]{1,0:T(8,128)(2,1)} %get-tuple-element.25), channel_id=1, source_target_pairs={{0,1},{1,2},{2,3},{3,0},{4,5},{5,6},{6,7},{7,4},{8,9},{9,10},{10,1... | collective-permute-start | bytes 442376 | tf_op jit(solution)/shard_map/ppermute | solution.py:491
  10.4 10.7 %collective-permute-start.4 = (bf16[64,1152]{1,0:T(8,128)(2,1)}, bf16[64,1152]{1,0:T(8,128)(2,1)S(1)}, u32[]{:S(2)}, u32[]{:S(2)}) collective-permute-start(bf16[64,1152]{1,0:T(8,128)(2,1)} %get-tuple-element.28), channel_id=1, source_target_pairs={{0,2},{1,3},{2,0},{3,1},{4,6},{5,7},{6,4},{7,5},{8,10},{9,11},{10,... | collective-permute-start | bytes 442376 | tf_op jit(solution)/shard_map/ppermute | solution.py:491
  12.0 9.2 %collective-permute-start.5 = (bf16[64,1152]{1,0:T(8,128)(2,1)}, bf16[64,1152]{1,0:T(8,128)(2,1)S(1)}, u32[]{:S(2)}, u32[]{:S(2)}) collective-permute-start(bf16[64,1152]{1,0:T(8,128)(2,1)} %get-tuple-element.29), channel_id=1, source_target_pairs={{0,3},{1,0},{2,1},{3,2},{4,7},{5,4},{6,5},{7,6},{8,11},{9,8},{10,9... | collective-permute-start | bytes 442376 | tf_op jit(solution)/shard_map/ppermute | solution.py:491
  16.4 19.4 %collective-permute-start.7 = (bf16[384,512]{1,0:T(8,128)(2,1)S(1)}, bf16[384,512]{1,0:T(8,128)(2,1)S(1)}, u32[]{:S(2)}, u32[]{:S(2)}) collective-permute-start(bf16[384,512]{1,0:T(8,128)(2,1)S(1)} %edge_rows.5), channel_id=1, source_target_pairs={{1,3},{2,0},{5,7},{6,4},{9,11},{10,8},{13,15},{14,12},{17,19},{18,... | collective-permute-start | bytes 1179656 | tf_op jit(solution)/shard_map/ppermute | solution.py:515
  17.9 32.5 %collective-permute-start.3 = (bf16[384,1024]{1,0:T(8,128)(2,1)S(1)}, bf16[384,1024]{1,0:T(8,128)(2,1)S(1)}, u32[]{:S(2)}, u32[]{:S(2)}) collective-permute-start(bf16[384,1024]{1,0:T(8,128)(2,1)S(1)} %edge_rows.3), channel_id=1, source_target_pairs={{0,1},{2,3},{1,0},{3,2},{4,5},{6,7},{5,4},{7,6},{8,9},{10,11},{9,8... | collective-permute-start | bytes 2359304 | tf_op jit(solution)/shard_map/ppermute | solution.py:513
  21.5 7.6 %collective-permute-start.9 = (bf16[16,1024]{1,0:T(8,128)(2,1)S(1)}, bf16[16,1024]{1,0:T(8,128)(2,1)S(1)}, u32[]{:S(2)}, u32[]{:S(2)}) collective-permute-start(bf16[16,1024]{1,0:T(8,128)(2,1)S(1)} %get-tuple-element.33), channel_id=1, source_target_pairs={{0,8},{4,12},{8,16},{12,20},{16,24},{20,28},{24,0},{28,4},{1,9},{5... | collective-permute-start | bytes 98312 | tf_op jit(solution)/shard_map/ppermute | solution.py:491
  23.2 6.8 %collective-permute-start.10 = (bf16[16,1024]{1,0:T(8,128)(2,1)S(1)}, bf16[16,1024]{1,0:T(8,128)(2,1)S(1)}, u32[]{:S(2)}, u32[]{:S(2)}) collective-permute-start(bf16[16,1024]{1,0:T(8,128)(2,1)S(1)} %get-tuple-element.34), channel_id=1, source_target_pairs={{0,16},{4,20},{8,24},{12,28},{16,0},{20,4},{24,8},{28,12},{1,17},{... | collective-permute-start | bytes 98312 | tf_op jit(solution)/shard_map/ppermute | solution.py:491
  25.7 4.2 %collective-permute-start.11 = (bf16[16,1024]{1,0:T(8,128)(2,1)S(1)}, bf16[16,1024]{1,0:T(8,128)(2,1)S(1)}, u32[]{:S(2)}, u32[]{:S(2)}) collective-permute-start(bf16[16,1024]{1,0:T(8,128)(2,1)S(1)} %get-tuple-element.35), channel_id=1, source_target_pairs={{0,24},{4,28},{8,0},{12,4},{16,8},{20,12},{24,16},{28,20},{1,25},{... | collective-permute-start | bytes 98312 | tf_op jit(solution)/shard_map/ppermute | solution.py:491
  29.1 14.9 %collective-permute-start.6 = (bf16[384,512]{1,0:T(8,128)(2,1)S(1)}, bf16[384,512]{1,0:T(8,128)(2,1)S(1)}, u32[]{:S(2)}, u32[]{:S(2)}) collective-permute-start(bf16[384,512]{1,0:T(8,128)(2,1)S(1)} %edge_rows.4), channel_id=1, source_target_pairs={{1,2},{2,1},{5,6},{6,5},{9,10},{10,9},{13,14},{14,13},{17,18},{18,... | collective-permute-start | bytes 1179656 | tf_op jit(solution)/shard_map/ppermute | solution.py:525
  30.7 19.7 %copy-start.4 = (f32[7,7,1024]{2,1,0:T(8,128)S(1)}, f32[7,7,1024]{2,1,0:T(8,128)}, u32[]{:S(2)}) copy-start(f32[7,7,1024]{2,1,0:T(8,128)} %refs_4_.1) | copy-start | bytes 602116
  30.7 19.7 %copy-start.6 = (bf16[192,40]{1,0:T(8,128)(2,1)S(1)}, bf16[192,40]{1,0:T(8,128)(2,1)}, u32[]{:S(2)}) copy-start(bf16[192,40]{1,0:T(8,128)(2,1)} %constant.59.clone.refs_3_) | copy-start | bytes 46084
  33.5 19.6 %copy-start.9 = (bf16[1024,1024]{1,0:T(8,128)(2,1)S(1)}, bf16[1024,1024]{1,0:T(8,128)(2,1)}, u32[]{:S(2)}) copy-start(bf16[1024,1024]{1,0:T(8,128)(2,1)} %proj_ref.1) | copy-start | bytes 6291460
  33.5 19.6 %copy-start.10 = (f32[1024]{0:T(1024)S(1)}, f32[1024]{0:T(1024)}, u32[]{:S(2)}) copy-start(f32[1024]{0:T(1024)} %param.23) | copy-start | bytes 12292
  33.5 19.6 %copy-start.11 = (f32[1024]{0:T(1024)S(1)}, f32[1024]{0:T(1024)}, u32[]{:S(2)}) copy-start(f32[1024]{0:T(1024)} %param.25) | copy-start | bytes 12292
  33.6 19.6 %copy-start.12 = (bf16[128,256]{1,0:T(8,128)(2,1)S(1)}, bf16[128,256]{1,0:T(8,128)(2,1)}, u32[]{:S(2)}) copy-start(bf16[128,256]{1,0:T(8,128)(2,1)} %constant.63.clone.cols_ref) | copy-start | bytes 196612
  33.6 4.0 %collective-permute-start.12 = (bf16[16,1024]{1,0:T(8,128)(2,1)S(1)}, bf16[16,1024]{1,0:T(8,128)(2,1)S(1)}, u32[]{:S(2)}, u32[]{:S(2)}) collective-permute-start(bf16[16,1024]{1,0:T(8,128)(2,1)S(1)} %get-tuple-element.40), channel_id=1, source_target_pairs={{0,24},{4,28},{8,0},{12,4},{16,8},{20,12},{24,16},{28,20},{1,25},{... | collective-permute-start | bytes 98312 | tf_op jit(solution)/shard_map/ppermute | solution.py:491
  35.8 5.7 %collective-permute-start.13 = (bf16[16,1024]{1,0:T(8,128)(2,1)S(1)}, bf16[16,1024]{1,0:T(8,128)(2,1)S(1)}, u32[]{:S(2)}, u32[]{:S(2)}) collective-permute-start(bf16[16,1024]{1,0:T(8,128)(2,1)S(1)} %get-tuple-element.41), channel_id=1, source_target_pairs={{0,16},{4,20},{8,24},{12,28},{16,0},{20,4},{24,8},{28,12},{1,17},{... | collective-permute-start | bytes 98312 | tf_op jit(solution)/shard_map/ppermute | solution.py:491
  35.8 5.8 %collective-permute-start.14 = (bf16[16,1024]{1,0:T(8,128)(2,1)S(1)}, bf16[16,1024]{1,0:T(8,128)(2,1)S(1)}, u32[]{:S(2)}, u32[]{:S(2)}) collective-permute-start(bf16[16,1024]{1,0:T(8,128)(2,1)S(1)} %get-tuple-element.42), channel_id=1, source_target_pairs={{0,8},{4,12},{8,16},{12,20},{16,24},{20,28},{24,0},{28,4},{1,9},{5... | collective-permute-start | bytes 98312 | tf_op jit(solution)/shard_map/ppermute | solution.py:491
  37.6 12.8 %collective-permute-start.8 = (bf16[384,512]{1,0:T(8,128)(2,1)S(1)}, bf16[384,512]{1,0:T(8,128)(2,1)S(1)}, u32[]{:S(2)}, u32[]{:S(2)}) collective-permute-start(bf16[384,512]{1,0:T(8,128)(2,1)S(1)} %after.1), channel_id=1, source_target_pairs={{3,2},{0,1},{7,6},{4,5},{11,10},{8,9},{15,14},{12,13},{19,18},{16,... | collective-permute-start | bytes 1179656 | tf_op jit(solution)/shard_map/ppermute | solution.py:521
  41.6 11.4 %collective-permute-start.17 = (bf16[64,1024]{1,0:T(8,128)(2,1)S(1)}, bf16[64,1024]{1,0:T(8,128)(2,1)S(1)}, u32[]{:S(2)}, u32[]{:S(2)}) collective-permute-start(bf16[64,1024]{1,0:T(8,128)(2,1)S(1)} %constant_dynamic-update-slice_fusion.rest_0_), channel_id=1, source_target_pairs={{0,1},{1,2},{2,3},{3,0},{4,5},{5,6},{6,7},{7,4},{8,9},{9,10},{10,1... | collective-permute-start | bytes 393224 | tf_op jit(solution)/shard_map/ppermute | solution.py:491
  43.6 9.5 %collective-permute-start.16 = (bf16[64,1024]{1,0:T(8,128)(2,1)S(1)}, bf16[64,1024]{1,0:T(8,128)(2,1)S(1)}, u32[]{:S(2)}, u32[]{:S(2)}) collective-permute-start(bf16[64,1024]{1,0:T(8,128)(2,1)S(1)} %constant_dynamic-update-slice_fusion.rest_0_), channel_id=1, source_target_pairs={{0,2},{1,3},{2,0},{3,1},{4,6},{5,7},{6,4},{7,5},{8,10},{9,11},{10,... | collective-permute-start | bytes 393224 | tf_op jit(solution)/shard_map/ppermute | solution.py:491
  44.1 9.1 %collective-permute-start.15 = (bf16[64,1024]{1,0:T(8,128)(2,1)S(1)}, bf16[64,1024]{1,0:T(8,128)(2,1)S(1)}, u32[]{:S(2)}, u32[]{:S(2)}) collective-permute-start(bf16[64,1024]{1,0:T(8,128)(2,1)S(1)} %constant_dynamic-update-slice_fusion.rest_0_), channel_id=1, source_target_pairs={{0,3},{1,0},{2,1},{3,2},{4,7},{5,4},{6,5},{7,6},{8,11},{9,8},{10,9... | collective-permute-start | bytes 393224 | tf_op jit(solution)/shard_map/ppermute | solution.py:491
  (10 other events, 95.9 us)

commit v6 on v5

--- a/solution.py
+++ b/solution.py
@@ -29,6 +29,10 @@
 
 def rms_scale(value, gain):
     return value * lax.rsqrt(jnp.mean(value * value, axis=-1, keepdims=True) + EPS) * gain
+
+
+def paired(count):
+    return count & (count - 1) == 0
 
 
 def split_index(value, count):
@@ -63,7 +67,7 @@
     outer, inner = split_index(place, slot_dev)
     outer, core = split_index(outer, 2)
     step_tok, step_z = split_index(outer, count_z)
-    at_z = split_index(step_z + my_z, count_z)[1]
+    at_z = step_z ^ my_z if paired(count_z) else split_index(step_z + my_z, count_z)[1]
     at_tok = split_index(step_tok + my_tok, count_tok)[1]
     wanted = ((at_z * 2 + core) * count_tok + at_tok) * slot_dev + inner
     pick = jnp.where(wanted == source, 1.0, 0.0).astype(BF16)
@@ -490,6 +494,11 @@
         count = lax.axis_size(axis)
         return lax.ppermute(value, axis, [(i, (i + step) % count) for i in range(count)])
 
+    def shift_z(value, step):
+        if not paired(count_z):
+            return shift(value, "fc", 2 * step)
+        return lax.ppermute(value, "fc", [(i, i ^ (2 * abs(step))) for i in range(count_fc)])
+
     other = [(i, i ^ 1) for i in range(count_fc)]
     tie = lax.optimization_barrier
     even = at_tok % 2 == 0
@@ -515,7 +524,7 @@
     around = lax.ppermute(around, "tok", [(1, 3), (2, 0)] if count_tok == 4 else swap(1))
 
     slot_in = gather_slots(parts, slot_gain, count_z)
-    arrived = [slot_in[0]] + [shift(slot_in[k], "fc", 2 * k) for k in range(1, count_z)]
+    arrived = [slot_in[0]] + [shift_z(slot_in[k], k) for k in range(1, count_z)]
     around, seen = after(around, slot_in[0]), slot_in[0]
     if count_tok == 4:
         around = lax.ppermute(around, "tok", [(3, 2), (0, 1)])
@@ -525,7 +534,7 @@
     direct = lax.ppermute(direct, "tok", swap(1))
     core = (at_fc % 2).astype(jnp.int32).reshape(1)
     made = experts(core, share, arrived, w_in, w_out, in_other, out_other, slots_exp)
-    back = [made[0]] + [shift(made[k], "fc", -2 * k) for k in range(1, count_z)]
+    back = [made[0]] + [shift_z(made[k], -k) for k in range(1, count_z)]
     mine = jnp.concatenate(back, axis=0)
     above, below = at_tok > 0, at_tok < count_tok - 1
     inside = jnp.stack([jnp.where(even, below, above), jnp.where(even, above, below)])

time: 66.8 us -> 66.3 us (level)
  waiting for transfers between devices: 8.26 us -> 9.85 us
  starting transfers between devices: 29.2 us -> 27.7 us
  local copies, waits for them, and re-layouts: 0.78 us -> 0.11 us
    ppermute x0 -> x6, starting transfers between devices: none -> 8.9 us  [shift_z(): lax.ppermute(value, 'fc', [(i, i ^ 2 * abs(step)) for i in range(count_fc)])]
    ppermute x12 -> x6, starting transfers between devices: 19.2 us -> 10.8 us  [shift(): lax.ppermute(value, axis, [(i, (i + step) % count) for i in range(count)])]
    ppermute x0 -> x6, waiting for transfers between devices: none -> 4.13 us  [shift_z(): lax.ppermute(value, 'fc', [(i, i ^ 2 * abs(step)) for i in range(count_fc)])]
    ppermute x1, starting transfers between devices: 3.96 us -> 1.96 us  [local(): around = lax.ppermute(around, 'tok', [(3, 2), (0, 1)])]
    ppermute x1, waiting for transfers between devices: 3.73 us -> 2.32 us  [local(): around = lax.ppermute(around, 'tok', [(3, 2), (0, 1)])]
    ppermute x12 -> x6, waiting for transfers between devices: 4.14 us -> 3.02 us  [shift(): lax.ppermute(value, axis, [(i, (i + step) % count) for i in range(count)])]
    unnamed x35, local copies, waits for them, and re-layouts: 0.78 us -> 0.1 us
  transfers between devices with their start and end apart: 18 -> 18, of which waited for: 5 -> 6; matrix products, arithmetic and copies ran while one was open for 1% -> 1% of each run, Pallas kernels for 21% -> 21%
where the time goes in v6:
time: 66.3 us; the launch traced here: 66.1 us
  starting transfers between devices  27.7 us (42%)
  Pallas kernels  27.4 us (41%)
  waiting for transfers between devices  9.85 us (15%)
  other arithmetic  0.73 us (1%)
    pallas_call x1, Pallas kernels, block_fields(): pl.pallas_call(functools.partial(block_kernel, dims), out_shape=jax.Shape...  13.4 us
    ppermute x6, starting transfers between devices, shift(): lax.ppermute(value, axis, [(i, (i + step) % count) for i in range(count)])  10.8 us
    ppermute x6, starting transfers between devices, shift_z(): lax.ppermute(value, 'fc', [(i, i ^ 2 * abs(step)) for i in range(count_fc)])  8.9 us
    pallas_call x1, Pallas kernels, dispatch(): pl.pallas_call(functools.partial(dispatch_kernel, layout), out_shape=[jax...  6.02 us
    pallas_call x2, Pallas kernels, combine_weights(): pl.pallas_call(functools.partial(combine_kernel, [len(parts) for parts in...  4.63 us
    ppermute x6, waiting for transfers between devices, shift_z(): lax.ppermute(value, 'fc', [(i, i ^ 2 * abs(step)) for i in range(count_fc)])  4.13 us
    ppermute x1, starting transfers between devices, local(): first_halo = lax.ppermute(first_halo, 'tok', swap(0))  3.28 us
    ppermute x6, waiting for transfers between devices, shift(): lax.ppermute(value, axis, [(i, (i + step) % count) for i in range(count)])  3.02 us
  transfers between devices with their start and end apart: 18, of which 6 were waited for; matrix products, arithmetic and copies ran while one was open for 1% of the time, Pallas kernels for 21%

profile of v6, /device:TPU:0, one launch (start us, length us, event | category | flops | bytes accessed | tf_op | source)
XLA Modules:
  0.0 66.1 jit_solution(10153319370335148778)
XLA Ops:
  0.0 0.5 collective-permute-start
  0.5 0.6 pad_add_fusion.index_ref
  1.2 6.0 %dispatch.1 = (bf16[256,1024]{1,0:T(8,128)(2,1)}, bf16[64,1152]{1,0:T(8,128)(2,1)}, bf16[64,1152]{1,0:T(8,128)(2,1)}, bf16[64,1152]{1,0:T(8,128)(2,1)}, bf16[64,1152]{1,0:T(8,128)(2,1)}) custom-call(s32[2]{0:T(128)} %pad_add_fusion.index_ref, bf16[1024,1024]{1,0:T(8,128)(2,1)} %bitcast.12, bf16[1024,256]{1,0:T(8,128)(2,1)} %keys_hbm.1, f32[1,1024]{1,0:T(1,128)} %bitcast.18), custom_call_target="tpu_custom_call" | custom-call | flops 1073741824 | bytes 4194304 | tf_op jit(solution)/shard_map/dispatch/pallas_call | solution.py:109
  7.6 2.9 %collective-permute-start.2 = (bf16[64,1152]{1,0:T(8,128)(2,1)}, bf16[64,1152]{1,0:T(8,128)(2,1)S(1)}, u32[]{:S(2)}, u32[]{:S(2)}) collective-permute-start(bf16[64,1152]{1,0:T(8,128)(2,1)} %get-tuple-element.25), channel_id=1, source_target_pairs={{0,1},{1,2},{2,3},{3,0},{4,5},{5,6},{6,7},{7,4},{8,9},{9,10},{10,1... | collective-permute-start | bytes 442376 | tf_op jit(solution)/shard_map/ppermute | solution.py:495
  10.4 1.5 %collective-permute-start.4 = (bf16[64,1152]{1,0:T(8,128)(2,1)}, bf16[64,1152]{1,0:T(8,128)(2,1)S(1)}, u32[]{:S(2)}, u32[]{:S(2)}) collective-permute-start(bf16[64,1152]{1,0:T(8,128)(2,1)} %get-tuple-element.28), channel_id=1, source_target_pairs={{0,2},{1,3},{2,0},{3,1},{4,6},{5,7},{6,4},{7,5},{8,10},{9,11},{10,... | collective-permute-start | bytes 442376 | tf_op jit(solution)/shard_map/ppermute | solution.py:495
  12.0 1.4 %collective-permute-start.5 = (bf16[64,1152]{1,0:T(8,128)(2,1)}, bf16[64,1152]{1,0:T(8,128)(2,1)S(1)}, u32[]{:S(2)}, u32[]{:S(2)}) collective-permute-start(bf16[64,1152]{1,0:T(8,128)(2,1)} %get-tuple-element.29), channel_id=1, source_target_pairs={{0,3},{1,0},{2,1},{3,2},{4,7},{5,4},{6,5},{7,6},{8,11},{9,8},{10,9... | collective-permute-start | bytes 442376 | tf_op jit(solution)/shard_map/ppermute | solution.py:495
  13.4 2.9 %collective-permute-done.2._.refs_1_ = bf16[64,1152]{1,0:T(8,128)(2,1)S(1)} collective-permute-done((bf16[64,1152]{1,0:T(8,128)(2,1)}, bf16[64,1152]{1,0:T(8,128)(2,1)S(1)}, u32[]{:S(2)}, u32[]{:S(2)}) %collective-permute-start.2) | collective-permute-done | bytes 147488 | tf_op jit(solution)/shard_map/ppermute | solution.py:495
  16.4 1.4 %collective-permute-start.7 = (bf16[384,512]{1,0:T(8,128)(2,1)S(1)}, bf16[384,512]{1,0:T(8,128)(2,1)S(1)}, u32[]{:S(2)}, u32[]{:S(2)}) collective-permute-start(bf16[384,512]{1,0:T(8,128)(2,1)S(1)} %edge_rows.5), channel_id=1, source_target_pairs={{1,3},{2,0},{5,7},{6,4},{9,11},{10,8},{13,15},{14,12},{17,19},{18,... | collective-permute-start | bytes 1179656 | tf_op jit(solution)/shard_map/ppermute | solution.py:524
  17.9 3.3 %collective-permute-start.3 = (bf16[384,1024]{1,0:T(8,128)(2,1)S(1)}, bf16[384,1024]{1,0:T(8,128)(2,1)S(1)}, u32[]{:S(2)}, u32[]{:S(2)}) collective-permute-start(bf16[384,1024]{1,0:T(8,128)(2,1)S(1)} %edge_rows.3), channel_id=1, source_target_pairs={{0,1},{2,3},{1,0},{3,2},{4,5},{6,7},{5,4},{7,6},{8,9},{10,11},{9,8... | collective-permute-start | bytes 2359304 | tf_op jit(solution)/shard_map/ppermute | solution.py:522
  21.5 1.6 %collective-permute-start.9 = (bf16[16,1024]{1,0:T(8,128)(2,1)S(1)}, bf16[16,1024]{1,0:T(8,128)(2,1)S(1)}, u32[]{:S(2)}, u32[]{:S(2)}) collective-permute-start(bf16[16,1024]{1,0:T(8,128)(2,1)S(1)} %get-tuple-element.33), channel_id=1, source_target_pairs={{0,8},{4,12},{8,0},{12,4},{16,24},{20,28},{24,16},{28,20},{1,9},{5... | collective-permute-start | bytes 98312 | tf_op jit(solution)/shard_map/ppermute | solution.py:500
  23.2 2.6 %collective-permute-start.10 = (bf16[16,1024]{1,0:T(8,128)(2,1)S(1)}, bf16[16,1024]{1,0:T(8,128)(2,1)S(1)}, u32[]{:S(2)}, u32[]{:S(2)}) collective-permute-start(bf16[16,1024]{1,0:T(8,128)(2,1)S(1)} %get-tuple-element.34), channel_id=1, source_target_pairs={{0,16},{4,20},{8,24},{12,28},{16,0},{20,4},{24,8},{28,12},{1,17},{... | collective-permute-start | bytes 98312 | tf_op jit(solution)/shard_map/ppermute | solution.py:500
  26.0 2.0 %combine_weights.2._.share_ref = bf16[1024,256]{1,0:T(8,128)(2,1)S(1)} custom-call(s32[1]{0:T(128)} %constant.57.clone.1.valid_ref, bf16[256,1024]{1,0:T(8,128)(2,1)S(1)} %copy-done.3, f32[1,1024]{1,0:T(1,128)S(1)} %bitcast.19, bf16[16,1024]{1,0:T(8,128)(2,1)S(1)} %get-tuple-element.30._.refs_0_, bf16[1024,1024]{1,0:T(8,128)(2,1)S(1)} %bitcast.15), custom_call_target="tpu_custom_call" | custom-call | flops 536870912 | bytes 2097152 | tf_op jit(solution)/shard_map/combine_weights/pallas_call | solution.py:280
  28.0 0.8 %collective-permute-start.6 = (bf16[384,512]{1,0:T(8,128)(2,1)S(1)}, bf16[384,512]{1,0:T(8,128)(2,1)S(1)}, u32[]{:S(2)}, u32[]{:S(2)}) collective-permute-start(bf16[384,512]{1,0:T(8,128)(2,1)S(1)} %edge_rows.4), channel_id=1, source_target_pairs={{1,2},{2,1},{5,6},{6,5},{9,10},{10,9},{13,14},{14,13},{17,18},{18,... | collective-permute-start | bytes 1179656 | tf_op jit(solution)/shard_map/ppermute | solution.py:534
  28.9 2.6 %collective-permute-done.11.refs_3_ = bf16[16,1024]{1,0:T(8,128)(2,1)S(1)} collective-permute-done((bf16[16,1024]{1,0:T(8,128)(2,1)S(1)}, bf16[16,1024]{1,0:T(8,128)(2,1)S(1)}, u32[]{:S(2)}, u32[]{:S(2)}) %collective-permute-start.11) | collective-permute-done | bytes 32800 | tf_op jit(solution)/shard_map/ppermute | solution.py:500
  31.5 2.8 %experts.1 = (bf16[16,1024]{1,0:T(8,128)(2,1)S(1)}, bf16[16,1024]{1,0:T(8,128)(2,1)S(1)}, bf16[16,1024]{1,0:T(8,128)(2,1)S(1)}, bf16[16,1024]{1,0:T(8,128)(2,1)S(1)}) custom-call(s32[1]{0:T(128)} %bitcast.8.core_ref, bf16[1024,256]{1,0:T(8,128)(2,1)S(1)} %combine_weights.2._.share_ref, bf16[2,1024,512]{2,1,0:T(8,128)(2,1)S(1)} %copy-done.1, ...), custom_call_target="tpu_custom_call" | custom-call | flops 536870912 | bytes 8388608 | tf_op jit(solution)/shard_map/experts/pallas_call | solution.py:204
  34.5 2.2 %collective-permute-start.13 = (bf16[16,1024]{1,0:T(8,128)(2,1)S(1)}, bf16[16,1024]{1,0:T(8,128)(2,1)S(1)}, u32[]{:S(2)}, u32[]{:S(2)}) collective-permute-start(bf16[16,1024]{1,0:T(8,128)(2,1)S(1)} %get-tuple-element.41), channel_id=1, source_target_pairs={{0,16},{4,20},{8,24},{12,28},{16,0},{20,4},{24,8},{28,12},{1,17},{... | collective-permute-start | bytes 98312 | tf_op jit(solution)/shard_map/ppermute | solution.py:500
  36.7 2.2 %collective-permute-start.14 = (bf16[16,1024]{1,0:T(8,128)(2,1)S(1)}, bf16[16,1024]{1,0:T(8,128)(2,1)S(1)}, u32[]{:S(2)}, u32[]{:S(2)}) collective-permute-start(bf16[16,1024]{1,0:T(8,128)(2,1)S(1)} %get-tuple-element.42), channel_id=1, source_target_pairs={{0,24},{4,28},{8,16},{12,20},{16,8},{20,12},{24,0},{28,4},{1,25},{... | collective-permute-start | bytes 98312 | tf_op jit(solution)/shard_map/ppermute | solution.py:500
  38.9 2.0 %collective-permute-start.8 = (bf16[384,512]{1,0:T(8,128)(2,1)S(1)}, bf16[384,512]{1,0:T(8,128)(2,1)S(1)}, u32[]{:S(2)}, u32[]{:S(2)}) collective-permute-start(bf16[384,512]{1,0:T(8,128)(2,1)S(1)} %after.1), channel_id=1, source_target_pairs={{3,2},{0,1},{7,6},{4,5},{11,10},{8,9},{15,14},{12,13},{19,18},{16,... | collective-permute-start | bytes 1179656 | tf_op jit(solution)/shard_map/ppermute | solution.py:530
  40.9 1.5 %collective-permute-done.14 = bf16[16,1024]{1,0:T(8,128)(2,1)S(1)} collective-permute-done((bf16[16,1024]{1,0:T(8,128)(2,1)S(1)}, bf16[16,1024]{1,0:T(8,128)(2,1)S(1)}, u32[]{:S(2)}, u32[]{:S(2)}) %collective-permute-start.14) | collective-permute-done | bytes 32800 | tf_op jit(solution)/shard_map/ppermute | solution.py:500
  42.4 2.0 %collective-permute-start.17 = (bf16[64,1024]{1,0:T(8,128)(2,1)S(1)}, bf16[64,1024]{1,0:T(8,128)(2,1)S(1)}, u32[]{:S(2)}, u32[]{:S(2)}) collective-permute-start(bf16[64,1024]{1,0:T(8,128)(2,1)S(1)} %constant_dynamic-update-slice_fusion.rest_0_), channel_id=1, source_target_pairs={{0,1},{1,2},{2,3},{3,0},{4,5},{5,6},{6,7},{7,4},{8,9},{9,10},{10,1... | collective-permute-start | bytes 393224 | tf_op jit(solution)/shard_map/ppermute | solution.py:495
  44.5 2.9 %collective-permute-start.15 = (bf16[64,1024]{1,0:T(8,128)(2,1)S(1)}, bf16[64,1024]{1,0:T(8,128)(2,1)S(1)}, u32[]{:S(2)}, u32[]{:S(2)}) collective-permute-start(bf16[64,1024]{1,0:T(8,128)(2,1)S(1)} %constant_dynamic-update-slice_fusion.rest_0_), channel_id=1, source_target_pairs={{0,3},{1,0},{2,1},{3,2},{4,7},{5,4},{6,5},{7,6},{8,11},{9,8},{10,9... | collective-permute-start | bytes 393224 | tf_op jit(solution)/shard_map/ppermute | solution.py:495
  47.5 2.3 %collective-permute-done.8.refs_2_.second_b = bf16[384,512]{1,0:T(8,128)(2,1)S(1)} collective-permute-done((bf16[384,512]{1,0:T(8,128)(2,1)S(1)}, bf16[384,512]{1,0:T(8,128)(2,1)S(1)}, u32[]{:S(2)}, u32[]{:S(2)}) %collective-permute-start.8) | collective-permute-done | bytes 393248 | tf_op jit(solution)/shard_map/ppermute | solution.py:530
  49.9 2.7 %combine_weights.3 = (bf16[384,256]{1,0:T(8,128)(2,1)S(1)}, bf16[384,256]{1,0:T(8,128)(2,1)S(1)}, f32[7,192,1024]{2,1,0:T(8,128)S(1)}) custom-call(s32[2]{0:T(128)S(1)} %add_convert_fusion.valid_ref, bf16[256,1024]{1,0:T(8,128)(2,1)S(1)} %copy-done.3, f32[1,1024]{1,0:T(1,128)S(1)} %bitcast.20, bf16[16,1024]{1,0:T(8,128)(2,1)S(1)} %get-tuple-element.36._, ...), custom_call_target="tpu_custom_call" | custom-call | flops 402653184 | bytes 1572864 | tf_op jit(solution)/shard_map/combine_weights/pallas_call | solution.py:280
  52.7 13.4 %block_fields.1 = bf16[1024,1024]{1,0:T(8,128)(2,1)} custom-call(s32[2]{0:T(128)S(1)} %broadcast_select_fusion.place_ref, bf16[1024,1024]{1,0:T(8,128)(2,1)S(1)} %bitcast.17, bf16[384,1024]{1,0:T(8,128)(2,1)S(1)} %collective-permute-done.3.refs_0_.first_ref, bf16[384,512]{1,0:T(8,128)(2,1)S(1)} %collective-permute-done.6.refs_1_.second_a, ...), custom_call_target="tpu_custom_call" | custom-call | flops 6442450944 | bytes 8388608 | tf_op jit(solution)/shard_map/block_fields/pallas_call | solution.py:457
  (61 shorter events, 1.6 us)
Async XLA Ops:
  0.0 7.2 %collective-permute-start = (bf16[2,1024,512]{2,1,0:T(8,128)(2,1)}, bf16[2,1024,512]{2,1,0:T(8,128)(2,1)}, u32[]{:S(2)}, u32[]{:S(2)}) collective-permute-start(bf16[2,1024,512]{2,1,0:T(8,128)(2,1)} %in_own.1), channel_id=1, source_target_pairs={{0,4},{4,0},{8,12},{12,8},{16,20},{20,16},{24,28},{28,24},{1,5},{5... | collective-permute-start | bytes 6291464 | tf_op jit(solution)/shard_map/ppermute | solution.py:513
  0.5 7.1 %collective-permute-start.1 = (bf16[2,512,1024]{2,1,0:T(8,128)(2,1)}, bf16[2,512,1024]{2,1,0:T(8,128)(2,1)}, u32[]{:S(2)}, u32[]{:S(2)}) collective-permute-start(bf16[2,512,1024]{2,1,0:T(8,128)(2,1)} %out_own.1), channel_id=1, source_target_pairs={{0,4},{4,0},{8,12},{12,8},{16,20},{20,16},{24,28},{28,24},{1,5},{5... | collective-permute-start | bytes 6291464 | tf_op jit(solution)/shard_map/ppermute | solution.py:514
  7.6 8.7 %collective-permute-start.2 = (bf16[64,1152]{1,0:T(8,128)(2,1)}, bf16[64,1152]{1,0:T(8,128)(2,1)S(1)}, u32[]{:S(2)}, u32[]{:S(2)}) collective-permute-start(bf16[64,1152]{1,0:T(8,128)(2,1)} %get-tuple-element.25), channel_id=1, source_target_pairs={{0,1},{1,2},{2,3},{3,0},{4,5},{5,6},{6,7},{7,4},{8,9},{9,10},{10,1... | collective-permute-start | bytes 442376 | tf_op jit(solution)/shard_map/ppermute | solution.py:495
  10.4 10.7 %collective-permute-start.4 = (bf16[64,1152]{1,0:T(8,128)(2,1)}, bf16[64,1152]{1,0:T(8,128)(2,1)S(1)}, u32[]{:S(2)}, u32[]{:S(2)}) collective-permute-start(bf16[64,1152]{1,0:T(8,128)(2,1)} %get-tuple-element.28), channel_id=1, source_target_pairs={{0,2},{1,3},{2,0},{3,1},{4,6},{5,7},{6,4},{7,5},{8,10},{9,11},{10,... | collective-permute-start | bytes 442376 | tf_op jit(solution)/shard_map/ppermute | solution.py:495
  12.0 9.2 %collective-permute-start.5 = (bf16[64,1152]{1,0:T(8,128)(2,1)}, bf16[64,1152]{1,0:T(8,128)(2,1)S(1)}, u32[]{:S(2)}, u32[]{:S(2)}) collective-permute-start(bf16[64,1152]{1,0:T(8,128)(2,1)} %get-tuple-element.29), channel_id=1, source_target_pairs={{0,3},{1,0},{2,1},{3,2},{4,7},{5,4},{6,5},{7,6},{8,11},{9,8},{10,9... | collective-permute-start | bytes 442376 | tf_op jit(solution)/shard_map/ppermute | solution.py:495
  16.4 20.3 %collective-permute-start.7 = (bf16[384,512]{1,0:T(8,128)(2,1)S(1)}, bf16[384,512]{1,0:T(8,128)(2,1)S(1)}, u32[]{:S(2)}, u32[]{:S(2)}) collective-permute-start(bf16[384,512]{1,0:T(8,128)(2,1)S(1)} %edge_rows.5), channel_id=1, source_target_pairs={{1,3},{2,0},{5,7},{6,4},{9,11},{10,8},{13,15},{14,12},{17,19},{18,... | collective-permute-start | bytes 1179656 | tf_op jit(solution)/shard_map/ppermute | solution.py:524
  17.9 32.0 %collective-permute-start.3 = (bf16[384,1024]{1,0:T(8,128)(2,1)S(1)}, bf16[384,1024]{1,0:T(8,128)(2,1)S(1)}, u32[]{:S(2)}, u32[]{:S(2)}) collective-permute-start(bf16[384,1024]{1,0:T(8,128)(2,1)S(1)} %edge_rows.3), channel_id=1, source_target_pairs={{0,1},{2,3},{1,0},{3,2},{4,5},{6,7},{5,4},{7,6},{8,9},{10,11},{9,8... | collective-permute-start | bytes 2359304 | tf_op jit(solution)/shard_map/ppermute | solution.py:522
  21.5 6.5 %collective-permute-start.9 = (bf16[16,1024]{1,0:T(8,128)(2,1)S(1)}, bf16[16,1024]{1,0:T(8,128)(2,1)S(1)}, u32[]{:S(2)}, u32[]{:S(2)}) collective-permute-start(bf16[16,1024]{1,0:T(8,128)(2,1)S(1)} %get-tuple-element.33), channel_id=1, source_target_pairs={{0,8},{4,12},{8,0},{12,4},{16,24},{20,28},{24,16},{28,20},{1,9},{5... | collective-permute-start | bytes 98312 | tf_op jit(solution)/shard_map/ppermute | solution.py:500
  23.2 5.7 %collective-permute-start.10 = (bf16[16,1024]{1,0:T(8,128)(2,1)S(1)}, bf16[16,1024]{1,0:T(8,128)(2,1)S(1)}, u32[]{:S(2)}, u32[]{:S(2)}) collective-permute-start(bf16[16,1024]{1,0:T(8,128)(2,1)S(1)} %get-tuple-element.34), channel_id=1, source_target_pairs={{0,16},{4,20},{8,24},{12,28},{16,0},{20,4},{24,8},{28,12},{1,17},{... | collective-permute-start | bytes 98312 | tf_op jit(solution)/shard_map/ppermute | solution.py:500
  25.8 5.7 %collective-permute-start.11 = (bf16[16,1024]{1,0:T(8,128)(2,1)S(1)}, bf16[16,1024]{1,0:T(8,128)(2,1)S(1)}, u32[]{:S(2)}, u32[]{:S(2)}) collective-permute-start(bf16[16,1024]{1,0:T(8,128)(2,1)S(1)} %get-tuple-element.35), channel_id=1, source_target_pairs={{0,24},{4,28},{8,16},{12,20},{16,8},{20,12},{24,0},{28,4},{1,25},{... | collective-permute-start | bytes 98312 | tf_op jit(solution)/shard_map/ppermute | solution.py:500
  28.0 16.5 %collective-permute-start.6 = (bf16[384,512]{1,0:T(8,128)(2,1)S(1)}, bf16[384,512]{1,0:T(8,128)(2,1)S(1)}, u32[]{:S(2)}, u32[]{:S(2)}) collective-permute-start(bf16[384,512]{1,0:T(8,128)(2,1)S(1)} %edge_rows.4), channel_id=1, source_target_pairs={{1,2},{2,1},{5,6},{6,5},{9,10},{10,9},{13,14},{14,13},{17,18},{18,... | collective-permute-start | bytes 1179656 | tf_op jit(solution)/shard_map/ppermute | solution.py:534
  31.5 18.4 %copy-start.4 = (f32[7,7,1024]{2,1,0:T(8,128)S(1)}, f32[7,7,1024]{2,1,0:T(8,128)}, u32[]{:S(2)}) copy-start(f32[7,7,1024]{2,1,0:T(8,128)} %refs_4_.1) | copy-start | bytes 602116
  31.5 18.4 %copy-start.6 = (bf16[192,40]{1,0:T(8,128)(2,1)S(1)}, bf16[192,40]{1,0:T(8,128)(2,1)}, u32[]{:S(2)}) copy-start(bf16[192,40]{1,0:T(8,128)(2,1)} %constant.59.clone.refs_3_) | copy-start | bytes 46084
  34.3 18.3 %copy-start.9 = (bf16[1024,1024]{1,0:T(8,128)(2,1)S(1)}, bf16[1024,1024]{1,0:T(8,128)(2,1)}, u32[]{:S(2)}) copy-start(bf16[1024,1024]{1,0:T(8,128)(2,1)} %proj_ref.1) | copy-start | bytes 6291460
  34.3 18.3 %copy-start.10 = (f32[1024]{0:T(1024)S(1)}, f32[1024]{0:T(1024)}, u32[]{:S(2)}) copy-start(f32[1024]{0:T(1024)} %param.23) | copy-start | bytes 12292
  34.4 18.3 %copy-start.11 = (f32[1024]{0:T(1024)S(1)}, f32[1024]{0:T(1024)}, u32[]{:S(2)}) copy-start(f32[1024]{0:T(1024)} %param.25) | copy-start | bytes 12292
  34.4 18.3 %copy-start.12 = (bf16[128,256]{1,0:T(8,128)(2,1)S(1)}, bf16[128,256]{1,0:T(8,128)(2,1)}, u32[]{:S(2)}) copy-start(bf16[128,256]{1,0:T(8,128)(2,1)} %constant.63.clone.cols_ref) | copy-start | bytes 196612
  34.4 4.5 %collective-permute-start.12 = (bf16[16,1024]{1,0:T(8,128)(2,1)S(1)}, bf16[16,1024]{1,0:T(8,128)(2,1)S(1)}, u32[]{:S(2)}, u32[]{:S(2)}) collective-permute-start(bf16[16,1024]{1,0:T(8,128)(2,1)S(1)} %get-tuple-element.40), channel_id=1, source_target_pairs={{0,8},{4,12},{8,0},{12,4},{16,24},{20,28},{24,16},{28,20},{1,9},{5... | collective-permute-start | bytes 98312 | tf_op jit(solution)/shard_map/ppermute | solution.py:500
  34.5 6.4 %collective-permute-start.13 = (bf16[16,1024]{1,0:T(8,128)(2,1)S(1)}, bf16[16,1024]{1,0:T(8,128)(2,1)S(1)}, u32[]{:S(2)}, u32[]{:S(2)}) collective-permute-start(bf16[16,1024]{1,0:T(8,128)(2,1)S(1)} %get-tuple-element.41), channel_id=1, source_target_pairs={{0,16},{4,20},{8,24},{12,28},{16,0},{20,4},{24,8},{28,12},{1,17},{... | collective-permute-start | bytes 98312 | tf_op jit(solution)/shard_map/ppermute | solution.py:500
  36.7 5.7 %collective-permute-start.14 = (bf16[16,1024]{1,0:T(8,128)(2,1)S(1)}, bf16[16,1024]{1,0:T(8,128)(2,1)S(1)}, u32[]{:S(2)}, u32[]{:S(2)}) collective-permute-start(bf16[16,1024]{1,0:T(8,128)(2,1)S(1)} %get-tuple-element.42), channel_id=1, source_target_pairs={{0,24},{4,28},{8,16},{12,20},{16,8},{20,12},{24,0},{28,4},{1,25},{... | collective-permute-start | bytes 98312 | tf_op jit(solution)/shard_map/ppermute | solution.py:500
  38.9 10.9 %collective-permute-start.8 = (bf16[384,512]{1,0:T(8,128)(2,1)S(1)}, bf16[384,512]{1,0:T(8,128)(2,1)S(1)}, u32[]{:S(2)}, u32[]{:S(2)}) collective-permute-start(bf16[384,512]{1,0:T(8,128)(2,1)S(1)} %after.1), channel_id=1, source_target_pairs={{3,2},{0,1},{7,6},{4,5},{11,10},{8,9},{15,14},{12,13},{19,18},{16,... | collective-permute-start | bytes 1179656 | tf_op jit(solution)/shard_map/ppermute | solution.py:530
  42.4 10.1 %collective-permute-start.17 = (bf16[64,1024]{1,0:T(8,128)(2,1)S(1)}, bf16[64,1024]{1,0:T(8,128)(2,1)S(1)}, u32[]{:S(2)}, u32[]{:S(2)}) collective-permute-start(bf16[64,1024]{1,0:T(8,128)(2,1)S(1)} %constant_dynamic-update-slice_fusion.rest_0_), channel_id=1, source_target_pairs={{0,1},{1,2},{2,3},{3,0},{4,5},{5,6},{6,7},{7,4},{8,9},{9,10},{10,1... | collective-permute-start | bytes 393224 | tf_op jit(solution)/shard_map/ppermute | solution.py:495
  44.5 8.1 %collective-permute-start.16 = (bf16[64,1024]{1,0:T(8,128)(2,1)S(1)}, bf16[64,1024]{1,0:T(8,128)(2,1)S(1)}, u32[]{:S(2)}, u32[]{:S(2)}) collective-permute-start(bf16[64,1024]{1,0:T(8,128)(2,1)S(1)} %constant_dynamic-update-slice_fusion.rest_0_), channel_id=1, source_target_pairs={{0,2},{1,3},{2,0},{3,1},{4,6},{5,7},{6,4},{7,5},{8,10},{9,11},{10,... | collective-permute-start | bytes 393224 | tf_op jit(solution)/shard_map/ppermute | solution.py:495
  44.5 8.1 %collective-permute-start.15 = (bf16[64,1024]{1,0:T(8,128)(2,1)S(1)}, bf16[64,1024]{1,0:T(8,128)(2,1)S(1)}, u32[]{:S(2)}, u32[]{:S(2)}) collective-permute-start(bf16[64,1024]{1,0:T(8,128)(2,1)S(1)} %constant_dynamic-update-slice_fusion.rest_0_), channel_id=1, source_target_pairs={{0,3},{1,0},{2,1},{3,2},{4,7},{5,4},{6,5},{7,6},{8,11},{9,8},{10,9... | collective-permute-start | bytes 393224 | tf_op jit(solution)/shard_map/ppermute | solution.py:495
  (10 other events, 95.6 us)

commit v7 on v6

--- a/solution.py
+++ b/solution.py
@@ -105,7 +105,7 @@
     total, width = cells.shape
     slots = keys.shape[1]
     part = slots // count_tok
-    count = 8
+    count = 4
     return pl.pallas_call(
         functools.partial(dispatch_kernel, layout),
         out_shape=[jax.ShapeDtypeStruct((slots, width), BF16)]

time: 66.3 us -> 66.3 us (level)
  transfers between devices with their start and end apart: 18 -> 18, of which waited for: 6 -> 6; matrix products, arithmetic and copies ran while one was open for 1% -> 1% of each run, Pallas kernels for 21% -> 20%
where the time goes in v7:
time: 66.3 us; the launch traced here: 66.1 us
  starting transfers between devices  27.7 us (42%)
  Pallas kernels  26.8 us (40%)
  waiting for transfers between devices  10.4 us (16%)
  other arithmetic  0.73 us (1%)
    pallas_call x1, Pallas kernels, block_fields(): pl.pallas_call(functools.partial(block_kernel, dims), out_shape=jax.Shape...  13.4 us
    ppermute x6, starting transfers between devices, shift(): lax.ppermute(value, axis, [(i, (i + step) % count) for i in range(count)])  10.8 us
    ppermute x6, starting transfers between devices, shift_z(): lax.ppermute(value, 'fc', [(i, i ^ 2 * abs(step)) for i in range(count_fc)])  8.9 us
    pallas_call x1, Pallas kernels, dispatch(): pl.pallas_call(functools.partial(dispatch_kernel, layout), out_shape=[jax...  5.47 us
    pallas_call x2, Pallas kernels, combine_weights(): pl.pallas_call(functools.partial(combine_kernel, [len(parts) for parts in...  4.63 us
    ppermute x6, waiting for transfers between devices, shift_z(): lax.ppermute(value, 'fc', [(i, i ^ 2 * abs(step)) for i in range(count_fc)])  4.13 us
    ppermute x1, starting transfers between devices, local(): first_halo = lax.ppermute(first_halo, 'tok', swap(0))  3.28 us
    ppermute x6, waiting for transfers between devices, shift(): lax.ppermute(value, axis, [(i, (i + step) % count) for i in range(count)])  3.02 us
  transfers between devices with their start and end apart: 18, of which 6 were waited for; matrix products, arithmetic and copies ran while one was open for 1% of the time, Pallas kernels for 20%

profile of v7, /device:TPU:0, one launch (start us, length us, event | category | flops | bytes accessed | tf_op | source)
XLA Modules:
  0.0 66.1 jit_solution(6208381799744312395)
XLA Ops:
  0.5 0.6 pad_add_fusion.index_ref
  1.2 5.5 %dispatch.1 = (bf16[256,1024]{1,0:T(8,128)(2,1)}, bf16[64,1152]{1,0:T(8,128)(2,1)}, bf16[64,1152]{1,0:T(8,128)(2,1)}, bf16[64,1152]{1,0:T(8,128)(2,1)}, bf16[64,1152]{1,0:T(8,128)(2,1)}) custom-call(s32[2]{0:T(128)} %pad_add_fusion.index_ref, bf16[1024,1024]{1,0:T(8,128)(2,1)} %bitcast.12, bf16[1024,256]{1,0:T(8,128)(2,1)} %keys_hbm.1, f32[1,1024]{1,0:T(1,128)} %bitcast.18), custom_call_target="tpu_custom_call" | custom-call | flops 1073741824 | bytes 4194304 | tf_op jit(solution)/shard_map/dispatch/pallas_call | solution.py:109
  6.7 0.9 %collective-permute-done.1.out_other = bf16[2,512,1024]{2,1,0:T(8,128)(2,1)} collective-permute-done((bf16[2,512,1024]{2,1,0:T(8,128)(2,1)}, bf16[2,512,1024]{2,1,0:T(8,128)(2,1)}, u32[]{:S(2)}, u32[]{:S(2)}) %collective-permute-start.1) | collective-permute-done | bytes 2097184 | tf_op jit(solution)/shard_map/ppermute | solution.py:514
  7.6 2.9 %collective-permute-start.2 = (bf16[64,1152]{1,0:T(8,128)(2,1)}, bf16[64,1152]{1,0:T(8,128)(2,1)S(1)}, u32[]{:S(2)}, u32[]{:S(2)}) collective-permute-start(bf16[64,1152]{1,0:T(8,128)(2,1)} %get-tuple-element.25), channel_id=1, source_target_pairs={{0,1},{1,2},{2,3},{3,0},{4,5},{5,6},{6,7},{7,4},{8,9},{9,10},{10,1... | collective-permute-start | bytes 442376 | tf_op jit(solution)/shard_map/ppermute | solution.py:495
  10.4 1.5 %collective-permute-start.4 = (bf16[64,1152]{1,0:T(8,128)(2,1)}, bf16[64,1152]{1,0:T(8,128)(2,1)S(1)}, u32[]{:S(2)}, u32[]{:S(2)}) collective-permute-start(bf16[64,1152]{1,0:T(8,128)(2,1)} %get-tuple-element.28), channel_id=1, source_target_pairs={{0,2},{1,3},{2,0},{3,1},{4,6},{5,7},{6,4},{7,5},{8,10},{9,11},{10,... | collective-permute-start | bytes 442376 | tf_op jit(solution)/shard_map/ppermute | solution.py:495
  12.0 1.4 %collective-permute-start.5 = (bf16[64,1152]{1,0:T(8,128)(2,1)}, bf16[64,1152]{1,0:T(8,128)(2,1)S(1)}, u32[]{:S(2)}, u32[]{:S(2)}) collective-permute-start(bf16[64,1152]{1,0:T(8,128)(2,1)} %get-tuple-element.29), channel_id=1, source_target_pairs={{0,3},{1,0},{2,1},{3,2},{4,7},{5,4},{6,5},{7,6},{8,11},{9,8},{10,9... | collective-permute-start | bytes 442376 | tf_op jit(solution)/shard_map/ppermute | solution.py:495
  13.4 2.9 %collective-permute-done.2._.refs_1_ = bf16[64,1152]{1,0:T(8,128)(2,1)S(1)} collective-permute-done((bf16[64,1152]{1,0:T(8,128)(2,1)}, bf16[64,1152]{1,0:T(8,128)(2,1)S(1)}, u32[]{:S(2)}, u32[]{:S(2)}) %collective-permute-start.2) | collective-permute-done | bytes 147488 | tf_op jit(solution)/shard_map/ppermute | solution.py:495
  16.4 1.4 %collective-permute-start.7 = (bf16[384,512]{1,0:T(8,128)(2,1)S(1)}, bf16[384,512]{1,0:T(8,128)(2,1)S(1)}, u32[]{:S(2)}, u32[]{:S(2)}) collective-permute-start(bf16[384,512]{1,0:T(8,128)(2,1)S(1)} %edge_rows.5), channel_id=1, source_target_pairs={{1,3},{2,0},{5,7},{6,4},{9,11},{10,8},{13,15},{14,12},{17,19},{18,... | collective-permute-start | bytes 1179656 | tf_op jit(solution)/shard_map/ppermute | solution.py:524
  17.9 3.3 %collective-permute-start.3 = (bf16[384,1024]{1,0:T(8,128)(2,1)S(1)}, bf16[384,1024]{1,0:T(8,128)(2,1)S(1)}, u32[]{:S(2)}, u32[]{:S(2)}) collective-permute-start(bf16[384,1024]{1,0:T(8,128)(2,1)S(1)} %edge_rows.3), channel_id=1, source_target_pairs={{0,1},{2,3},{1,0},{3,2},{4,5},{6,7},{5,4},{7,6},{8,9},{10,11},{9,8... | collective-permute-start | bytes 2359304 | tf_op jit(solution)/shard_map/ppermute | solution.py:522
  21.5 1.6 %collective-permute-start.9 = (bf16[16,1024]{1,0:T(8,128)(2,1)S(1)}, bf16[16,1024]{1,0:T(8,128)(2,1)S(1)}, u32[]{:S(2)}, u32[]{:S(2)}) collective-permute-start(bf16[16,1024]{1,0:T(8,128)(2,1)S(1)} %get-tuple-element.33), channel_id=1, source_target_pairs={{0,8},{4,12},{8,0},{12,4},{16,24},{20,28},{24,16},{28,20},{1,9},{5... | collective-permute-start | bytes 98312 | tf_op jit(solution)/shard_map/ppermute | solution.py:500
  23.2 2.6 %collective-permute-start.10 = (bf16[16,1024]{1,0:T(8,128)(2,1)S(1)}, bf16[16,1024]{1,0:T(8,128)(2,1)S(1)}, u32[]{:S(2)}, u32[]{:S(2)}) collective-permute-start(bf16[16,1024]{1,0:T(8,128)(2,1)S(1)} %get-tuple-element.34), channel_id=1, source_target_pairs={{0,16},{4,20},{8,24},{12,28},{16,0},{20,4},{24,8},{28,12},{1,17},{... | collective-permute-start | bytes 98312 | tf_op jit(solution)/shard_map/ppermute | solution.py:500
  26.0 2.0 %combine_weights.2._.share_ref = bf16[1024,256]{1,0:T(8,128)(2,1)S(1)} custom-call(s32[1]{0:T(128)} %constant.57.clone.1.valid_ref, bf16[256,1024]{1,0:T(8,128)(2,1)S(1)} %copy-done.3, f32[1,1024]{1,0:T(1,128)S(1)} %bitcast.19, bf16[16,1024]{1,0:T(8,128)(2,1)S(1)} %get-tuple-element.30._.refs_0_, bf16[1024,1024]{1,0:T(8,128)(2,1)S(1)} %bitcast.15), custom_call_target="tpu_custom_call" | custom-call | flops 536870912 | bytes 2097152 | tf_op jit(solution)/shard_map/combine_weights/pallas_call | solution.py:280
  28.0 0.8 %collective-permute-start.6 = (bf16[384,512]{1,0:T(8,128)(2,1)S(1)}, bf16[384,512]{1,0:T(8,128)(2,1)S(1)}, u32[]{:S(2)}, u32[]{:S(2)}) collective-permute-start(bf16[384,512]{1,0:T(8,128)(2,1)S(1)} %edge_rows.4), channel_id=1, source_target_pairs={{1,2},{2,1},{5,6},{6,5},{9,10},{10,9},{13,14},{14,13},{17,18},{18,... | collective-permute-start | bytes 1179656 | tf_op jit(solution)/shard_map/ppermute | solution.py:534
  28.9 2.6 %collective-permute-done.11.refs_3_ = bf16[16,1024]{1,0:T(8,128)(2,1)S(1)} collective-permute-done((bf16[16,1024]{1,0:T(8,128)(2,1)S(1)}, bf16[16,1024]{1,0:T(8,128)(2,1)S(1)}, u32[]{:S(2)}, u32[]{:S(2)}) %collective-permute-start.11) | collective-permute-done | bytes 32800 | tf_op jit(solution)/shard_map/ppermute | solution.py:500
  31.5 2.8 %experts.1 = (bf16[16,1024]{1,0:T(8,128)(2,1)S(1)}, bf16[16,1024]{1,0:T(8,128)(2,1)S(1)}, bf16[16,1024]{1,0:T(8,128)(2,1)S(1)}, bf16[16,1024]{1,0:T(8,128)(2,1)S(1)}) custom-call(s32[1]{0:T(128)} %bitcast.8.core_ref, bf16[1024,256]{1,0:T(8,128)(2,1)S(1)} %combine_weights.2._.share_ref, bf16[2,1024,512]{2,1,0:T(8,128)(2,1)S(1)} %copy-done.1, ...), custom_call_target="tpu_custom_call" | custom-call | flops 536870912 | bytes 8388608 | tf_op jit(solution)/shard_map/experts/pallas_call | solution.py:204
  34.5 2.2 %collective-permute-start.13 = (bf16[16,1024]{1,0:T(8,128)(2,1)S(1)}, bf16[16,1024]{1,0:T(8,128)(2,1)S(1)}, u32[]{:S(2)}, u32[]{:S(2)}) collective-permute-start(bf16[16,1024]{1,0:T(8,128)(2,1)S(1)} %get-tuple-element.41), channel_id=1, source_target_pairs={{0,16},{4,20},{8,24},{12,28},{16,0},{20,4},{24,8},{28,12},{1,17},{... | collective-permute-start | bytes 98312 | tf_op jit(solution)/shard_map/ppermute | solution.py:500
  36.7 2.2 %collective-permute-start.14 = (bf16[16,1024]{1,0:T(8,128)(2,1)S(1)}, bf16[16,1024]{1,0:T(8,128)(2,1)S(1)}, u32[]{:S(2)}, u32[]{:S(2)}) collective-permute-start(bf16[16,1024]{1,0:T(8,128)(2,1)S(1)} %get-tuple-element.42), channel_id=1, source_target_pairs={{0,24},{4,28},{8,16},{12,20},{16,8},{20,12},{24,0},{28,4},{1,25},{... | collective-permute-start | bytes 98312 | tf_op jit(solution)/shard_map/ppermute | solution.py:500
  38.9 2.0 %collective-permute-start.8 = (bf16[384,512]{1,0:T(8,128)(2,1)S(1)}, bf16[384,512]{1,0:T(8,128)(2,1)S(1)}, u32[]{:S(2)}, u32[]{:S(2)}) collective-permute-start(bf16[384,512]{1,0:T(8,128)(2,1)S(1)} %after.1), channel_id=1, source_target_pairs={{3,2},{0,1},{7,6},{4,5},{11,10},{8,9},{15,14},{12,13},{19,18},{16,... | collective-permute-start | bytes 1179656 | tf_op jit(solution)/shard_map/ppermute | solution.py:530
  40.9 1.5 %collective-permute-done.14 = bf16[16,1024]{1,0:T(8,128)(2,1)S(1)} collective-permute-done((bf16[16,1024]{1,0:T(8,128)(2,1)S(1)}, bf16[16,1024]{1,0:T(8,128)(2,1)S(1)}, u32[]{:S(2)}, u32[]{:S(2)}) %collective-permute-start.14) | collective-permute-done | bytes 32800 | tf_op jit(solution)/shard_map/ppermute | solution.py:500
  42.4 2.0 %collective-permute-start.17 = (bf16[64,1024]{1,0:T(8,128)(2,1)S(1)}, bf16[64,1024]{1,0:T(8,128)(2,1)S(1)}, u32[]{:S(2)}, u32[]{:S(2)}) collective-permute-start(bf16[64,1024]{1,0:T(8,128)(2,1)S(1)} %constant_dynamic-update-slice_fusion.rest_0_), channel_id=1, source_target_pairs={{0,1},{1,2},{2,3},{3,0},{4,5},{5,6},{6,7},{7,4},{8,9},{9,10},{10,1... | collective-permute-start | bytes 393224 | tf_op jit(solution)/shard_map/ppermute | solution.py:495
  44.5 2.9 %collective-permute-start.15 = (bf16[64,1024]{1,0:T(8,128)(2,1)S(1)}, bf16[64,1024]{1,0:T(8,128)(2,1)S(1)}, u32[]{:S(2)}, u32[]{:S(2)}) collective-permute-start(bf16[64,1024]{1,0:T(8,128)(2,1)S(1)} %constant_dynamic-update-slice_fusion.rest_0_), channel_id=1, source_target_pairs={{0,3},{1,0},{2,1},{3,2},{4,7},{5,4},{6,5},{7,6},{8,11},{9,8},{10,9... | collective-permute-start | bytes 393224 | tf_op jit(solution)/shard_map/ppermute | solution.py:495
  47.5 2.3 %collective-permute-done.8.refs_2_.second_b = bf16[384,512]{1,0:T(8,128)(2,1)S(1)} collective-permute-done((bf16[384,512]{1,0:T(8,128)(2,1)S(1)}, bf16[384,512]{1,0:T(8,128)(2,1)S(1)}, u32[]{:S(2)}, u32[]{:S(2)}) %collective-permute-start.8) | collective-permute-done | bytes 393248 | tf_op jit(solution)/shard_map/ppermute | solution.py:530
  49.9 2.7 %combine_weights.3 = (bf16[384,256]{1,0:T(8,128)(2,1)S(1)}, bf16[384,256]{1,0:T(8,128)(2,1)S(1)}, f32[7,192,1024]{2,1,0:T(8,128)S(1)}) custom-call(s32[2]{0:T(128)S(1)} %add_convert_fusion.valid_ref, bf16[256,1024]{1,0:T(8,128)(2,1)S(1)} %copy-done.3, f32[1,1024]{1,0:T(1,128)S(1)} %bitcast.20, bf16[16,1024]{1,0:T(8,128)(2,1)S(1)} %get-tuple-element.36._, ...), custom_call_target="tpu_custom_call" | custom-call | flops 402653184 | bytes 1572864 | tf_op jit(solution)/shard_map/combine_weights/pallas_call | solution.py:280
  52.7 13.4 %block_fields.1 = bf16[1024,1024]{1,0:T(8,128)(2,1)} custom-call(s32[2]{0:T(128)S(1)} %broadcast_select_fusion.place_ref, bf16[1024,1024]{1,0:T(8,128)(2,1)S(1)} %bitcast.17, bf16[384,1024]{1,0:T(8,128)(2,1)S(1)} %collective-permute-done.3.refs_0_.first_ref, bf16[384,512]{1,0:T(8,128)(2,1)S(1)} %collective-permute-done.6.refs_1_.second_a, ...), custom_call_target="tpu_custom_call" | custom-call | flops 6442450944 | bytes 8388608 | tf_op jit(solution)/shard_map/block_fields/pallas_call | solution.py:457
  (61 shorter events, 1.7 us)
Async XLA Ops:
  0.0 6.6 %collective-permute-start = (bf16[2,1024,512]{2,1,0:T(8,128)(2,1)}, bf16[2,1024,512]{2,1,0:T(8,128)(2,1)}, u32[]{:S(2)}, u32[]{:S(2)}) collective-permute-start(bf16[2,1024,512]{2,1,0:T(8,128)(2,1)} %in_own.1), channel_id=1, source_target_pairs={{0,4},{4,0},{8,12},{12,8},{16,20},{20,16},{24,28},{28,24},{1,5},{5... | collective-permute-start | bytes 6291464 | tf_op jit(solution)/shard_map/ppermute | solution.py:513
  0.5 7.1 %collective-permute-start.1 = (bf16[2,512,1024]{2,1,0:T(8,128)(2,1)}, bf16[2,512,1024]{2,1,0:T(8,128)(2,1)}, u32[]{:S(2)}, u32[]{:S(2)}) collective-permute-start(bf16[2,512,1024]{2,1,0:T(8,128)(2,1)} %out_own.1), channel_id=1, source_target_pairs={{0,4},{4,0},{8,12},{12,8},{16,20},{20,16},{24,28},{28,24},{1,5},{5... | collective-permute-start | bytes 6291464 | tf_op jit(solution)/shard_map/ppermute | solution.py:514
  7.6 8.7 %collective-permute-start.2 = (bf16[64,1152]{1,0:T(8,128)(2,1)}, bf16[64,1152]{1,0:T(8,128)(2,1)S(1)}, u32[]{:S(2)}, u32[]{:S(2)}) collective-permute-start(bf16[64,1152]{1,0:T(8,128)(2,1)} %get-tuple-element.25), channel_id=1, source_target_pairs={{0,1},{1,2},{2,3},{3,0},{4,5},{5,6},{6,7},{7,4},{8,9},{9,10},{10,1... | collective-permute-start | bytes 442376 | tf_op jit(solution)/shard_map/ppermute | solution.py:495
  10.4 10.7 %collective-permute-start.4 = (bf16[64,1152]{1,0:T(8,128)(2,1)}, bf16[64,1152]{1,0:T(8,128)(2,1)S(1)}, u32[]{:S(2)}, u32[]{:S(2)}) collective-permute-start(bf16[64,1152]{1,0:T(8,128)(2,1)} %get-tuple-element.28), channel_id=1, source_target_pairs={{0,2},{1,3},{2,0},{3,1},{4,6},{5,7},{6,4},{7,5},{8,10},{9,11},{10,... | collective-permute-start | bytes 442376 | tf_op jit(solution)/shard_map/ppermute | solution.py:495
  12.0 9.2 %collective-permute-start.5 = (bf16[64,1152]{1,0:T(8,128)(2,1)}, bf16[64,1152]{1,0:T(8,128)(2,1)S(1)}, u32[]{:S(2)}, u32[]{:S(2)}) collective-permute-start(bf16[64,1152]{1,0:T(8,128)(2,1)} %get-tuple-element.29), channel_id=1, source_target_pairs={{0,3},{1,0},{2,1},{3,2},{4,7},{5,4},{6,5},{7,6},{8,11},{9,8},{10,9... | collective-permute-start | bytes 442376 | tf_op jit(solution)/shard_map/ppermute | solution.py:495
  16.4 20.3 %collective-permute-start.7 = (bf16[384,512]{1,0:T(8,128)(2,1)S(1)}, bf16[384,512]{1,0:T(8,128)(2,1)S(1)}, u32[]{:S(2)}, u32[]{:S(2)}) collective-permute-start(bf16[384,512]{1,0:T(8,128)(2,1)S(1)} %edge_rows.5), channel_id=1, source_target_pairs={{1,3},{2,0},{5,7},{6,4},{9,11},{10,8},{13,15},{14,12},{17,19},{18,... | collective-permute-start | bytes 1179656 | tf_op jit(solution)/shard_map/ppermute | solution.py:524
  17.9 32.0 %collective-permute-start.3 = (bf16[384,1024]{1,0:T(8,128)(2,1)S(1)}, bf16[384,1024]{1,0:T(8,128)(2,1)S(1)}, u32[]{:S(2)}, u32[]{:S(2)}) collective-permute-start(bf16[384,1024]{1,0:T(8,128)(2,1)S(1)} %edge_rows.3), channel_id=1, source_target_pairs={{0,1},{2,3},{1,0},{3,2},{4,5},{6,7},{5,4},{7,6},{8,9},{10,11},{9,8... | collective-permute-start | bytes 2359304 | tf_op jit(solution)/shard_map/ppermute | solution.py:522
  21.5 6.5 %collective-permute-start.9 = (bf16[16,1024]{1,0:T(8,128)(2,1)S(1)}, bf16[16,1024]{1,0:T(8,128)(2,1)S(1)}, u32[]{:S(2)}, u32[]{:S(2)}) collective-permute-start(bf16[16,1024]{1,0:T(8,128)(2,1)S(1)} %get-tuple-element.33), channel_id=1, source_target_pairs={{0,8},{4,12},{8,0},{12,4},{16,24},{20,28},{24,16},{28,20},{1,9},{5... | collective-permute-start | bytes 98312 | tf_op jit(solution)/shard_map/ppermute | solution.py:500
  23.2 5.7 %collective-permute-start.10 = (bf16[16,1024]{1,0:T(8,128)(2,1)S(1)}, bf16[16,1024]{1,0:T(8,128)(2,1)S(1)}, u32[]{:S(2)}, u32[]{:S(2)}) collective-permute-start(bf16[16,1024]{1,0:T(8,128)(2,1)S(1)} %get-tuple-element.34), channel_id=1, source_target_pairs={{0,16},{4,20},{8,24},{12,28},{16,0},{20,4},{24,8},{28,12},{1,17},{... | collective-permute-start | bytes 98312 | tf_op jit(solution)/shard_map/ppermute | solution.py:500
  25.8 5.7 %collective-permute-start.11 = (bf16[16,1024]{1,0:T(8,128)(2,1)S(1)}, bf16[16,1024]{1,0:T(8,128)(2,1)S(1)}, u32[]{:S(2)}, u32[]{:S(2)}) collective-permute-start(bf16[16,1024]{1,0:T(8,128)(2,1)S(1)} %get-tuple-element.35), channel_id=1, source_target_pairs={{0,24},{4,28},{8,16},{12,20},{16,8},{20,12},{24,0},{28,4},{1,25},{... | collective-permute-start | bytes 98312 | tf_op jit(solution)/shard_map/ppermute | solution.py:500
  28.0 16.5 %collective-permute-start.6 = (bf16[384,512]{1,0:T(8,128)(2,1)S(1)}, bf16[384,512]{1,0:T(8,128)(2,1)S(1)}, u32[]{:S(2)}, u32[]{:S(2)}) collective-permute-start(bf16[384,512]{1,0:T(8,128)(2,1)S(1)} %edge_rows.4), channel_id=1, source_target_pairs={{1,2},{2,1},{5,6},{6,5},{9,10},{10,9},{13,14},{14,13},{17,18},{18,... | collective-permute-start | bytes 1179656 | tf_op jit(solution)/shard_map/ppermute | solution.py:534
  31.5 18.4 %copy-start.4 = (f32[7,7,1024]{2,1,0:T(8,128)S(1)}, f32[7,7,1024]{2,1,0:T(8,128)}, u32[]{:S(2)}) copy-start(f32[7,7,1024]{2,1,0:T(8,128)} %refs_4_.1) | copy-start | bytes 602116
  31.5 18.4 %copy-start.6 = (bf16[192,40]{1,0:T(8,128)(2,1)S(1)}, bf16[192,40]{1,0:T(8,128)(2,1)}, u32[]{:S(2)}) copy-start(bf16[192,40]{1,0:T(8,128)(2,1)} %constant.59.clone.refs_3_) | copy-start | bytes 46084
  34.3 18.3 %copy-start.9 = (bf16[1024,1024]{1,0:T(8,128)(2,1)S(1)}, bf16[1024,1024]{1,0:T(8,128)(2,1)}, u32[]{:S(2)}) copy-start(bf16[1024,1024]{1,0:T(8,128)(2,1)} %proj_ref.1) | copy-start | bytes 6291460
  34.3 18.3 %copy-start.10 = (f32[1024]{0:T(1024)S(1)}, f32[1024]{0:T(1024)}, u32[]{:S(2)}) copy-start(f32[1024]{0:T(1024)} %param.23) | copy-start | bytes 12292
  34.4 18.3 %copy-start.11 = (f32[1024]{0:T(1024)S(1)}, f32[1024]{0:T(1024)}, u32[]{:S(2)}) copy-start(f32[1024]{0:T(1024)} %param.25) | copy-start | bytes 12292
  34.4 18.3 %copy-start.12 = (bf16[128,256]{1,0:T(8,128)(2,1)S(1)}, bf16[128,256]{1,0:T(8,128)(2,1)}, u32[]{:S(2)}) copy-start(bf16[128,256]{1,0:T(8,128)(2,1)} %constant.63.clone.cols_ref) | copy-start | bytes 196612
  34.4 4.5 %collective-permute-start.12 = (bf16[16,1024]{1,0:T(8,128)(2,1)S(1)}, bf16[16,1024]{1,0:T(8,128)(2,1)S(1)}, u32[]{:S(2)}, u32[]{:S(2)}) collective-permute-start(bf16[16,1024]{1,0:T(8,128)(2,1)S(1)} %get-tuple-element.40), channel_id=1, source_target_pairs={{0,8},{4,12},{8,0},{12,4},{16,24},{20,28},{24,16},{28,20},{1,9},{5... | collective-permute-start | bytes 98312 | tf_op jit(solution)/shard_map/ppermute | solution.py:500
  34.5 6.4 %collective-permute-start.13 = (bf16[16,1024]{1,0:T(8,128)(2,1)S(1)}, bf16[16,1024]{1,0:T(8,128)(2,1)S(1)}, u32[]{:S(2)}, u32[]{:S(2)}) collective-permute-start(bf16[16,1024]{1,0:T(8,128)(2,1)S(1)} %get-tuple-element.41), channel_id=1, source_target_pairs={{0,16},{4,20},{8,24},{12,28},{16,0},{20,4},{24,8},{28,12},{1,17},{... | collective-permute-start | bytes 98312 | tf_op jit(solution)/shard_map/ppermute | solution.py:500
  36.7 5.7 %collective-permute-start.14 = (bf16[16,1024]{1,0:T(8,128)(2,1)S(1)}, bf16[16,1024]{1,0:T(8,128)(2,1)S(1)}, u32[]{:S(2)}, u32[]{:S(2)}) collective-permute-start(bf16[16,1024]{1,0:T(8,128)(2,1)S(1)} %get-tuple-element.42), channel_id=1, source_target_pairs={{0,24},{4,28},{8,16},{12,20},{16,8},{20,12},{24,0},{28,4},{1,25},{... | collective-permute-start | bytes 98312 | tf_op jit(solution)/shard_map/ppermute | solution.py:500
  38.9 10.9 %collective-permute-start.8 = (bf16[384,512]{1,0:T(8,128)(2,1)S(1)}, bf16[384,512]{1,0:T(8,128)(2,1)S(1)}, u32[]{:S(2)}, u32[]{:S(2)}) collective-permute-start(bf16[384,512]{1,0:T(8,128)(2,1)S(1)} %after.1), channel_id=1, source_target_pairs={{3,2},{0,1},{7,6},{4,5},{11,10},{8,9},{15,14},{12,13},{19,18},{16,... | collective-permute-start | bytes 1179656 | tf_op jit(solution)/shard_map/ppermute | solution.py:530
  42.4 10.1 %collective-permute-start.17 = (bf16[64,1024]{1,0:T(8,128)(2,1)S(1)}, bf16[64,1024]{1,0:T(8,128)(2,1)S(1)}, u32[]{:S(2)}, u32[]{:S(2)}) collective-permute-start(bf16[64,1024]{1,0:T(8,128)(2,1)S(1)} %constant_dynamic-update-slice_fusion.rest_0_), channel_id=1, source_target_pairs={{0,1},{1,2},{2,3},{3,0},{4,5},{5,6},{6,7},{7,4},{8,9},{9,10},{10,1... | collective-permute-start | bytes 393224 | tf_op jit(solution)/shard_map/ppermute | solution.py:495
  44.5 8.1 %collective-permute-start.16 = (bf16[64,1024]{1,0:T(8,128)(2,1)S(1)}, bf16[64,1024]{1,0:T(8,128)(2,1)S(1)}, u32[]{:S(2)}, u32[]{:S(2)}) collective-permute-start(bf16[64,1024]{1,0:T(8,128)(2,1)S(1)} %constant_dynamic-update-slice_fusion.rest_0_), channel_id=1, source_target_pairs={{0,2},{1,3},{2,0},{3,1},{4,6},{5,7},{6,4},{7,5},{8,10},{9,11},{10,... | collective-permute-start | bytes 393224 | tf_op jit(solution)/shard_map/ppermute | solution.py:495
  44.5 8.1 %collective-permute-start.15 = (bf16[64,1024]{1,0:T(8,128)(2,1)S(1)}, bf16[64,1024]{1,0:T(8,128)(2,1)S(1)}, u32[]{:S(2)}, u32[]{:S(2)}) collective-permute-start(bf16[64,1024]{1,0:T(8,128)(2,1)S(1)} %constant_dynamic-update-slice_fusion.rest_0_), channel_id=1, source_target_pairs={{0,3},{1,0},{2,1},{3,2},{4,7},{5,4},{6,5},{7,6},{8,11},{9,8},{10,9... | collective-permute-start | bytes 393224 | tf_op jit(solution)/shard_map/ppermute | solution.py:495
  (10 other events, 95.6 us)
